TPU v7x, 768 devices: a whole 4x8x12 slice. The times are simulated.
768 devices in a mesh: ctx: 16 (over z_hi, x), chan: 48 (over z_lo, y, core).
Axes of the slice: x: 4, y: 8, z: 12 (z_hi: 4, z_lo: 3; z = z_hi * 3 + z_lo), core: 2. Of those that a mesh axis runs over, the one named last changes fastest.
Arguments:
- query_gate: float32 [768, 131072], P('chan', 'ctx'), parts along dimension 0, may hold values from -6 to 6
- key_gate: float32 [768, 131072], P('chan', 'ctx'), parts along dimension 0, may hold values from -6 to 6
- value_rows: float32 [768, 131072], P('chan', 'ctx'), parts along dimension 0, may hold values from -6 to 6
- filter_index: int32 [768], P('chan'), parts along dimension 0, may hold values from 0 to 47
- residues: float32 [48, 16], replicated, may hold values from -1.5 to 1.5
- decay_rates: float32 [48, 16], replicated, may hold values from 7.6293945e-06 to 0.1
- skip_gain: float32 [768], P('chan'), parts along dimension 0, may hold values from 0.5 to 1.5
Outputs:
- mixed_out: float32 [768, 131072], P('chan', 'ctx'), parts along dimension 0
There are 48 independent parts, one for each index of `chan`. A program takes and returns all parts, laid end to end along the dimension named above; an argument that names none is the same for every part. Nothing has to cross between parts.
Inputs may be any that keep to these rules, and one draw needn't show every extreme that they name: `filter_index`: each channel names one of the 48 filters.
All inputs are finite; a program needn't handle non-finite values.
Results may differ from a plain program's by a relative error of at most 0.000071.
Values sent between devices are 32-bit elements; how exact they have to be, the bound alone decides.
No kernel may reach another device: no remote copies, remote signals or barrier semaphores. Data moves between devices by JAX's collectives and lax.ppermute only.
A program may use at most 32 MiB of HBM per device.

v0:
```python
import jax
import jax.numpy as jnp
from jax import lax
from jax.sharding import PartitionSpec as P


def from_everyone(shard, axis):
    copies = jnp.broadcast_to(shard, (lax.axis_size(axis), *shard.shape))
    return lax.all_to_all(copies, axis, split_axis=0, concat_axis=0, tiled=True)


def joined_along(tiles, dim):
    tiles = jnp.moveaxis(tiles, 0, dim)
    shape = tiles.shape
    return tiles.reshape(*shape[:dim], shape[dim] * shape[dim + 1], *shape[dim + 2 :])


def gathered_copies(shard, axis, dim):
    tiles = from_everyone(shard, axis)
    return joined_along(tiles, dim)


def local_modes(signal_row, rate_row, gain_row):
    length = signal_row.shape[0]
    blocks = length // 128
    within = jnp.arange(128, dtype=jnp.int32)
    lag = (within[:, None] - within[None, :]).astype(jnp.float32)
    inside = jnp.where(
        lag[None] >= 0.0, jnp.exp(-rate_row[:, None, None] * jnp.maximum(lag, 0.0)[None]), 0.0
    )
    grid = signal_row.reshape(blocks, 128)
    partial_value = jnp.einsum("nts,bs->nbt", inside, grid, precision=lax.Precision.HIGHEST)
    block_ends = partial_value[:, :, 127]
    block_ids = jnp.arange(blocks, dtype=jnp.int32)
    gap = (block_ids[:, None] - 1 - block_ids[None, :]).astype(jnp.float32)
    carry_tab = jnp.where(
        gap[None] >= 0.0,
        jnp.exp(-rate_row[:, None, None] * 128.0 * jnp.maximum(gap, 0.0)[None]),
        0.0,
    )
    carry_in = jnp.einsum("nbk,nk->nb", carry_tab, block_ends, precision=lax.Precision.HIGHEST)
    lead = jnp.exp(-rate_row[:, None] * (within.astype(jnp.float32) + 1.0)[None, :])
    states = partial_value + carry_in[:, :, None] * lead[:, None, :]
    conv_row = jnp.einsum("n,nbt->bt", gain_row, states, precision=lax.Precision.HIGHEST).reshape(
        length
    )
    return (conv_row, states[:, blocks - 1, 127])


def carry_modes(rate_row, gain_row, state_row, length):
    steps = jnp.arange(length, dtype=jnp.int32).astype(jnp.float32) + 1.0
    fade = jnp.exp(-rate_row[:, None] * steps[None, :])
    return jnp.einsum("n,nt->t", gain_row * state_row, fade, precision=lax.Precision.HIGHEST)


def per_device(query_gate, key_gate, value_rows, filter_index, residues, decay_rates, skip_gain):
    mixed_kv = key_gate * value_rows
    channels, length = mixed_kv.shape
    devices = lax.axis_size("ctx")
    here_index = lax.axis_index("ctx")
    onehot = (
        filter_index[:, None] == jnp.arange(residues.shape[0], dtype=jnp.int32)[None, :]
    ).astype(jnp.float32)
    chan_weight = jnp.dot(onehot, residues, precision=lax.Precision.HIGHEST)
    chan_rate = jnp.dot(onehot, decay_rates, precision=lax.Precision.HIGHEST)
    mode_gain = chan_weight * jnp.sqrt(-jnp.expm1(-2.0 * chan_rate))
    conv_local, end_states = lax.map(
        lambda packed: local_modes(packed[0], packed[1], packed[2]),
        (mixed_kv, chan_rate, mode_gain),
    )
    every_state = gathered_copies(end_states[None], "ctx", 0)
    dev_ids = jnp.arange(devices, dtype=jnp.int32)
    distance = (here_index - 1 - dev_ids).astype(jnp.float32)
    weight_dev = jnp.where(
        distance[:, None, None] >= 0.0,
        jnp.exp(-chan_rate[None] * float(length) * jnp.maximum(distance, 0.0)[:, None, None]),
        0.0,
    )
    carried = jnp.sum(weight_dev * every_state, axis=0)
    conv_out = conv_local + lax.map(
        lambda packed: carry_modes(packed[0], packed[1], packed[2], length),
        (chan_rate, mode_gain, carried),
    )
    return query_gate * (conv_out + skip_gain[:, None] * mixed_kv)


def solution(mesh):
    placed = (P("chan", "ctx"), P("chan", "ctx"), P("chan", "ctx"), P("chan"), P(), P(), P("chan"))
    return jax.shard_map(
        per_device, mesh=mesh, in_specs=placed, out_specs=P("chan", "ctx"), check_vma=False
    )
```

profile of v0, /device:TPU:56, one launch (start us, length us, event | category | flops | bytes accessed | tf_op | source)
XLA Modules:
  0.0 124.0 jit_solution(14311480587718227610)
XLA Ops:
  0.0 0.7 copy-done
  1.6 1.3 %mul.188 = f32[16,8192]{1,0:T(8,128)S(1)} multiply(f32[16,8192]{1,0:T(8,128)} %param.12, f32[16,8192]{1,0:T(8,128)} %param.13) | non-fusion elementwise | flops 131072 | bytes 1572864 | tf_op jit(solution)/shard_map/mul | solution.py:57
  2.9 76.7 %while.24 = (s32[]{:T(128)}, f32[16,8192]{1,0:T(8,128)S(1)}, f32[16,16]{1,0:T(8,128)S(1)}, f32[16,16]{1,0:T(8,128)S(1)}, f32[16,8192]{1,0:T(8,128)S(1)}, /*index=5*/f32[16,16]{1,0:T(8,128)S(1)}, s32[]{:T(128)}, s32[]{:T(128)}) while((s32[]{:T(128)}, f32[16,8192]{1,0:T(8,128)S(1)}, f32[16,16]{1,0:T(8,128)S(1)}, f32[16,16]{1,0:T(8,128)S(1)}, ...), condition=%wide.region_1.2_spmd, body=%wide.region_0.1_spmd.sunk | while | flops 204730752 | bytes 2547633 | solution.py:67
  3.4 1.4 %fusion.65 = f32[64,16,128]{2,0,1:T(8,128)S(1)} fusion(f32[64,128,1]{1,0,2:T(8,128)S(1)} %bitcast.76, f32[128,128]{1,0:T(8,128)S(1)} %convert_maximum_fusion.5, f32[16]{0:T(128)S(1)} %get-tuple-element.204, pred[128,128]{1,0:T(8,128)(4,1)S(1)} %convert_compare_fusion.5), kind=kOutput, calls=%fused_computation.13.clone.1 | convolution fusion | flops 201850880 | bytes 639040 | tf_op jit(solution)/shard_map/while/body/eval_jaxpr/nts,bs->nbt/dot_general | solution.py:32
  5.2 1.0 fusion.66
  6.9 0.7 fusion.67
  8.2 1.4 %fusion.65 = f32[64,16,128]{2,0,1:T(8,128)S(1)} fusion(f32[64,128,1]{1,0,2:T(8,128)S(1)} %bitcast.76, f32[128,128]{1,0:T(8,128)S(1)} %convert_maximum_fusion.5, f32[16]{0:T(128)S(1)} %get-tuple-element.204, pred[128,128]{1,0:T(8,128)(4,1)S(1)} %convert_compare_fusion.5), kind=kOutput, calls=%fused_computation.13.clone.1 | convolution fusion | flops 201850880 | bytes 639040 | tf_op jit(solution)/shard_map/while/body/eval_jaxpr/nts,bs->nbt/dot_general | solution.py:32
  10.0 1.0 fusion.66
  13.0 1.4 %fusion.65 = f32[64,16,128]{2,0,1:T(8,128)S(1)} fusion(f32[64,128,1]{1,0,2:T(8,128)S(1)} %bitcast.76, f32[128,128]{1,0:T(8,128)S(1)} %convert_maximum_fusion.5, f32[16]{0:T(128)S(1)} %get-tuple-element.204, pred[128,128]{1,0:T(8,128)(4,1)S(1)} %convert_compare_fusion.5), kind=kOutput, calls=%fused_computation.13.clone.1 | convolution fusion | flops 201850880 | bytes 639040 | tf_op jit(solution)/shard_map/while/body/eval_jaxpr/nts,bs->nbt/dot_general | solution.py:32
  14.8 1.0 fusion.66
  17.8 1.4 %fusion.65 = f32[64,16,128]{2,0,1:T(8,128)S(1)} fusion(f32[64,128,1]{1,0,2:T(8,128)S(1)} %bitcast.76, f32[128,128]{1,0:T(8,128)S(1)} %convert_maximum_fusion.5, f32[16]{0:T(128)S(1)} %get-tuple-element.204, pred[128,128]{1,0:T(8,128)(4,1)S(1)} %convert_compare_fusion.5), kind=kOutput, calls=%fused_computation.13.clone.1 | convolution fusion | flops 201850880 | bytes 639040 | tf_op jit(solution)/shard_map/while/body/eval_jaxpr/nts,bs->nbt/dot_general | solution.py:32
  19.6 1.0 fusion.66
  22.6 1.4 %fusion.65 = f32[64,16,128]{2,0,1:T(8,128)S(1)} fusion(f32[64,128,1]{1,0,2:T(8,128)S(1)} %bitcast.76, f32[128,128]{1,0:T(8,128)S(1)} %convert_maximum_fusion.5, f32[16]{0:T(128)S(1)} %get-tuple-element.204, pred[128,128]{1,0:T(8,128)(4,1)S(1)} %convert_compare_fusion.5), kind=kOutput, calls=%fused_computation.13.clone.1 | convolution fusion | flops 201850880 | bytes 639040 | tf_op jit(solution)/shard_map/while/body/eval_jaxpr/nts,bs->nbt/dot_general | solution.py:32
  24.4 1.0 fusion.66
  27.4 1.4 %fusion.65 = f32[64,16,128]{2,0,1:T(8,128)S(1)} fusion(f32[64,128,1]{1,0,2:T(8,128)S(1)} %bitcast.76, f32[128,128]{1,0:T(8,128)S(1)} %convert_maximum_fusion.5, f32[16]{0:T(128)S(1)} %get-tuple-element.204, pred[128,128]{1,0:T(8,128)(4,1)S(1)} %convert_compare_fusion.5), kind=kOutput, calls=%fused_computation.13.clone.1 | convolution fusion | flops 201850880 | bytes 639040 | tf_op jit(solution)/shard_map/while/body/eval_jaxpr/nts,bs->nbt/dot_general | solution.py:32
  29.2 1.0 fusion.66
  32.2 1.4 %fusion.65 = f32[64,16,128]{2,0,1:T(8,128)S(1)} fusion(f32[64,128,1]{1,0,2:T(8,128)S(1)} %bitcast.76, f32[128,128]{1,0:T(8,128)S(1)} %convert_maximum_fusion.5, f32[16]{0:T(128)S(1)} %get-tuple-element.204, pred[128,128]{1,0:T(8,128)(4,1)S(1)} %convert_compare_fusion.5), kind=kOutput, calls=%fused_computation.13.clone.1 | convolution fusion | flops 201850880 | bytes 639040 | tf_op jit(solution)/shard_map/while/body/eval_jaxpr/nts,bs->nbt/dot_general | solution.py:32
  34.0 1.0 fusion.66
  37.0 1.4 %fusion.65 = f32[64,16,128]{2,0,1:T(8,128)S(1)} fusion(f32[64,128,1]{1,0,2:T(8,128)S(1)} %bitcast.76, f32[128,128]{1,0:T(8,128)S(1)} %convert_maximum_fusion.5, f32[16]{0:T(128)S(1)} %get-tuple-element.204, pred[128,128]{1,0:T(8,128)(4,1)S(1)} %convert_compare_fusion.5), kind=kOutput, calls=%fused_computation.13.clone.1 | convolution fusion | flops 201850880 | bytes 639040 | tf_op jit(solution)/shard_map/while/body/eval_jaxpr/nts,bs->nbt/dot_general | solution.py:32
  38.7 1.0 fusion.66
  41.8 1.4 %fusion.65 = f32[64,16,128]{2,0,1:T(8,128)S(1)} fusion(f32[64,128,1]{1,0,2:T(8,128)S(1)} %bitcast.76, f32[128,128]{1,0:T(8,128)S(1)} %convert_maximum_fusion.5, f32[16]{0:T(128)S(1)} %get-tuple-element.204, pred[128,128]{1,0:T(8,128)(4,1)S(1)} %convert_compare_fusion.5), kind=kOutput, calls=%fused_computation.13.clone.1 | convolution fusion | flops 201850880 | bytes 639040 | tf_op jit(solution)/shard_map/while/body/eval_jaxpr/nts,bs->nbt/dot_general | solution.py:32
  43.5 1.0 fusion.66
  45.2 0.7 fusion.67
  46.6 1.4 %fusion.65 = f32[64,16,128]{2,0,1:T(8,128)S(1)} fusion(f32[64,128,1]{1,0,2:T(8,128)S(1)} %bitcast.76, f32[128,128]{1,0:T(8,128)S(1)} %convert_maximum_fusion.5, f32[16]{0:T(128)S(1)} %get-tuple-element.204, pred[128,128]{1,0:T(8,128)(4,1)S(1)} %convert_compare_fusion.5), kind=kOutput, calls=%fused_computation.13.clone.1 | convolution fusion | flops 201850880 | bytes 639040 | tf_op jit(solution)/shard_map/while/body/eval_jaxpr/nts,bs->nbt/dot_general | solution.py:32
  48.3 1.0 fusion.66
  50.0 0.7 fusion.67
  51.3 1.4 %fusion.65 = f32[64,16,128]{2,0,1:T(8,128)S(1)} fusion(f32[64,128,1]{1,0,2:T(8,128)S(1)} %bitcast.76, f32[128,128]{1,0:T(8,128)S(1)} %convert_maximum_fusion.5, f32[16]{0:T(128)S(1)} %get-tuple-element.204, pred[128,128]{1,0:T(8,128)(4,1)S(1)} %convert_compare_fusion.5), kind=kOutput, calls=%fused_computation.13.clone.1 | convolution fusion | flops 201850880 | bytes 639040 | tf_op jit(solution)/shard_map/while/body/eval_jaxpr/nts,bs->nbt/dot_general | solution.py:32
  53.1 1.0 fusion.66
  54.8 0.7 fusion.67
  56.1 1.4 %fusion.65 = f32[64,16,128]{2,0,1:T(8,128)S(1)} fusion(f32[64,128,1]{1,0,2:T(8,128)S(1)} %bitcast.76, f32[128,128]{1,0:T(8,128)S(1)} %convert_maximum_fusion.5, f32[16]{0:T(128)S(1)} %get-tuple-element.204, pred[128,128]{1,0:T(8,128)(4,1)S(1)} %convert_compare_fusion.5), kind=kOutput, calls=%fused_computation.13.clone.1 | convolution fusion | flops 201850880 | bytes 639040 | tf_op jit(solution)/shard_map/while/body/eval_jaxpr/nts,bs->nbt/dot_general | solution.py:32
  57.9 1.0 fusion.66
  59.6 0.7 fusion.67
  60.9 1.4 %fusion.65 = f32[64,16,128]{2,0,1:T(8,128)S(1)} fusion(f32[64,128,1]{1,0,2:T(8,128)S(1)} %bitcast.76, f32[128,128]{1,0:T(8,128)S(1)} %convert_maximum_fusion.5, f32[16]{0:T(128)S(1)} %get-tuple-element.204, pred[128,128]{1,0:T(8,128)(4,1)S(1)} %convert_compare_fusion.5), kind=kOutput, calls=%fused_computation.13.clone.1 | convolution fusion | flops 201850880 | bytes 639040 | tf_op jit(solution)/shard_map/while/body/eval_jaxpr/nts,bs->nbt/dot_general | solution.py:32
  62.7 1.0 fusion.66
  65.7 1.4 %fusion.65 = f32[64,16,128]{2,0,1:T(8,128)S(1)} fusion(f32[64,128,1]{1,0,2:T(8,128)S(1)} %bitcast.76, f32[128,128]{1,0:T(8,128)S(1)} %convert_maximum_fusion.5, f32[16]{0:T(128)S(1)} %get-tuple-element.204, pred[128,128]{1,0:T(8,128)(4,1)S(1)} %convert_compare_fusion.5), kind=kOutput, calls=%fused_computation.13.clone.1 | convolution fusion | flops 201850880 | bytes 639040 | tf_op jit(solution)/shard_map/while/body/eval_jaxpr/nts,bs->nbt/dot_general | solution.py:32
  67.5 1.0 fusion.66
  70.5 1.4 %fusion.65 = f32[64,16,128]{2,0,1:T(8,128)S(1)} fusion(f32[64,128,1]{1,0,2:T(8,128)S(1)} %bitcast.76, f32[128,128]{1,0:T(8,128)S(1)} %convert_maximum_fusion.5, f32[16]{0:T(128)S(1)} %get-tuple-element.204, pred[128,128]{1,0:T(8,128)(4,1)S(1)} %convert_compare_fusion.5), kind=kOutput, calls=%fused_computation.13.clone.1 | convolution fusion | flops 201850880 | bytes 639040 | tf_op jit(solution)/shard_map/while/body/eval_jaxpr/nts,bs->nbt/dot_general | solution.py:32
  72.3 1.0 fusion.66
  74.0 0.7 fusion.67
  75.3 1.4 %fusion.65 = f32[64,16,128]{2,0,1:T(8,128)S(1)} fusion(f32[64,128,1]{1,0,2:T(8,128)S(1)} %bitcast.76, f32[128,128]{1,0:T(8,128)S(1)} %convert_maximum_fusion.5, f32[16]{0:T(128)S(1)} %get-tuple-element.204, pred[128,128]{1,0:T(8,128)(4,1)S(1)} %convert_compare_fusion.5), kind=kOutput, calls=%fused_computation.13.clone.1 | convolution fusion | flops 201850880 | bytes 639040 | tf_op jit(solution)/shard_map/while/body/eval_jaxpr/nts,bs->nbt/dot_general | solution.py:32
  77.1 1.0 fusion.66
  78.8 0.7 fusion.67
  79.6 0.7 reshape.201
  80.3 17.1 %all-to-all-start = ((f32[16,1,256]{2,1,0:T(1,128)}), f32[16,1,256]{2,1,0:T(1,128)S(1)}, u32[]{:S(2)}, u32[]{:S(2)}) async-start(f32[16,1,256]{2,1,0:T(1,128)} %reshape.201), calls=%async_computation | async-start | bytes 32768 | tf_op jit(solution)/shard_map/all_to_all | solution.py:9
  97.4 12.4 %all-to-all-done = f32[16,1,256]{2,1,0:T(1,128)S(1)} async-done(((f32[16,1,256]{2,1,0:T(1,128)}), f32[16,1,256]{2,1,0:T(1,128)S(1)}, u32[]{:S(2)}, u32[]{:S(2)}) %all-to-all-start) | async-done | bytes 16416 | tf_op jit(solution)/shard_map/all_to_all | solution.py:9
  110.3 0.7 reduce.4
  111.3 11.1 %while.25 = (s32[]{:T(128)}, f32[16,8192]{1,0:T(8,128)S(1)}, f32[16,16]{1,0:T(8,128)S(1)}, f32[16,16]{1,0:T(8,128)S(1)}, f32[16,16]{1,0:T(8,128)S(1)}, /*index=5*/s32[]{:T(128)}, s32[]{:T(128)}) while((s32[]{:T(128)}, f32[16,8192]{1,0:T(8,128)S(1)}, f32[16,16]{1,0:T(8,128)S(1)}, f32[16,16]{1,0:T(8,128)S(1)}, f32[16,16]{1,0:T(8,128)S(1)}, ...), condition=%wide.region_4.5_spmd, body=%wide.region_3.4_spmd.sunk | while | flops 1720354 | bytes 165601 | solution.py:80
  123.1 0.9 add_multiply_fusion
  (365 shorter events, 44.8 us)
Async XLA Ops:
  0.0 0.7 copy-start
  0.0 0.7 copy-start.4
  0.7 0.7 copy-start.3
  80.3 29.5 %all-to-all-start = ((f32[16,1,256]{2,1,0:T(1,128)}), f32[16,1,256]{2,1,0:T(1,128)S(1)}, u32[]{:S(2)}, u32[]{:S(2)}) async-start(f32[16,1,256]{2,1,0:T(1,128)} %reshape.201), calls=%async_computation | async-start | bytes 32768 | tf_op jit(solution)/shard_map/all_to_all | solution.py:9
  111.2 11.2 %copy-start.1 = (f32[16,8192]{1,0:T(8,128)S(1)}, f32[16,8192]{1,0:T(8,128)}, u32[]{:S(2)}) copy-start(f32[16,8192]{1,0:T(8,128)} %param.11) | copy-start | bytes 1572868
  122.4 0.7 copy-start.2
where the time goes:
time: 124 us
  matrix products  57.2 us (46%)
  local copies, waits for them, and re-layouts  17.7 us (14%)
  other arithmetic  17.5 us (14%)
  starting transfers between devices  17.1 us (14%)
  waiting for transfers between devices  12.4 us (10%)
  loops' own time  2.11 us (2%)
    dot_general x16, matrix products, local_modes(): jnp.einsum('nts,bs->nbt', inside, grid, precision=lax.Precision.HIGHEST)  22 us
    all_to_all x1, starting transfers between devices, from_everyone(): return lax.all_to_all(copies, axis, split_axis=0, concat_axis=0, tiled=True)  17.1 us
    dot_general x16, matrix products, local_modes(): jnp.einsum('nbk,nk->nb', carry_tab, block_ends, precision=lax.Precision.H...  16.6 us
    all_to_all x1, waiting for transfers between devices, from_everyone(): return lax.all_to_all(copies, axis, split_axis=0, concat_axis=0, tiled=True)  12.4 us
    dot_general x16, matrix products, local_modes(): jnp.einsum('n,nbt->bt', gain_row, states, precision=lax.Precision.HIGHEST)  10.4 us
    dot_general x16, matrix products, carry_modes(): jnp.einsum('n,nt->t', gain_row * state_row, fade, precision=lax.Precision...  7.76 us
    slice x16, local copies, waits for them, and re-layouts, local_modes(): block_ends = partial_value[:, :, 127]  6.28 us
    dynamic_update_slice x48, local copies, waits for them, and re-layouts, per_device(): lax.map(lambda packed: local_modes(packed[0], packed[1], packed[2]), (mix...  5.3 us
  transfers between devices with their start and end apart: 1, of which 1 were waited for; matrix products, arithmetic and copies ran while one was open for 0% of the time, Pallas kernels for 0%

commit v1 on v0

v1 whole, which is shorter than its diff:
```python
import jax
import jax.numpy as jnp
from jax import lax
from jax.experimental import pallas as pl
from jax.experimental.pallas import tpu as pltpu
from jax.sharding import PartitionSpec as P

BLOCK = 128
HALF = 8
F32, BF16 = jnp.float32, jnp.bfloat16
NN = (((1,), (0,)), ((), ()))
NT = (((1,), (1,)), ((), ()))


def split(value):
    high = value.astype(BF16)
    return high, (value - high.astype(F32)).astype(BF16)


def iota(shape, dim):
    return lax.broadcasted_iota(jnp.int32, shape, dim)


def lanes_of(table, modes):
    channels = table.shape[0]
    spread_shape = (modes, channels * modes)
    spread = (iota(spread_shape, 1) % modes == iota(spread_shape, 0)).astype(F32)
    wide = lax.dot_general(table, spread, NN, precision=lax.Precision.HIGHEST, preferred_element_type=F32)
    own = iota(wide.shape, 1) // modes == iota(wide.shape, 0)
    return jnp.sum(jnp.where(own, wide, 0.0), axis=0, keepdims=True)


def one_minus_exp(x):
    series = jnp.full_like(x, 1.0)
    for k in range(9, 1, -1):
        series = 1.0 - x * series * (1.0 / k)
    return jnp.where(x <= 0.25, x * series, 1.0 - jnp.exp(-x))


def state_kernel(index_ref, rates_ref, residues_ref, key_ref, value_ref, end_ref, rate_ref, gain_ref, rate_rows, weight_rows):
    channels, modes = rate_rows.shape
    blocks = key_ref.shape[1] // BLOCK
    for c in range(channels):
        rate_rows[c : c + 1, :] = rates_ref[pl.ds(index_ref[c], 1), :]
        weight_rows[c : c + 1, :] = residues_ref[pl.ds(index_ref[c], 1), :]
    rates = rate_rows[...]
    gains = weight_rows[...] * jnp.sqrt(one_minus_exp(2.0 * rates))
    rate_row = lanes_of(rates, modes)
    gain_row = lanes_of(gains, modes)
    own = iota((HALF, BLOCK), 1) // modes == iota((HALF, BLOCK), 0)
    for g in range(channels // HALF):
        lanes = slice(g * BLOCK, (g + 1) * BLOCK)
        rate = rate_row[:, lanes]
        rate_ref[g : g + 1, :] = rate
        gain_ref[g : g + 1, :] = gain_row[:, lanes]
        to_end = (BLOCK - 1 - iota((BLOCK, BLOCK), 0)).astype(F32)
        fade_high, fade_low = split(jnp.exp(-rate * to_end))
        fades = jnp.concatenate([fade_high, fade_high, fade_low], axis=0)
        later = (BLOCK * (blocks - 1 - iota((blocks, BLOCK), 0))).astype(F32)
        block_fade = jnp.exp(-rate * later)
        rows = slice(g * HALF, (g + 1) * HALF)
        total = jnp.zeros((HALF, BLOCK), F32)
        for start in range(0, blocks, 16):
            mixed = jnp.concatenate(
                [
                    key_ref[rows, b * BLOCK : (b + 1) * BLOCK] * value_ref[rows, b * BLOCK : (b + 1) * BLOCK]
                    for b in range(start, start + 16)
                ],
                axis=0,
            )
            high, low = split(mixed)
            states = lax.dot_general(
                jnp.concatenate([high, low, high], axis=1), fades, NN, preferred_element_type=F32
            )
            for b in range(16):
                total = total + block_fade[start + b : start + b + 1, :] * states[b * HALF : (b + 1) * HALF, :]
        end_ref[g : g + 1, :] = jnp.sum(jnp.where(own, total, 0.0), axis=0, keepdims=True)


def output_kernel(modes, query_ref, key_ref, value_ref, skip_ref, rate_ref, gain_ref, carried_ref, out_ref, mixed_rows, conv_rows, carry_rows):
    channels = query_ref.shape[0]
    blocks = key_ref.shape[1] // BLOCK
    own = iota((HALF, BLOCK), 1) // modes == iota((HALF, BLOCK), 0)
    own_gain = iota((channels, BLOCK), 1) // modes
    square = (BLOCK, BLOCK)
    causal = iota(square, 1) >= iota(square, 0)
    for g in range(channels // HALF):
        rows = slice(g * HALF, (g + 1) * HALF)
        rate, gain = rate_ref[g : g + 1, :], gain_ref[g : g + 1, :]
        place = iota(square, 0).astype(F32)
        tail = gain * jnp.exp(-rate * place)
        sums = (iota((HALF, BLOCK), 1) // modes == iota((HALF, BLOCK), 0)).astype(F32)
        taps = lax.dot_general(sums, tail, NT, precision=lax.Precision.HIGHEST, preferred_element_type=F32)
        to_end = BLOCK - 1.0 - place
        fade_high, fade_low = split(jnp.exp(-rate * to_end))
        fades = jnp.concatenate([fade_high, fade_high, fade_low], axis=0)
        lead_high, lead_low = split(tail * jnp.exp(-rate))
        leads = jnp.concatenate([lead_high, lead_high, lead_low], axis=1)
        step = jnp.exp(-rate * float(BLOCK))
        state = jnp.broadcast_to(carried_ref[g : g + 1, :], (HALF, BLOCK))
        for start in range(0, blocks, 16):
            mixed = jnp.concatenate(
                [
                    key_ref[rows, b * BLOCK : (b + 1) * BLOCK] * value_ref[rows, b * BLOCK : (b + 1) * BLOCK]
                    for b in range(start, start + 16)
                ],
                axis=0,
            )
            mixed_rows[start * HALF : (start + 16) * HALF, :] = mixed
            high, low = split(mixed)
            states = lax.dot_general(
                jnp.concatenate([high, low, high], axis=1), fades, NN, preferred_element_type=F32
            )
            entering = []
            for b in range(16):
                entering.append(jnp.where(own, state, 0.0))
                state = state * step + states[b * HALF : (b + 1) * HALF, :]
            high, low = split(jnp.concatenate(entering, axis=0))
            carry_rows[start * HALF : (start + 16) * HALF, :] = lax.dot_general(
                jnp.concatenate([high, low, high], axis=1), leads, NT, preferred_element_type=F32
            )
        for c in range(HALF):
            shifted = pltpu.roll(jnp.broadcast_to(taps[c : c + 1, :], square), 0, 1, stride=1, stride_axis=0)
            tap_high, tap_low = split(jnp.where(causal, shifted, 0.0))
            weights = jnp.concatenate([tap_high, tap_high, tap_low], axis=0)
            high, low = split(mixed_rows[pl.ds(c, blocks, stride=HALF), :])
            conv_rows[pl.ds(c, blocks, stride=HALF), :] = lax.dot_general(
                jnp.concatenate([high, low, high], axis=1), weights, NN, preferred_element_type=F32
            )
        skip = skip_ref[rows, :]
        for b in range(blocks):
            here = slice(b * HALF, (b + 1) * HALF)
            lanes = slice(b * BLOCK, (b + 1) * BLOCK)
            conv = conv_rows[here, :] + carry_rows[here, :] + skip * mixed_rows[here, :]
            out_ref[rows, lanes] = query_ref[rows, lanes] * conv


VMEM = pl.BlockSpec(memory_space=pltpu.VMEM)


def per_device(query_gate, key_gate, value_rows, filter_index, residues, decay_rates, skip_gain):
    channels, length = key_gate.shape
    modes = residues.shape[1]
    blocks = length // BLOCK
    groups = channels // HALF
    row = jax.ShapeDtypeStruct((groups, BLOCK), F32)
    ends, rate, gain = pl.pallas_call(
        state_kernel,
        out_shape=(row, row, row),
        in_specs=[pl.BlockSpec(memory_space=pltpu.SMEM)] + [VMEM] * 4,
        out_specs=(VMEM, VMEM, VMEM),
        scratch_shapes=[pltpu.VMEM((channels, modes), F32), pltpu.VMEM((channels, modes), F32)],
        compiler_params=pltpu.CompilerParams(vmem_limit_bytes=16 * 2**20),
        cost_estimate=pl.CostEstimate(flops=2 * 3 * 1024 * 128 * 128, bytes_accessed=2**20, transcendentals=2**16),
    )(filter_index, decay_rates, residues, key_gate, value_rows)

    devices = lax.axis_size("ctx")
    here = lax.axis_index("ctx")
    copies = jnp.broadcast_to(ends.reshape(1, 1, -1), (devices, 1, ends.size))
    every = lax.all_to_all(copies, "ctx", split_axis=0, concat_axis=0, tiled=True).reshape(devices, groups, BLOCK)
    distance = (here - 1 - jnp.arange(devices, dtype=jnp.int32)).astype(F32)[:, None, None]
    fade = jnp.where(distance >= 0.0, jnp.exp(-rate[None] * float(length) * jnp.maximum(distance, 0.0)), 0.0)
    carried = jnp.sum(fade * every, axis=0)

    rows = pltpu.VMEM((blocks * HALF, BLOCK), F32)
    return pl.pallas_call(
        lambda *refs: output_kernel(modes, *refs),
        out_shape=jax.ShapeDtypeStruct(query_gate.shape, F32),
        in_specs=[VMEM] * 7,
        out_specs=VMEM,
        scratch_shapes=[rows, rows, rows],
        compiler_params=pltpu.CompilerParams(vmem_limit_bytes=24 * 2**20),
        cost_estimate=pl.CostEstimate(flops=2 * 9 * 1024 * 128 * 128, bytes_accessed=2**21, transcendentals=2**16),
    )(query_gate, key_gate, value_rows, skip_gain[:, None], rate, gain, carried)


def solution(mesh):
    placed = (P("chan", "ctx"), P("chan", "ctx"), P("chan", "ctx"), P("chan"), P(), P(), P("chan"))
    return jax.shard_map(
        per_device, mesh=mesh, in_specs=placed, out_specs=P("chan", "ctx"), check_vma=False
    )
```

time: 124 us -> 39.1 us (0.32)
  the two profiles are of different devices: /device:TPU:56 before, /device:TPU:8 now
where the time goes in v1:
time: 39.1 us; the launch traced here: 38.8 us
  starting transfers between devices  17.1 us (44%)
  waiting for transfers between devices  11.6 us (30%)
  local copies, waits for them, and re-layouts  5.93 us (15%)
  Pallas kernels  3.95 us (10%)
    all_to_all x1, starting transfers between devices, per_device(): lax.all_to_all(copies, 'ctx', split_axis=0, concat_axis=0, tiled=True)  17.1 us
    all_to_all x1, waiting for transfers between devices, per_device(): lax.all_to_all(copies, 'ctx', split_axis=0, concat_axis=0, tiled=True)  11.6 us
    unnamed x18, local copies, waits for them, and re-layouts  5.22 us
    pallas_call x1, Pallas kernels, per_device(): pl.pallas_call(lambda *refs: output_kernel(modes, *refs), out_shape=jax.S...  2.84 us
    pallas_call x1, Pallas kernels, per_device(): pl.pallas_call(state_kernel, out_shape=(row, row, row), in_specs=[pl.Bloc...  1.12 us
  transfers between devices with their start and end apart: 1, of which 1 were waited for; matrix products, arithmetic and copies ran while one was open for 0% of the time, Pallas kernels for 0%

profile of v1, /device:TPU:8, one launch (start us, length us, event | category | flops | bytes accessed | tf_op | source)
XLA Modules:
  0.0 38.8 jit_solution(2130850210492754211)
XLA Ops:
  0.0 0.0 copy-start.6
  0.0 0.8 %copy.15.residues_ref = f32[48,16]{1,0:T(8,128)S(1)} copy(f32[48,16]{0,1:T(8,128)} %param.11) | data formatting | bytes 6144 | tf_op args[4]
  0.8 0.0 copy-done.6
  0.8 0.0 copy-start.5
  0.8 0.1 copy.14.rates_ref
  0.9 0.6 %copy-done.5 = s32[16]{0:T(128)S(1)} copy-done((s32[16]{0:T(128)S(1)}, s32[16]{0:T(128)}, u32[]{:S(2)}) %copy-start.5) | copy-done | bytes 88
  1.5 0.0 copy-start
  1.5 1.0 %copy-done = f32[16,8192]{1,0:T(8,128)S(1)} copy-done((f32[16,8192]{1,0:T(8,128)S(1)}, f32[16,8192]{1,0:T(8,128)}, u32[]{:S(2)}) %copy-start) | copy-done | bytes 524312
  2.5 0.0 copy-start.2
  2.5 1.0 %copy-done.2 = f32[16,8192]{1,0:T(8,128)S(1)} copy-done((f32[16,8192]{1,0:T(8,128)S(1)}, f32[16,8192]{1,0:T(8,128)}, u32[]{:S(2)}) %copy-start.2) | copy-done | bytes 524312
  3.5 0.0 copy-start.1
  3.5 0.0 copy-start.3
  3.5 1.1 %shard_map.73 = (f32[2,128]{1,0:T(2,128)S(1)}, f32[2,128]{1,0:T(2,128)S(1)}, f32[2,128]{1,0:T(2,128)S(1)}) custom-call(s32[16]{0:T(128)S(1)} %copy-done.5, f32[48,16]{1,0:T(8,128)S(1)} %copy.14.rates_ref, f32[48,16]{1,0:T(8,128)S(1)} %copy.15.residues_ref, f32[16,8192]{1,0:T(8,128)S(1)} %copy-done, f32[16,8192]{1,0:T(8,128)S(1)} %copy-done.2), custom_call_target="tpu_custom_call" | custom-call | flops 100663296 | bytes 1048576 | tf_op jit(solution)/shard_map/pallas_call | solution.py:147
  4.7 0.6 %broadcast_in_dim.28 = f32[16,1,256]{2,1,0:T(1,128)} broadcast(f32[256]{0:T(256)S(1)} %bitcast.6), dimensions={2} | broadcast | bytes 17408 | tf_op jit(solution)/shard_map/broadcast_in_dim | solution.py:159
  5.3 17.1 %all-to-all-start = ((f32[16,1,256]{2,1,0:T(1,128)}), f32[16,1,256]{2,1,0:T(1,128)S(1)}, u32[]{:S(2)}, u32[]{:S(2)}) async-start(f32[16,1,256]{2,1,0:T(1,128)} %broadcast_in_dim.28), calls=%async_computation | async-start | bytes 32768 | tf_op jit(solution)/shard_map/all_to_all | solution.py:160
  22.4 0.0 copy-start.7
  22.4 0.6 %copy-done.7 = f32[16]{0:T(128)S(1)} copy-done((f32[16]{0:T(128)S(1)}, f32[16]{0:T(128)}, u32[]{:S(2)}) %copy-start.7) | copy-done | bytes 88
  23.1 0.1 copy.17.refs_3_
  23.1 11.6 %all-to-all-done = f32[16,1,256]{2,1,0:T(1,128)S(1)} async-done(((f32[16,1,256]{2,1,0:T(1,128)}), f32[16,1,256]{2,1,0:T(1,128)S(1)}, u32[]{:S(2)}, u32[]{:S(2)}) %all-to-all-start) | async-done | bytes 16416 | tf_op jit(solution)/shard_map/all_to_all | solution.py:160
  34.8 0.1 fusion.1
  34.9 0.0 copy-done.1
  34.9 0.0 copy-done.3
  34.9 0.0 copy-start.4
  34.9 1.0 %copy-done.4 = f32[16,8192]{1,0:T(8,128)S(1)} copy-done((f32[16,8192]{1,0:T(8,128)S(1)}, f32[16,8192]{1,0:T(8,128)}, u32[]{:S(2)}) %copy-start.4) | copy-done | bytes 524312
  35.9 2.8 %shard_map.74 = f32[16,8192]{1,0:T(8,128)} custom-call(f32[16,8192]{1,0:T(8,128)S(1)} %copy-done.4, f32[16,8192]{1,0:T(8,128)S(1)} %copy-done.1, f32[16,8192]{1,0:T(8,128)S(1)} %copy-done.3, f32[16,1]{1,0:T(8,128)S(1)} %copy.17.refs_3_, f32[2,128]{1,0:T(2,128)S(1)} %get-tuple-element.8.refs_4_, f32[2,128]{1,0:T(2,128)S(1)} %get-tuple-element.9.refs_5_, ...), custom_call_target="tpu_custom_call" | custom-call | flops 301989888 | bytes 2097152 | tf_op jit(solution)/shard_map/pallas_call | solution.py:166
  (3 shorter events, 0.0 us)
Async XLA Ops:
  0.0 0.8 %copy-start.6 = (f32[48,16]{0,1:T(8,128)S(1)}, f32[48,16]{0,1:T(8,128)}, u32[]{:S(2)}) copy-start(f32[48,16]{0,1:T(8,128)} %param.12) | copy-start | bytes 9220
  0.8 0.7 %copy-start.5 = (s32[16]{0:T(128)S(1)}, s32[16]{0:T(128)}, u32[]{:S(2)}) copy-start(s32[16]{0:T(128)} %index_ref.1) | copy-start | bytes 196
  1.5 1.0 %copy-start = (f32[16,8192]{1,0:T(8,128)S(1)}, f32[16,8192]{1,0:T(8,128)}, u32[]{:S(2)}) copy-start(f32[16,8192]{1,0:T(8,128)} %refs_1_.1) | copy-start | bytes 1572868
  2.5 1.0 %copy-start.2 = (f32[16,8192]{1,0:T(8,128)S(1)}, f32[16,8192]{1,0:T(8,128)}, u32[]{:S(2)}) copy-start(f32[16,8192]{1,0:T(8,128)} %refs_2_.1) | copy-start | bytes 1572868
  3.5 31.3 %copy-start.1 = (f32[16,8192]{1,0:T(8,128)S(1)}, f32[16,8192]{1,0:T(8,128)}, u32[]{:S(2)}) copy-start(f32[16,8192]{1,0:T(8,128)} %refs_1_.1) | copy-start | bytes 1572868
  3.5 31.4 %copy-start.3 = (f32[16,8192]{1,0:T(8,128)S(1)}, f32[16,8192]{1,0:T(8,128)}, u32[]{:S(2)}) copy-start(f32[16,8192]{1,0:T(8,128)} %refs_2_.1) | copy-start | bytes 1572868
  5.3 29.5 %all-to-all-start = ((f32[16,1,256]{2,1,0:T(1,128)}), f32[16,1,256]{2,1,0:T(1,128)S(1)}, u32[]{:S(2)}, u32[]{:S(2)}) async-start(f32[16,1,256]{2,1,0:T(1,128)} %broadcast_in_dim.28), calls=%async_computation | async-start | bytes 32768 | tf_op jit(solution)/shard_map/all_to_all | solution.py:160
  22.4 0.7 %copy-start.7 = (f32[16]{0:T(128)S(1)}, f32[16]{0:T(128)}, u32[]{:S(2)}) copy-start(f32[16]{0:T(128)} %param.13) | copy-start | bytes 196
  34.9 1.0 %copy-start.4 = (f32[16,8192]{1,0:T(8,128)S(1)}, f32[16,8192]{1,0:T(8,128)}, u32[]{:S(2)}) copy-start(f32[16,8192]{1,0:T(8,128)} %refs_0_.1) | copy-start | bytes 1572868

commit v2 on v1

v2 whole, which is shorter than its diff:
```python
import jax
import jax.numpy as jnp
from jax import lax
from jax.experimental import pallas as pl
from jax.experimental.pallas import tpu as pltpu
from jax.sharding import PartitionSpec as P

BLOCK = 128
HALF = 8
F32, BF16 = jnp.float32, jnp.bfloat16
NN = (((1,), (0,)), ((), ()))
NT = (((1,), (1,)), ((), ()))


def split(value):
    high = value.astype(BF16)
    return high, (value - high.astype(F32)).astype(BF16)


def iota(shape, dim):
    return lax.broadcasted_iota(jnp.int32, shape, dim)


def one_minus_exp(x):
    series = jnp.full_like(x, 1.0)
    for k in range(9, 1, -1):
        series = 1.0 - x * series * (1.0 / k)
    return jnp.where(x <= 0.25, x * series, 1.0 - jnp.exp(-x))


def state_kernel(
    side, index_hbm, rates_hbm, residues_hbm, skip_hbm, key_hbm, value_hbm, query_hbm,
    end_ref, rate_ref, gain_ref, far_ref, row_ref, before_ref, skip_ref, mixed_ref, query_ref,
    index_ref, rates_ref, residues_ref, skip_row, key_ref, value_ref, sems,
):
    channels, length = key_ref.shape
    modes, filters = rates_ref.shape
    blocks = length // BLOCK
    groups = channels // HALF
    small = [
        pltpu.make_async_copy(source, target, sems.at[2 * groups + 1 + i])
        for i, (source, target) in enumerate(
            ((index_hbm, index_ref), (rates_hbm, rates_ref), (residues_hbm, residues_ref), (skip_hbm, skip_row))
        )
    ]
    for copy in small:
        copy.start()
    loads = []
    for g in range(groups):
        rows = slice(g * HALF, (g + 1) * HALF)
        pair = [
            pltpu.make_async_copy(source.at[rows, :], target.at[rows, :], sems.at[2 * g + i])
            for i, (source, target) in enumerate(((key_hbm, key_ref), (value_hbm, value_ref)))
        ]
        for copy in pair:
            copy.start()
        loads.append(pair)
    query_load = pltpu.make_async_copy(query_hbm, query_ref, sems.at[2 * groups])
    query_load.start()
    for copy in small:
        copy.wait()

    wide = (channels, channels * modes)
    spread = (iota(wide, 1) // modes == iota(wide, 0)).astype(BF16)
    chosen = (iota((filters, channels), 0) == index_ref[...]).astype(BF16)
    chosen = lax.dot_general(chosen, spread, NN, preferred_element_type=F32)
    own_mode = iota((modes, channels * modes), 1) % modes == iota((modes, channels * modes), 0)

    def lanes_of(table):
        spread_table = lax.dot_general(
            table, chosen, NN, precision=lax.Precision.HIGHEST, preferred_element_type=F32
        )
        return jnp.sum(jnp.where(own_mode, spread_table, 0.0), axis=0, keepdims=True)

    rate_row = lanes_of(rates_ref[...])
    gain_row = lanes_of(residues_ref[...]) * jnp.sqrt(one_minus_exp(2.0 * rate_row))
    own = iota((HALF, BLOCK), 1) // modes == iota((HALF, BLOCK), 0)
    place = lax.axis_index("ctx") % side
    same = iota((channels, channels), 0) == iota((channels, channels), 1)
    skip = jnp.sum(jnp.where(same, skip_row[...], 0.0), axis=1, keepdims=True)
    skip_ref[...] = jnp.broadcast_to(skip, skip_ref.shape)
    for g in range(groups):
        lanes = slice(g * BLOCK, (g + 1) * BLOCK)
        rate = rate_row[:, lanes]
        here = slice(g, g + 1)
        rate_ref[here, :] = rate
        gain_ref[here, :] = gain_row[:, lanes]
        passed = -rate * float(length)
        far_ref[0, here, :] = jnp.exp(passed * float(side))
        far_ref[1, here, :] = jnp.exp(passed * place.astype(F32))
        for x in range(side):
            row_ref[x, here, :] = jnp.exp(passed * float(side - 1 - x))
            gap = (place - 1 - x).astype(F32)
            before_ref[x, here, :] = jnp.where(gap >= 0.0, jnp.exp(passed * jnp.maximum(gap, 0.0)), 0.0)
        to_end = (BLOCK - 1 - iota((BLOCK, BLOCK), 0)).astype(F32)
        fade_high, fade_low = split(jnp.exp(-rate * to_end))
        fades = jnp.concatenate([fade_high, fade_high, fade_low], axis=0)
        later = (BLOCK * (blocks - 1 - iota((blocks, BLOCK), 0))).astype(F32)
        block_fade = jnp.exp(-rate * later)
        rows = slice(g * HALF, (g + 1) * HALF)
        total = jnp.zeros((HALF, BLOCK), F32)
        for copy in loads[g]:
            copy.wait()
        for start in range(0, blocks, 16):
            mixed = jnp.concatenate(
                [
                    key_ref[rows, b * BLOCK : (b + 1) * BLOCK] * value_ref[rows, b * BLOCK : (b + 1) * BLOCK]
                    for b in range(start, start + 16)
                ],
                axis=0,
            )
            mixed_ref[g, start * HALF : (start + 16) * HALF, :] = mixed
            high, low = split(mixed)
            states = lax.dot_general(
                jnp.concatenate([high, low, high], axis=1), fades, NN, preferred_element_type=F32
            )
            for b in range(16):
                total = total + block_fade[start + b : start + b + 1, :] * states[b * HALF : (b + 1) * HALF, :]
        end_ref[here, :] = jnp.sum(jnp.where(own, total, 0.0), axis=0, keepdims=True)
    query_load.wait()


def output_kernel(
    modes, query_ref, mixed_ref, skip_ref, rate_ref, gain_ref, far_ref, near_ref, carried_ref, out_ref, conv_rows, carry_rows
):
    channels, length = query_ref.shape
    blocks = length // BLOCK
    own = iota((HALF, BLOCK), 1) // modes == iota((HALF, BLOCK), 0)
    square = (BLOCK, BLOCK)
    causal = iota(square, 1) >= iota(square, 0)
    for g in range(channels // HALF):
        rows = slice(g * HALF, (g + 1) * HALF)
        here = slice(g, g + 1)
        rate, gain = rate_ref[here, :], gain_ref[here, :]
        place = iota(square, 0).astype(F32)
        tail = gain * jnp.exp(-rate * place)
        taps = lax.dot_general(
            own.astype(F32), tail, NT, precision=lax.Precision.HIGHEST, preferred_element_type=F32
        )
        to_end = BLOCK - 1.0 - place
        fade_high, fade_low = split(jnp.exp(-rate * to_end))
        fades = jnp.concatenate([fade_high, fade_high, fade_low], axis=0)
        lead_high, lead_low = split(tail * jnp.exp(-rate))
        leads = jnp.concatenate([lead_high, lead_high, lead_low], axis=1)
        step = jnp.exp(-rate * float(BLOCK))
        entered = near_ref[here, :] + far_ref[1, here, :] * carried_ref[here, :]
        state = jnp.broadcast_to(entered, (HALF, BLOCK))
        for start in range(0, blocks, 16):
            some = slice(start * HALF, (start + 16) * HALF)
            high, low = split(mixed_ref[g, some, :])
            states = lax.dot_general(
                jnp.concatenate([high, low, high], axis=1), fades, NN, preferred_element_type=F32
            )
            entering = []
            for b in range(16):
                entering.append(jnp.where(own, state, 0.0))
                state = state * step + states[b * HALF : (b + 1) * HALF, :]
            high, low = split(jnp.concatenate(entering, axis=0))
            carry_rows[some, :] = lax.dot_general(
                jnp.concatenate([high, low, high], axis=1), leads, NT, preferred_element_type=F32
            )
        for c in range(HALF):
            shifted = pltpu.roll(jnp.broadcast_to(taps[c : c + 1, :], square), 0, 1, stride=1, stride_axis=0)
            tap_high, tap_low = split(jnp.where(causal, shifted, 0.0))
            weights = jnp.concatenate([tap_high, tap_high, tap_low], axis=0)
            high, low = split(mixed_ref[g, pl.ds(c, blocks, stride=HALF), :])
            conv_rows[pl.ds(c, blocks, stride=HALF), :] = lax.dot_general(
                jnp.concatenate([high, low, high], axis=1), weights, NN, preferred_element_type=F32
            )
        skip = skip_ref[rows, :]
        for b in range(blocks):
            some = slice(b * HALF, (b + 1) * HALF)
            lanes = slice(b * BLOCK, (b + 1) * BLOCK)
            conv = conv_rows[some, :] + carry_rows[some, :] + skip * mixed_ref[g, some, :]
            out_ref[rows, lanes] = query_ref[rows, lanes] * conv


VMEM = pl.BlockSpec(memory_space=pltpu.VMEM)
HBM = pl.BlockSpec(memory_space=pltpu.HBM)
SIDE = 4


def shape(*dims):
    return jax.ShapeDtypeStruct(dims, F32)


def per_device(query_gate, key_gate, value_rows, filter_index, residues, decay_rates, skip_gain):
    channels, length = key_gate.shape
    modes = residues.shape[1]
    blocks = length // BLOCK
    groups = channels // HALF
    line = (groups, BLOCK)
    ends, rate, gain, far, in_row, before, skip, mixed, query = pl.pallas_call(
        lambda *refs: state_kernel(SIDE, *refs),
        out_shape=(
            shape(*line), shape(*line), shape(*line), shape(2, *line), shape(SIDE, *line), shape(SIDE, *line),
            shape(channels, BLOCK), shape(groups, blocks * HALF, BLOCK), shape(channels, length),
        ),
        in_specs=[HBM] * 7,
        out_specs=(VMEM,) * 9,
        scratch_shapes=[
            pltpu.VMEM((1, channels), jnp.int32),
            pltpu.VMEM((modes, residues.shape[0]), F32),
            pltpu.VMEM((modes, residues.shape[0]), F32),
            pltpu.VMEM((1, channels), F32),
            pltpu.VMEM((channels, length), F32),
            pltpu.VMEM((channels, length), F32),
            pltpu.SemaphoreType.DMA((2 * groups + 5,)),
        ],
        compiler_params=pltpu.CompilerParams(vmem_limit_bytes=16 * 2**20),
        cost_estimate=pl.CostEstimate(flops=2 * 3 * 1024 * 128 * 128, bytes_accessed=2**20, transcendentals=2**16),
    )(
        *(
            pltpu.with_memory_space_constraint(array, pltpu.HBM)
            for array in (
                filter_index.reshape(1, channels), decay_rates.T, residues.T, skip_gain.reshape(1, channels),
                key_gate, value_rows, query_gate,
            )
        )
    )

    rows = lax.axis_size("ctx") // SIDE
    every = lax.all_gather(ends, "ctx", axis_index_groups=[[r * SIDE + x for x in range(SIDE)] for r in range(rows)])
    total = jnp.sum(in_row * every, axis=0)
    near = jnp.sum(before * every, axis=0)
    carried = jnp.zeros(line, F32)
    for r in range(rows - 1):
        sent = total + far[0] * carried if r else total
        pairs = [(r * SIDE + x, (r + 1) * SIDE + x) for x in range(SIDE)]
        carried = carried + lax.ppermute(sent, "ctx", pairs)

    stripe = pltpu.VMEM((blocks * HALF, BLOCK), F32)
    return pl.pallas_call(
        lambda *refs: output_kernel(modes, *refs),
        out_shape=shape(channels, length),
        in_specs=[VMEM] * 8,
        out_specs=VMEM,
        scratch_shapes=[stripe, stripe],
        compiler_params=pltpu.CompilerParams(vmem_limit_bytes=24 * 2**20),
        cost_estimate=pl.CostEstimate(flops=2 * 9 * 1024 * 128 * 128, bytes_accessed=2**21, transcendentals=2**16),
    )(query, mixed, skip, rate, gain, far, near, carried)


def solution(mesh):
    placed = (P("chan", "ctx"), P("chan", "ctx"), P("chan", "ctx"), P("chan"), P(), P(), P("chan"))
    return jax.shard_map(
        per_device, mesh=mesh, in_specs=placed, out_specs=P("chan", "ctx"), check_vma=False
    )
```

time: 39.1 us -> 29.3 us (0.75)
  the two profiles are of different devices: /device:TPU:8 before, /device:TPU:760 now
where the time goes in v2:
time: 29.3 us; the launch traced here: 29.2 us
  waiting for transfers between devices  12.2 us (42%)
  blocking collectives  9.72 us (33%)
  Pallas kernels  4.53 us (15%)
  starting transfers between devices  2.61 us (9%)
    ppermute x3, waiting for transfers between devices, per_device(): carried = carried + lax.ppermute(sent, 'ctx', pairs)  12.2 us
    all_gather x1, blocking collectives, per_device(): lax.all_gather(ends, 'ctx', axis_index_groups=[[r * SIDE + x for x in ran...  9.72 us
    pallas_call x1, Pallas kernels, per_device(): pl.pallas_call(lambda *refs: output_kernel(modes, *refs), out_shape=shape...  2.81 us
    ppermute x3, starting transfers between devices, per_device(): carried = carried + lax.ppermute(sent, 'ctx', pairs)  2.61 us
    pallas_call x1, Pallas kernels, per_device(): pl.pallas_call(lambda *refs: state_kernel(SIDE, *refs), out_shape=(shape(...  1.72 us
  transfers between devices with their start and end apart: 3, of which 1 were waited for; matrix products, arithmetic and copies ran while one was open for 0% of the time, Pallas kernels for 0%

profile of v2, /device:TPU:760, one launch (start us, length us, event | category | flops | bytes accessed | tf_op | source)
XLA Modules:
  0.0 29.2 jit_solution(4890482880970431286)
XLA Ops:
  0.0 1.7 %shard_map.73 = (f32[2,128]{1,0:T(2,128)S(1)}, f32[2,128]{1,0:T(2,128)S(1)}, f32[2,128]{1,0:T(2,128)S(1)}, f32[2,2,128]{2,1,0:T(2,128)S(1)}, f32[4,2,128]{2,1,0:...) custom-call(s32[1,16]{1,0:T(1,128)} %bitcast.15, ...), custom_call_target="tpu_custom_call" | custom-call | flops 100663296 | bytes 1048576 | tf_op jit(solution)/shard_map/pallas_call | solution.py:193
  1.7 9.7 %all-gather.1 = f32[4,2,128]{2,1,0:T(2,128)S(1)} all-gather(f32[1,2,128]{2,1,0:T(2,128)S(1)} %bitcast.12), channel_id=2, replica_groups={{0,48,96,144},{192,240,288,336},{384,432,480,528},{576,624,672,720},{1,..., dimensions={0}, use_global_device_ids=true | all-gather | bytes 5120 | tf_op jit(solution)/shard_map/all_gather | solution.py:223
  11.5 0.7 %collective-permute-start = (f32[2,128]{1,0:T(2,128)S(1)}, f32[2,128]{1,0:T(2,128)S(1)}, u32[]{:S(2)}, u32[]{:S(2)}) collective-permute-start(f32[2,128]{1,0:T(2,128)S(1)} %get-tuple-element.23), channel_id=1, source_target_pairs={{0,192},{48,240},{96,288},{144,336},{1,193},{49,241},{97,289},{145... | collective-permute-start | bytes 3080 | tf_op jit(solution)/shard_map/ppermute | solution.py:230
  12.1 0.0 collective-permute-done
  12.2 0.7 %collective-permute-start.1 = (f32[2,128]{1,0:T(2,128)S(1)}, f32[2,128]{1,0:T(2,128)S(1)}, u32[]{:S(2)}, u32[]{:S(2)}) collective-permute-start(f32[2,128]{1,0:T(2,128)S(1)} %fusion), channel_id=1, source_target_pairs={{192,384},{240,432},{288,480},{336,528},{193,385},{241,433},{289,4... | collective-permute-start | bytes 3080 | tf_op jit(solution)/shard_map/ppermute | solution.py:230
  12.8 0.0 collective-permute-done.1
  12.9 1.3 %collective-permute-start.2 = (f32[2,128]{1,0:T(2,128)S(1)}, f32[2,128]{1,0:T(2,128)S(1)}, u32[]{:S(2)}, u32[]{:S(2)}) collective-permute-start(f32[2,128]{1,0:T(2,128)S(1)} %get-tuple-element.25), channel_id=1, source_target_pairs={{384,576},{432,624},{480,672},{528,720},{385,577},{433,625},{481,6... | collective-permute-start | bytes 3080 | tf_op jit(solution)/shard_map/ppermute | solution.py:230
  14.2 12.2 %collective-permute-done.2 = f32[2,128]{1,0:T(2,128)S(1)} collective-permute-done((f32[2,128]{1,0:T(2,128)S(1)}, f32[2,128]{1,0:T(2,128)S(1)}, u32[]{:S(2)}, u32[]{:S(2)}) %collective-permute-start.2) | collective-permute-done | bytes 1056 | tf_op jit(solution)/shard_map/ppermute | solution.py:230
  26.3 2.8 %shard_map.74 = f32[16,8192]{1,0:T(8,128)} custom-call(f32[16,8192]{1,0:T(8,128)S(1)} %get-tuple-element.14.refs_0_, f32[2,512,128]{2,1,0:T(8,128)S(1)} %get-tuple-element.15.refs_1_, f32[16,128]{1,0:T(8,128)S(1)} %get-tuple-element.16.refs_2_, f32[2,128]{1,0:T(2,128)S(1)} %get-tuple-element.17.refs_3_, f32[2,128]{1,0:T(2,128)S(1)} %get-tuple-element.18.refs_4_, ...), custom_call_target="tpu_custom_call" | custom-call | flops 301989888 | bytes 2097152 | tf_op jit(solution)/shard_map/pallas_call | solution.py:233
  (4 shorter events, 0.0 us)
Async XLA Ops:
  11.5 0.7 %collective-permute-start = (f32[2,128]{1,0:T(2,128)S(1)}, f32[2,128]{1,0:T(2,128)S(1)}, u32[]{:S(2)}, u32[]{:S(2)}) collective-permute-start(f32[2,128]{1,0:T(2,128)S(1)} %get-tuple-element.23), channel_id=1, source_target_pairs={{0,192},{48,240},{96,288},{144,336},{1,193},{49,241},{97,289},{145... | collective-permute-start | bytes 3080 | tf_op jit(solution)/shard_map/ppermute | solution.py:230
  12.2 0.7 %collective-permute-start.1 = (f32[2,128]{1,0:T(2,128)S(1)}, f32[2,128]{1,0:T(2,128)S(1)}, u32[]{:S(2)}, u32[]{:S(2)}) collective-permute-start(f32[2,128]{1,0:T(2,128)S(1)} %fusion), channel_id=1, source_target_pairs={{192,384},{240,432},{288,480},{336,528},{193,385},{241,433},{289,4... | collective-permute-start | bytes 3080 | tf_op jit(solution)/shard_map/ppermute | solution.py:230
  12.9 13.5 %collective-permute-start.2 = (f32[2,128]{1,0:T(2,128)S(1)}, f32[2,128]{1,0:T(2,128)S(1)}, u32[]{:S(2)}, u32[]{:S(2)}) collective-permute-start(f32[2,128]{1,0:T(2,128)S(1)} %get-tuple-element.25), channel_id=1, source_target_pairs={{384,576},{432,624},{480,672},{528,720},{385,577},{433,625},{481,6... | collective-permute-start | bytes 3080 | tf_op jit(solution)/shard_map/ppermute | solution.py:230

commit v3 on v2

--- a/solution.py
+++ b/solution.py
@@ -30,7 +30,7 @@
 
 def state_kernel(
     side, index_hbm, rates_hbm, residues_hbm, skip_hbm, key_hbm, value_hbm, query_hbm,
-    end_ref, rate_ref, gain_ref, far_ref, row_ref, before_ref, skip_ref, mixed_ref, query_ref,
+    end_ref, rate_ref, gain_ref, far_ref, pair_ref, row_ref, skip_ref, mixed_ref, state_ref, query_ref,
     index_ref, rates_ref, residues_ref, skip_row, key_ref, value_ref, sems,
 ):
     channels, length = key_ref.shape
@@ -76,6 +76,7 @@
     gain_row = lanes_of(residues_ref[...]) * jnp.sqrt(one_minus_exp(2.0 * rate_row))
     own = iota((HALF, BLOCK), 1) // modes == iota((HALF, BLOCK), 0)
     place = lax.axis_index("ctx") % side
+    odd, upper = place % 2 == 1, place >= 2
     same = iota((channels, channels), 0) == iota((channels, channels), 1)
     skip = jnp.sum(jnp.where(same, skip_row[...], 0.0), axis=1, keepdims=True)
     skip_ref[...] = jnp.broadcast_to(skip, skip_ref.shape)
@@ -88,10 +89,13 @@
         passed = -rate * float(length)
         far_ref[0, here, :] = jnp.exp(passed * float(side))
         far_ref[1, here, :] = jnp.exp(passed * place.astype(F32))
-        for x in range(side):
-            row_ref[x, here, :] = jnp.exp(passed * float(side - 1 - x))
-            gap = (place - 1 - x).astype(F32)
-            before_ref[x, here, :] = jnp.where(gap >= 0.0, jnp.exp(passed * jnp.maximum(gap, 0.0)), 0.0)
+        once, twice = jnp.exp(passed), jnp.exp(2.0 * passed)
+        pair_ref[0, here, :] = jnp.where(odd, 1.0, once)
+        pair_ref[1, here, :] = jnp.where(odd, once, 1.0)
+        pair_ref[2, here, :] = jnp.where(odd, jnp.ones_like(once), 0.0)
+        row_ref[0, here, :] = jnp.where(upper, 1.0, twice)
+        row_ref[1, here, :] = jnp.where(upper, twice, 1.0)
+        row_ref[2, here, :] = jnp.where(upper, jnp.where(odd, once, 1.0), 0.0)
         to_end = (BLOCK - 1 - iota((BLOCK, BLOCK), 0)).astype(F32)
         fade_high, fade_low = split(jnp.exp(-rate * to_end))
         fades = jnp.concatenate([fade_high, fade_high, fade_low], axis=0)
@@ -114,65 +118,81 @@
             states = lax.dot_general(
                 jnp.concatenate([high, low, high], axis=1), fades, NN, preferred_element_type=F32
             )
+            state_ref[g, start * HALF : (start + 16) * HALF, :] = states
             for b in range(16):
                 total = total + block_fade[start + b : start + b + 1, :] * states[b * HALF : (b + 1) * HALF, :]
         end_ref[here, :] = jnp.sum(jnp.where(own, total, 0.0), axis=0, keepdims=True)
     query_load.wait()
 
 
+def local_kernel(g, modes, mixed_ref, state_ref, skip_ref, rate_ref, gain_ref, base_ref, enter_ref, conv_rows):
+    blocks = base_ref.shape[0] // HALF
+    square = (BLOCK, BLOCK)
+    own = iota((HALF, BLOCK), 1) // modes == iota((HALF, BLOCK), 0)
+    causal = iota(square, 1) >= iota(square, 0)
+    rate, gain = rate_ref[g : g + 1, :], gain_ref[g : g + 1, :]
+    tail = gain * jnp.exp(-rate * iota(square, 0).astype(F32))
+    taps = lax.dot_general(
+        own.astype(F32), tail, NT, precision=lax.Precision.HIGHEST, preferred_element_type=F32
+    )
+    step = jnp.exp(-rate * float(BLOCK))
+    state = jnp.zeros((HALF, BLOCK), F32)
+    for b in range(blocks):
+        some = slice(b * HALF, (b + 1) * HALF)
+        enter_ref[some, :] = jnp.where(own, state, 0.0)
+        state = state * step + state_ref[g, some, :]
+    for c in range(HALF):
+        shifted = pltpu.roll(jnp.broadcast_to(taps[c : c + 1, :], square), 0, 1, stride=1, stride_axis=0)
+        weights = jnp.concatenate(split(jnp.where(causal, shifted, 0.0)), axis=1)
+        signal = jnp.concatenate(split(mixed_ref[g, pl.ds(c, blocks, stride=HALF), :]), axis=0)
+        parts = lax.dot_general(signal, weights, NN, preferred_element_type=F32)
+        conv_rows[pl.ds(c, blocks, stride=HALF), :] = parts[:blocks, :BLOCK] + (
+            parts[:blocks, BLOCK:] + parts[blocks:, :BLOCK]
+        )
+    skip = skip_ref[g * HALF : (g + 1) * HALF, :]
+    for b in range(blocks):
+        some = slice(b * HALF, (b + 1) * HALF)
+        base_ref[some, :] = conv_rows[some, :] + skip * mixed_ref[g, some, :]
+
+
 def output_kernel(
-    modes, query_ref, mixed_ref, skip_ref, rate_ref, gain_ref, far_ref, near_ref, carried_ref, out_ref, conv_rows, carry_rows
+    modes, query_ref, rate_ref, gain_ref, far_ref, near_ref, carried_ref, *rest
 ):
+    groups = rate_ref.shape[0]
+    bases, enters = rest[:groups], rest[groups : 2 * groups]
+    out_hbm, out_ref, sems = rest[2 * groups :]
     channels, length = query_ref.shape
     blocks = length // BLOCK
     own = iota((HALF, BLOCK), 1) // modes == iota((HALF, BLOCK), 0)
     square = (BLOCK, BLOCK)
-    causal = iota(square, 1) >= iota(square, 0)
-    for g in range(channels // HALF):
+    stores = []
+    for g in range(groups):
         rows = slice(g * HALF, (g + 1) * HALF)
         here = slice(g, g + 1)
         rate, gain = rate_ref[here, :], gain_ref[here, :]
-        place = iota(square, 0).astype(F32)
-        tail = gain * jnp.exp(-rate * place)
-        taps = lax.dot_general(
-            own.astype(F32), tail, NT, precision=lax.Precision.HIGHEST, preferred_element_type=F32
-        )
-        to_end = BLOCK - 1.0 - place
-        fade_high, fade_low = split(jnp.exp(-rate * to_end))
-        fades = jnp.concatenate([fade_high, fade_high, fade_low], axis=0)
-        lead_high, lead_low = split(tail * jnp.exp(-rate))
+        after = iota(square, 0).astype(F32) + 1.0
+        lead_high, lead_low = split(gain * jnp.exp(-rate * after))
         leads = jnp.concatenate([lead_high, lead_high, lead_low], axis=1)
-        step = jnp.exp(-rate * float(BLOCK))
         entered = near_ref[here, :] + far_ref[1, here, :] * carried_ref[here, :]
-        state = jnp.broadcast_to(entered, (HALF, BLOCK))
+        fades = entered * jnp.exp(-rate * (BLOCK * iota((blocks, BLOCK), 0)).astype(F32))
         for start in range(0, blocks, 16):
             some = slice(start * HALF, (start + 16) * HALF)
-            high, low = split(mixed_ref[g, some, :])
-            states = lax.dot_general(
-                jnp.concatenate([high, low, high], axis=1), fades, NN, preferred_element_type=F32
-            )
-            entering = []
+            added = jnp.concatenate(
+                [jnp.where(own, fades[b : b + 1, :], 0.0) for b in range(start, start + 16)], axis=0
+            )
+            high, low = split(enters[g][some, :] + added)
+            conv = bases[g][some, :] + lax.dot_general(
+                jnp.concatenate([high, low, high], axis=1), leads, NT, preferred_element_type=F32
+            )
             for b in range(16):
-                entering.append(jnp.where(own, state, 0.0))
-                state = state * step + states[b * HALF : (b + 1) * HALF, :]
-            high, low = split(jnp.concatenate(entering, axis=0))
-            carry_rows[some, :] = lax.dot_general(
-                jnp.concatenate([high, low, high], axis=1), leads, NT, preferred_element_type=F32
-            )
-        for c in range(HALF):
-            shifted = pltpu.roll(jnp.broadcast_to(taps[c : c + 1, :], square), 0, 1, stride=1, stride_axis=0)
-            tap_high, tap_low = split(jnp.where(causal, shifted, 0.0))
-            weights = jnp.concatenate([tap_high, tap_high, tap_low], axis=0)
-            high, low = split(mixed_ref[g, pl.ds(c, blocks, stride=HALF), :])
-            conv_rows[pl.ds(c, blocks, stride=HALF), :] = lax.dot_general(
-                jnp.concatenate([high, low, high], axis=1), weights, NN, preferred_element_type=F32
-            )
-        skip = skip_ref[rows, :]
-        for b in range(blocks):
-            some = slice(b * HALF, (b + 1) * HALF)
-            lanes = slice(b * BLOCK, (b + 1) * BLOCK)
-            conv = conv_rows[some, :] + carry_rows[some, :] + skip * mixed_ref[g, some, :]
-            out_ref[rows, lanes] = query_ref[rows, lanes] * conv
+                lanes = slice((start + b) * BLOCK, (start + b + 1) * BLOCK)
+                out_ref[rows, lanes] = query_ref[rows, lanes] * conv[b * HALF : (b + 1) * HALF, :]
+            lanes = slice(start * BLOCK, (start + 16) * BLOCK)
+            store = pltpu.make_async_copy(out_ref.at[rows, lanes], out_hbm.at[rows, lanes], sems.at[len(stores)])
+            store.start()
+            stores.append(store)
+    for store in stores:
+        store.wait()
 
 
 VMEM = pl.BlockSpec(memory_space=pltpu.VMEM)
@@ -190,14 +210,15 @@
     blocks = length // BLOCK
     groups = channels // HALF
     line = (groups, BLOCK)
-    ends, rate, gain, far, in_row, before, skip, mixed, query = pl.pallas_call(
+    stripes = (groups, blocks * HALF, BLOCK)
+    ends, rate, gain, far, pair, row, skip, mixed, state, query = pl.pallas_call(
         lambda *refs: state_kernel(SIDE, *refs),
         out_shape=(
-            shape(*line), shape(*line), shape(*line), shape(2, *line), shape(SIDE, *line), shape(SIDE, *line),
-            shape(channels, BLOCK), shape(groups, blocks * HALF, BLOCK), shape(channels, length),
+            shape(*line), shape(*line), shape(*line), shape(2, *line), shape(3, *line), shape(3, *line),
+            shape(channels, BLOCK), shape(*stripes), shape(*stripes), shape(channels, length),
         ),
         in_specs=[HBM] * 7,
-        out_specs=(VMEM,) * 9,
+        out_specs=(VMEM,) * 10,
         scratch_shapes=[
             pltpu.VMEM((1, channels), jnp.int32),
             pltpu.VMEM((modes, residues.shape[0]), F32),
@@ -219,26 +240,40 @@
         )
     )
 
-    rows = lax.axis_size("ctx") // SIDE
-    every = lax.all_gather(ends, "ctx", axis_index_groups=[[r * SIDE + x for x in range(SIDE)] for r in range(rows)])
-    total = jnp.sum(in_row * every, axis=0)
-    near = jnp.sum(before * every, axis=0)
+    def local(g):
+        return pl.pallas_call(
+            lambda *refs: local_kernel(g, modes, *refs),
+            out_shape=(shape(*stripes[1:]), shape(*stripes[1:])),
+            in_specs=[VMEM] * 5,
+            out_specs=(VMEM, VMEM),
+            scratch_shapes=[pltpu.VMEM(stripes[1:], F32)],
+            compiler_params=pltpu.CompilerParams(vmem_limit_bytes=16 * 2**20),
+            cost_estimate=pl.CostEstimate(flops=2 * 4 * 512 * 128 * 128, bytes_accessed=2**19, transcendentals=2**14),
+        )(mixed, state, skip, rate, gain)
+
+    devices = lax.axis_size("ctx")
+    partner = lax.ppermute(ends, "ctx", [(d, d ^ 1) for d in range(devices)])
+    partner, first = lax.optimization_barrier((partner, local(0)))
+    both = pair[0] * ends + pair[1] * partner
+    across = lax.ppermute(both, "ctx", [(d, d ^ 3) for d in range(devices)])
+    across, second = lax.optimization_barrier((across, local(1)))
+    total = row[0] * both + row[1] * across
+    near = pair[2] * partner + row[2] * across
     carried = jnp.zeros(line, F32)
-    for r in range(rows - 1):
+    for r in range(devices // SIDE - 1):
         sent = total + far[0] * carried if r else total
         pairs = [(r * SIDE + x, (r + 1) * SIDE + x) for x in range(SIDE)]
         carried = carried + lax.ppermute(sent, "ctx", pairs)
 
-    stripe = pltpu.VMEM((blocks * HALF, BLOCK), F32)
     return pl.pallas_call(
         lambda *refs: output_kernel(modes, *refs),
         out_shape=shape(channels, length),
-        in_specs=[VMEM] * 8,
-        out_specs=VMEM,
-        scratch_shapes=[stripe, stripe],
-        compiler_params=pltpu.CompilerParams(vmem_limit_bytes=24 * 2**20),
-        cost_estimate=pl.CostEstimate(flops=2 * 9 * 1024 * 128 * 128, bytes_accessed=2**21, transcendentals=2**16),
-    )(query, mixed, skip, rate, gain, far, near, carried)
+        in_specs=[VMEM] * (6 + 2 * groups),
+        out_specs=HBM,
+        scratch_shapes=[pltpu.VMEM((channels, length), F32), pltpu.SemaphoreType.DMA((groups * blocks // 16,))],
+        compiler_params=pltpu.CompilerParams(vmem_limit_bytes=16 * 2**20),
+        cost_estimate=pl.CostEstimate(flops=2 * 3 * 1024 * 128 * 128, bytes_accessed=2**21, transcendentals=2**16),
+    )(query, rate, gain, far, near, carried, first[0], second[0], first[1], second[1])
 
 
 def solution(mesh):

time: 29.3 us -> 30.1 us (1.027)
  the two profiles are of different devices: /device:TPU:760 before, /device:TPU:766 now
where the time goes in v3:
time: 30.1 us; the launch traced here: 29.9 us
  waiting for transfers between devices  17.6 us (58%)
  starting transfers between devices  7.72 us (26%)
  Pallas kernels  4.5 us (15%)
    ppermute x3, waiting for transfers between devices, per_device(): carried = carried + lax.ppermute(sent, 'ctx', pairs)  12.2 us
    ppermute x1, waiting for transfers between devices, per_device(): across = lax.ppermute(both, 'ctx', [(d, d ^ 3) for d in range(devices)])  3.47 us
    ppermute x1, starting transfers between devices, per_device(): partner = lax.ppermute(ends, 'ctx', [(d, d ^ 1) for d in range(devices)])  2.74 us
    ppermute x3, starting transfers between devices, per_device(): carried = carried + lax.ppermute(sent, 'ctx', pairs)  2.6 us
    ppermute x1, starting transfers between devices, per_device(): across = lax.ppermute(both, 'ctx', [(d, d ^ 3) for d in range(devices)])  2.37 us
    ppermute x1, waiting for transfers between devices, per_device(): partner = lax.ppermute(ends, 'ctx', [(d, d ^ 1) for d in range(devices)])  1.91 us
    pallas_call x1, Pallas kernels, per_device(): pl.pallas_call(lambda *refs: state_kernel(SIDE, *refs), out_shape=(shape(...  1.71 us
    pallas_call x2, Pallas kernels, local(): pl.pallas_call(lambda *refs: local_kernel(g, modes, *refs), out_shape=(sh...  1.6 us
  transfers between devices with their start and end apart: 5, of which 3 were waited for; matrix products, arithmetic and copies ran while one was open for 0% of the time, Pallas kernels for 5%

profile of v3, /device:TPU:766, one launch (start us, length us, event | category | flops | bytes accessed | tf_op | source)
XLA Modules:
  0.0 29.9 jit_solution(3367076588813117847)
XLA Ops:
  0.0 1.7 %shard_map.73 = (f32[2,128]{1,0:T(2,128)S(1)}, f32[2,128]{1,0:T(2,128)S(1)}, f32[2,128]{1,0:T(2,128)S(1)}, f32[2,2,128]{2,1,0:T(2,128)S(1)}, f32[3,2,128]{2,1,0:...) custom-call(s32[1,16]{1,0:T(1,128)} %bitcast.37, ...), custom_call_target="tpu_custom_call" | custom-call | flops 100663296 | bytes 1048576 | tf_op jit(solution)/shard_map/pallas_call | solution.py:214
  1.7 2.7 %collective-permute-start = (f32[2,128]{1,0:T(2,128)S(1)}, f32[2,128]{1,0:T(2,128)S(1)}, u32[]{:S(2)}, u32[]{:S(2)}) collective-permute-start(f32[2,128]{1,0:T(2,128)S(1)} %get-tuple-element.30), channel_id=1, source_target_pairs={{0,48},{48,0},{96,144},{144,96},{192,240},{240,192},{288,336},{336... | collective-permute-start | bytes 3080 | tf_op jit(solution)/shard_map/ppermute | solution.py:255
  4.5 0.8 %shard_map.74 = (f32[512,128]{1,0:T(8,128)S(1)}, f32[512,128]{1,0:T(8,128)S(1)}) custom-call(f32[2,512,128]{2,1,0:T(8,128)S(1)} %get-tuple-element.31.refs_0_, f32[2,512,128]{2,1,0:T(8,128)S(1)} %get-tuple-element.32.refs_1_, f32[16,128]{1,0:T(8,128)S(1)} %get-tuple-element.33.refs_2_, f32[2,128]{1,0:T(2,128)S(1)} %get-tuple-element.26.refs_3_.refs_1_, ...), custom_call_target="tpu_custom_call" | custom-call | flops 67108864 | bytes 524288 | tf_op jit(solution)/shard_map/pallas_call | solution.py:244
  5.3 1.9 %collective-permute-done = f32[2,128]{1,0:T(2,128)S(1)} collective-permute-done((f32[2,128]{1,0:T(2,128)S(1)}, f32[2,128]{1,0:T(2,128)S(1)}, u32[]{:S(2)}, u32[]{:S(2)}) %collective-permute-start) | collective-permute-done | bytes 1056 | tf_op jit(solution)/shard_map/ppermute | solution.py:255
  7.2 2.4 %collective-permute-start.1 = (f32[2,128]{1,0:T(2,128)S(1)}, f32[2,128]{1,0:T(2,128)S(1)}, u32[]{:S(2)}, u32[]{:S(2)}) collective-permute-start(f32[2,128]{1,0:T(2,128)S(1)} %fusion.3), channel_id=1, source_target_pairs={{0,144},{48,96},{96,48},{144,0},{192,336},{240,288},{288,240},{336... | collective-permute-start | bytes 3080 | tf_op jit(solution)/shard_map/ppermute | solution.py:258
  9.6 0.8 %shard_map.75 = (f32[512,128]{1,0:T(8,128)S(1)}, f32[512,128]{1,0:T(8,128)S(1)}) custom-call(f32[2,512,128]{2,1,0:T(8,128)S(1)} %get-tuple-element.31.refs_0_, f32[2,512,128]{2,1,0:T(8,128)S(1)} %get-tuple-element.32.refs_1_, f32[16,128]{1,0:T(8,128)S(1)} %get-tuple-element.33.refs_2_, f32[2,128]{1,0:T(2,128)S(1)} %get-tuple-element.26.refs_3_.refs_1_, ...), custom_call_target="tpu_custom_call" | custom-call | flops 67108864 | bytes 524288 | tf_op jit(solution)/shard_map/pallas_call | solution.py:244
  10.4 3.5 %collective-permute-done.1 = f32[2,128]{1,0:T(2,128)S(1)} collective-permute-done((f32[2,128]{1,0:T(2,128)S(1)}, f32[2,128]{1,0:T(2,128)S(1)}, u32[]{:S(2)}, u32[]{:S(2)}) %collective-permute-start.1) | collective-permute-done | bytes 1056 | tf_op jit(solution)/shard_map/ppermute | solution.py:258
  13.9 0.7 %collective-permute-start.2 = (f32[2,128]{1,0:T(2,128)S(1)}, f32[2,128]{1,0:T(2,128)S(1)}, u32[]{:S(2)}, u32[]{:S(2)}) collective-permute-start(f32[2,128]{1,0:T(2,128)S(1)} %get-tuple-element.47), channel_id=1, source_target_pairs={{0,192},{48,240},{96,288},{144,336},{1,193},{49,241},{97,289},{145... | collective-permute-start | bytes 3080 | tf_op jit(solution)/shard_map/ppermute | solution.py:266
  14.5 0.0 collective-permute-done.2
  14.5 0.7 %collective-permute-start.3 = (f32[2,128]{1,0:T(2,128)S(1)}, f32[2,128]{1,0:T(2,128)S(1)}, u32[]{:S(2)}, u32[]{:S(2)}) collective-permute-start(f32[2,128]{1,0:T(2,128)S(1)} %fusion), channel_id=1, source_target_pairs={{192,384},{240,432},{288,480},{336,528},{193,385},{241,433},{289,4... | collective-permute-start | bytes 3080 | tf_op jit(solution)/shard_map/ppermute | solution.py:266
  15.2 0.0 collective-permute-done.3
  15.2 1.3 %collective-permute-start.4 = (f32[2,128]{1,0:T(2,128)S(1)}, f32[2,128]{1,0:T(2,128)S(1)}, u32[]{:S(2)}, u32[]{:S(2)}) collective-permute-start(f32[2,128]{1,0:T(2,128)S(1)} %get-tuple-element.45), channel_id=1, source_target_pairs={{384,576},{432,624},{480,672},{528,720},{385,577},{433,625},{481,6... | collective-permute-start | bytes 3080 | tf_op jit(solution)/shard_map/ppermute | solution.py:266
  16.5 12.2 %collective-permute-done.4 = f32[2,128]{1,0:T(2,128)S(1)} collective-permute-done((f32[2,128]{1,0:T(2,128)S(1)}, f32[2,128]{1,0:T(2,128)S(1)}, u32[]{:S(2)}, u32[]{:S(2)}) %collective-permute-start.4) | collective-permute-done | bytes 1056 | tf_op jit(solution)/shard_map/ppermute | solution.py:266
  28.7 1.2 %shard_map.76 = f32[16,8192]{1,0:T(8,128)} custom-call(f32[16,8192]{1,0:T(8,128)S(1)} %get-tuple-element.25.refs_0_, f32[2,128]{1,0:T(2,128)S(1)} %get-tuple-element.26.refs_3_.refs_1_, f32[2,128]{1,0:T(2,128)S(1)} %get-tuple-element.27.refs_4_.refs_2_, f32[2,2,128]{2,1,0:T(2,128)S(1)} %get-tuple-element.28.refs_3_, f32[2,128]{1,0:T(2,128)S(1)} %get-tuple-element.48.refs_4_, ...), custom_call_target="tpu_custom_call" | custom-call | flops 100663296 | bytes 2097152 | tf_op jit(solution)/shard_map/pallas_call | solution.py:268
  (5 shorter events, 0.0 us)
Async XLA Ops:
  1.7 5.5 %collective-permute-start = (f32[2,128]{1,0:T(2,128)S(1)}, f32[2,128]{1,0:T(2,128)S(1)}, u32[]{:S(2)}, u32[]{:S(2)}) collective-permute-start(f32[2,128]{1,0:T(2,128)S(1)} %get-tuple-element.30), channel_id=1, source_target_pairs={{0,48},{48,0},{96,144},{144,96},{192,240},{240,192},{288,336},{336... | collective-permute-start | bytes 3080 | tf_op jit(solution)/shard_map/ppermute | solution.py:255
  7.2 6.7 %collective-permute-start.1 = (f32[2,128]{1,0:T(2,128)S(1)}, f32[2,128]{1,0:T(2,128)S(1)}, u32[]{:S(2)}, u32[]{:S(2)}) collective-permute-start(f32[2,128]{1,0:T(2,128)S(1)} %fusion.3), channel_id=1, source_target_pairs={{0,144},{48,96},{96,48},{144,0},{192,336},{240,288},{288,240},{336... | collective-permute-start | bytes 3080 | tf_op jit(solution)/shard_map/ppermute | solution.py:258
  13.9 0.7 %collective-permute-start.2 = (f32[2,128]{1,0:T(2,128)S(1)}, f32[2,128]{1,0:T(2,128)S(1)}, u32[]{:S(2)}, u32[]{:S(2)}) collective-permute-start(f32[2,128]{1,0:T(2,128)S(1)} %get-tuple-element.47), channel_id=1, source_target_pairs={{0,192},{48,240},{96,288},{144,336},{1,193},{49,241},{97,289},{145... | collective-permute-start | bytes 3080 | tf_op jit(solution)/shard_map/ppermute | solution.py:266
  14.5 0.7 %collective-permute-start.3 = (f32[2,128]{1,0:T(2,128)S(1)}, f32[2,128]{1,0:T(2,128)S(1)}, u32[]{:S(2)}, u32[]{:S(2)}) collective-permute-start(f32[2,128]{1,0:T(2,128)S(1)} %fusion), channel_id=1, source_target_pairs={{192,384},{240,432},{288,480},{336,528},{193,385},{241,433},{289,4... | collective-permute-start | bytes 3080 | tf_op jit(solution)/shard_map/ppermute | solution.py:266
  15.2 13.5 %collective-permute-start.4 = (f32[2,128]{1,0:T(2,128)S(1)}, f32[2,128]{1,0:T(2,128)S(1)}, u32[]{:S(2)}, u32[]{:S(2)}) collective-permute-start(f32[2,128]{1,0:T(2,128)S(1)} %get-tuple-element.45), channel_id=1, source_target_pairs={{384,576},{432,624},{480,672},{528,720},{385,577},{433,625},{481,6... | collective-permute-start | bytes 3080 | tf_op jit(solution)/shard_map/ppermute | solution.py:266

commit v4 on v3

--- a/solution.py
+++ b/solution.py
@@ -251,19 +251,23 @@
             cost_estimate=pl.CostEstimate(flops=2 * 4 * 512 * 128 * 128, bytes_accessed=2**19, transcendentals=2**14),
         )(mixed, state, skip, rate, gain)
 
-    devices = lax.axis_size("ctx")
-    partner = lax.ppermute(ends, "ctx", [(d, d ^ 1) for d in range(devices)])
-    partner, first = lax.optimization_barrier((partner, local(0)))
-    both = pair[0] * ends + pair[1] * partner
-    across = lax.ppermute(both, "ctx", [(d, d ^ 3) for d in range(devices)])
-    across, second = lax.optimization_barrier((across, local(1)))
-    total = row[0] * both + row[1] * across
-    near = pair[2] * partner + row[2] * across
-    carried = jnp.zeros(line, F32)
-    for r in range(devices // SIDE - 1):
-        sent = total + far[0] * carried if r else total
-        pairs = [(r * SIDE + x, (r + 1) * SIDE + x) for x in range(SIDE)]
-        carried = carried + lax.ppermute(sent, "ctx", pairs)
+    rows = lax.axis_size("ctx") // SIDE
+    carried, near, mine = jnp.zeros(line, F32), jnp.zeros(line, F32), ends
+    for r in range(rows):
+        cells = [(r * SIDE + x, r * SIDE) for x in range(SIDE)]
+        last = r == rows - 1
+        partner = lax.ppermute(mine, "ctx", [(d, base + ((d - base) ^ 1)) for d, base in cells])
+        if last:
+            partner, first = lax.optimization_barrier((partner, local(0)))
+        both = pair[0] * mine + pair[1] * partner
+        across = lax.ppermute(both, "ctx", [(d, base + ((d - base) ^ 3)) for d, base in cells])
+        if last:
+            across, second = lax.optimization_barrier((across, local(1)))
+        near = near + pair[2] * partner + row[2] * across
+        if not last:
+            sent = row[0] * both + row[1] * across + far[0] * carried
+            sent, mine = lax.optimization_barrier((sent, mine))
+            carried = carried + lax.ppermute(sent, "ctx", [(d, d + SIDE) for d, _ in cells])
 
     return pl.pallas_call(
         lambda *refs: output_kernel(modes, *refs),

time: 30.1 us -> 32.6 us (1.083)
  the two profiles are of different devices: /device:TPU:766 before, /device:TPU:192 now
where the time goes in v4:
time: 32.6 us; the launch traced here: 32.3 us
  starting transfers between devices  15.3 us (47%)
  waiting for transfers between devices  12.3 us (38%)
  Pallas kernels  4.5 us (14%)
    ppermute x3, waiting for transfers between devices, per_device(): lax.ppermute(sent, 'ctx', [(d, d + SIDE) for d, _ in cells])  11.5 us
    ppermute x4, starting transfers between devices, per_device(): lax.ppermute(both, 'ctx', [(d, base + (d - base ^ 3)) for d, base in cells])  6.64 us
    ppermute x4, starting transfers between devices, per_device(): lax.ppermute(mine, 'ctx', [(d, base + (d - base ^ 1)) for d, base in cells])  5.39 us
    ppermute x3, starting transfers between devices, per_device(): lax.ppermute(sent, 'ctx', [(d, d + SIDE) for d, _ in cells])  3.24 us
    pallas_call x1, Pallas kernels, per_device(): pl.pallas_call(lambda *refs: state_kernel(SIDE, *refs), out_shape=(shape(...  1.71 us
    pallas_call x2, Pallas kernels, local(): pl.pallas_call(lambda *refs: local_kernel(g, modes, *refs), out_shape=(sh...  1.6 us
    pallas_call x1, Pallas kernels, per_device(): pl.pallas_call(lambda *refs: output_kernel(modes, *refs), out_shape=shape...  1.19 us
    ppermute x4, waiting for transfers between devices, per_device(): lax.ppermute(mine, 'ctx', [(d, base + (d - base ^ 1)) for d, base in cells])  0.76 us
  transfers between devices with their start and end apart: 11, of which 3 were waited for; matrix products, arithmetic and copies ran while one was open for 0% of the time, Pallas kernels for 5%

profile of v4, /device:TPU:192, one launch (start us, length us, event | category | flops | bytes accessed | tf_op | source)
XLA Modules:
  0.0 32.3 jit_solution(14631183724969006508)
XLA Ops:
  0.0 1.7 %shard_map.73 = (f32[2,128]{1,0:T(2,128)S(1)}, f32[2,128]{1,0:T(2,128)S(1)}, f32[2,128]{1,0:T(2,128)S(1)}, f32[2,2,128]{2,1,0:T(2,128)S(1)}, f32[3,2,128]{2,1,0:...) custom-call(s32[1,16]{1,0:T(1,128)} %bitcast.108, ...), custom_call_target="tpu_custom_call" | custom-call | flops 100663296 | bytes 1048576 | tf_op jit(solution)/shard_map/pallas_call | solution.py:214
  1.7 0.7 %collective-permute-start = (f32[2,128]{1,0:T(2,128)S(1)}, f32[2,128]{1,0:T(2,128)S(1)}, u32[]{:S(2)}, u32[]{:S(2)}) collective-permute-start(f32[2,128]{1,0:T(2,128)S(1)} %get-tuple-element.42), channel_id=1, source_target_pairs={{0,48},{48,0},{96,144},{144,96},{1,49},{49,1},{97,145},{145,97},{2... | collective-permute-start | bytes 3080 | tf_op jit(solution)/shard_map/ppermute | solution.py:259
  2.4 0.0 collective-permute-done
  2.4 0.7 %collective-permute-start.1 = (f32[2,128]{1,0:T(2,128)S(1)}, f32[2,128]{1,0:T(2,128)S(1)}, u32[]{:S(2)}, u32[]{:S(2)}) collective-permute-start(f32[2,128]{1,0:T(2,128)S(1)} %fusion.6), channel_id=1, source_target_pairs={{0,144},{48,96},{96,48},{144,0},{1,145},{49,97},{97,49},{145,1},{2... | collective-permute-start | bytes 3080 | tf_op jit(solution)/shard_map/ppermute | solution.py:263
  3.1 0.0 collective-permute-done.1
  3.1 3.4 %collective-permute-start.2 = (f32[2,128]{1,0:T(2,128)S(1)}, f32[2,128]{1,0:T(2,128)S(1)}, u32[]{:S(2)}, u32[]{:S(2)}) collective-permute-start(f32[2,128]{1,0:T(2,128)S(1)} %get-tuple-element.42), channel_id=1, source_target_pairs={{192,240},{240,192},{288,336},{336,288},{193,241},{241,193},{289,3... | collective-permute-start | bytes 3080 | tf_op jit(solution)/shard_map/ppermute | solution.py:259
  6.5 1.3 %collective-permute-start.4 = (f32[2,128]{1,0:T(2,128)S(1)}, f32[2,128]{1,0:T(2,128)S(1)}, u32[]{:S(2)}, u32[]{:S(2)}) collective-permute-start(f32[2,128]{1,0:T(2,128)S(1)} %fusion), channel_id=1, source_target_pairs={{0,192},{48,240},{96,288},{144,336},{1,193},{49,241},{97,289},{145... | collective-permute-start | bytes 3080 | tf_op jit(solution)/shard_map/ppermute | solution.py:270
  7.8 0.8 %collective-permute-done.2 = f32[2,128]{1,0:T(2,128)S(1)} collective-permute-done((f32[2,128]{1,0:T(2,128)S(1)}, f32[2,128]{1,0:T(2,128)S(1)}, u32[]{:S(2)}, u32[]{:S(2)}) %collective-permute-start.2) | collective-permute-done | bytes 1056 | tf_op jit(solution)/shard_map/ppermute | solution.py:259
  8.6 4.7 %collective-permute-start.3 = (f32[2,128]{1,0:T(2,128)S(1)}, f32[2,128]{1,0:T(2,128)S(1)}, u32[]{:S(2)}, u32[]{:S(2)}) collective-permute-start(f32[2,128]{1,0:T(2,128)S(1)} %fusion.7), channel_id=1, source_target_pairs={{192,336},{240,288},{288,240},{336,192},{193,337},{241,289},{289,2... | collective-permute-start | bytes 3080 | tf_op jit(solution)/shard_map/ppermute | solution.py:263
  13.2 10.9 %collective-permute-done.4 = f32[2,128]{1,0:T(2,128)S(1)} collective-permute-done((f32[2,128]{1,0:T(2,128)S(1)}, f32[2,128]{1,0:T(2,128)S(1)}, u32[]{:S(2)}, u32[]{:S(2)}) %collective-permute-start.4) | collective-permute-done | bytes 1056 | tf_op jit(solution)/shard_map/ppermute | solution.py:270
  24.2 0.0 collective-permute-done.3
  24.2 0.7 %collective-permute-start.5 = (f32[2,128]{1,0:T(2,128)S(1)}, f32[2,128]{1,0:T(2,128)S(1)}, u32[]{:S(2)}, u32[]{:S(2)}) collective-permute-start(f32[2,128]{1,0:T(2,128)S(1)} %get-tuple-element.42), channel_id=1, source_target_pairs={{384,432},{432,384},{480,528},{528,480},{385,433},{433,385},{481,5... | collective-permute-start | bytes 3080 | tf_op jit(solution)/shard_map/ppermute | solution.py:259
  24.9 1.3 %collective-permute-start.7 = (f32[2,128]{1,0:T(2,128)S(1)}, f32[2,128]{1,0:T(2,128)S(1)}, u32[]{:S(2)}, u32[]{:S(2)}) collective-permute-start(f32[2,128]{1,0:T(2,128)S(1)} %fusion.1), channel_id=1, source_target_pairs={{192,384},{240,432},{288,480},{336,528},{193,385},{241,433},{289,4... | collective-permute-start | bytes 3080 | tf_op jit(solution)/shard_map/ppermute | solution.py:270
  26.2 0.0 collective-permute-done.5
  26.2 0.7 %collective-permute-start.6 = (f32[2,128]{1,0:T(2,128)S(1)}, f32[2,128]{1,0:T(2,128)S(1)}, u32[]{:S(2)}, u32[]{:S(2)}) collective-permute-start(f32[2,128]{1,0:T(2,128)S(1)} %fusion.8), channel_id=1, source_target_pairs={{384,528},{432,480},{480,432},{528,384},{385,529},{433,481},{481,4... | collective-permute-start | bytes 3080 | tf_op jit(solution)/shard_map/ppermute | solution.py:263
  26.9 0.6 %collective-permute-done.7 = f32[2,128]{1,0:T(2,128)S(1)} collective-permute-done((f32[2,128]{1,0:T(2,128)S(1)}, f32[2,128]{1,0:T(2,128)S(1)}, u32[]{:S(2)}, u32[]{:S(2)}) %collective-permute-start.7) | collective-permute-done | bytes 1056 | tf_op jit(solution)/shard_map/ppermute | solution.py:270
  27.4 0.0 collective-permute-done.6
  27.5 0.7 %collective-permute-start.8 = (f32[2,128]{1,0:T(2,128)S(1)}, f32[2,128]{1,0:T(2,128)S(1)}, u32[]{:S(2)}, u32[]{:S(2)}) collective-permute-start(f32[2,128]{1,0:T(2,128)S(1)} %get-tuple-element.42), channel_id=1, source_target_pairs={{576,624},{624,576},{672,720},{720,672},{577,625},{625,577},{673,7... | collective-permute-start | bytes 3080 | tf_op jit(solution)/shard_map/ppermute | solution.py:259
  28.1 0.8 %shard_map.74 = (f32[512,128]{1,0:T(8,128)S(1)}, f32[512,128]{1,0:T(8,128)S(1)}) custom-call(f32[2,512,128]{2,1,0:T(8,128)S(1)} %get-tuple-element.43.refs_0_, f32[2,512,128]{2,1,0:T(8,128)S(1)} %get-tuple-element.44.refs_1_, f32[16,128]{1,0:T(8,128)S(1)} %get-tuple-element.45.refs_2_, f32[2,128]{1,0:T(2,128)S(1)} %get-tuple-element.32.refs_3_.refs_1_, ...), custom_call_target="tpu_custom_call" | custom-call | flops 67108864 | bytes 524288 | tf_op jit(solution)/shard_map/pallas_call | solution.py:244
  28.9 0.7 %collective-permute-start.10 = (f32[2,128]{1,0:T(2,128)S(1)}, f32[2,128]{1,0:T(2,128)S(1)}, u32[]{:S(2)}, u32[]{:S(2)}) collective-permute-start(f32[2,128]{1,0:T(2,128)S(1)} %get-tuple-element.52), channel_id=1, source_target_pairs={{384,576},{432,624},{480,672},{528,720},{385,577},{433,625},{481,6... | collective-permute-start | bytes 3080 | tf_op jit(solution)/shard_map/ppermute | solution.py:270
  29.6 0.0 collective-permute-done.8
  29.6 0.7 %collective-permute-start.9 = (f32[2,128]{1,0:T(2,128)S(1)}, f32[2,128]{1,0:T(2,128)S(1)}, u32[]{:S(2)}, u32[]{:S(2)}) collective-permute-start(f32[2,128]{1,0:T(2,128)S(1)} %fusion.9), channel_id=1, source_target_pairs={{576,720},{624,672},{672,624},{720,576},{577,721},{625,673},{673,6... | collective-permute-start | bytes 3080 | tf_op jit(solution)/shard_map/ppermute | solution.py:263
  30.3 0.8 %shard_map.75 = (f32[512,128]{1,0:T(8,128)S(1)}, f32[512,128]{1,0:T(8,128)S(1)}) custom-call(f32[2,512,128]{2,1,0:T(8,128)S(1)} %get-tuple-element.43.refs_0_, f32[2,512,128]{2,1,0:T(8,128)S(1)} %get-tuple-element.44.refs_1_, f32[16,128]{1,0:T(8,128)S(1)} %get-tuple-element.45.refs_2_, f32[2,128]{1,0:T(2,128)S(1)} %get-tuple-element.32.refs_3_.refs_1_, ...), custom_call_target="tpu_custom_call" | custom-call | flops 67108864 | bytes 524288 | tf_op jit(solution)/shard_map/pallas_call | solution.py:244
  31.1 0.0 collective-permute-done.10
  31.1 0.0 collective-permute-done.9
  31.2 1.2 %shard_map.76 = f32[16,8192]{1,0:T(8,128)} custom-call(f32[16,8192]{1,0:T(8,128)S(1)} %get-tuple-element.31.refs_0_, f32[2,128]{1,0:T(2,128)S(1)} %get-tuple-element.32.refs_3_.refs_1_, f32[2,128]{1,0:T(2,128)S(1)} %get-tuple-element.33.refs_4_.refs_2_, f32[2,2,128]{2,1,0:T(2,128)S(1)} %get-tuple-element.34.refs_3_, f32[2,128]{1,0:T(2,128)S(1)} %fusion.16.refs_4_, ...), custom_call_target="tpu_custom_call" | custom-call | flops 100663296 | bytes 2097152 | tf_op jit(solution)/shard_map/pallas_call | solution.py:272
  (9 shorter events, 0.1 us)
Async XLA Ops:
  1.7 0.7 %collective-permute-start = (f32[2,128]{1,0:T(2,128)S(1)}, f32[2,128]{1,0:T(2,128)S(1)}, u32[]{:S(2)}, u32[]{:S(2)}) collective-permute-start(f32[2,128]{1,0:T(2,128)S(1)} %get-tuple-element.42), channel_id=1, source_target_pairs={{0,48},{48,0},{96,144},{144,96},{1,49},{49,1},{97,145},{145,97},{2... | collective-permute-start | bytes 3080 | tf_op jit(solution)/shard_map/ppermute | solution.py:259
  2.4 0.7 %collective-permute-start.1 = (f32[2,128]{1,0:T(2,128)S(1)}, f32[2,128]{1,0:T(2,128)S(1)}, u32[]{:S(2)}, u32[]{:S(2)}) collective-permute-start(f32[2,128]{1,0:T(2,128)S(1)} %fusion.6), channel_id=1, source_target_pairs={{0,144},{48,96},{96,48},{144,0},{1,145},{49,97},{97,49},{145,1},{2... | collective-permute-start | bytes 3080 | tf_op jit(solution)/shard_map/ppermute | solution.py:263
  3.1 5.5 %collective-permute-start.2 = (f32[2,128]{1,0:T(2,128)S(1)}, f32[2,128]{1,0:T(2,128)S(1)}, u32[]{:S(2)}, u32[]{:S(2)}) collective-permute-start(f32[2,128]{1,0:T(2,128)S(1)} %get-tuple-element.42), channel_id=1, source_target_pairs={{192,240},{240,192},{288,336},{336,288},{193,241},{241,193},{289,3... | collective-permute-start | bytes 3080 | tf_op jit(solution)/shard_map/ppermute | solution.py:259
  6.5 17.7 %collective-permute-start.4 = (f32[2,128]{1,0:T(2,128)S(1)}, f32[2,128]{1,0:T(2,128)S(1)}, u32[]{:S(2)}, u32[]{:S(2)}) collective-permute-start(f32[2,128]{1,0:T(2,128)S(1)} %fusion), channel_id=1, source_target_pairs={{0,192},{48,240},{96,288},{144,336},{1,193},{49,241},{97,289},{145... | collective-permute-start | bytes 3080 | tf_op jit(solution)/shard_map/ppermute | solution.py:270
  8.6 15.6 %collective-permute-start.3 = (f32[2,128]{1,0:T(2,128)S(1)}, f32[2,128]{1,0:T(2,128)S(1)}, u32[]{:S(2)}, u32[]{:S(2)}) collective-permute-start(f32[2,128]{1,0:T(2,128)S(1)} %fusion.7), channel_id=1, source_target_pairs={{192,336},{240,288},{288,240},{336,192},{193,337},{241,289},{289,2... | collective-permute-start | bytes 3080 | tf_op jit(solution)/shard_map/ppermute | solution.py:263
  24.2 2.0 %collective-permute-start.5 = (f32[2,128]{1,0:T(2,128)S(1)}, f32[2,128]{1,0:T(2,128)S(1)}, u32[]{:S(2)}, u32[]{:S(2)}) collective-permute-start(f32[2,128]{1,0:T(2,128)S(1)} %get-tuple-element.42), channel_id=1, source_target_pairs={{384,432},{432,384},{480,528},{528,480},{385,433},{433,385},{481,5... | collective-permute-start | bytes 3080 | tf_op jit(solution)/shard_map/ppermute | solution.py:259
  24.9 2.6 %collective-permute-start.7 = (f32[2,128]{1,0:T(2,128)S(1)}, f32[2,128]{1,0:T(2,128)S(1)}, u32[]{:S(2)}, u32[]{:S(2)}) collective-permute-start(f32[2,128]{1,0:T(2,128)S(1)} %fusion.1), channel_id=1, source_target_pairs={{192,384},{240,432},{288,480},{336,528},{193,385},{241,433},{289,4... | collective-permute-start | bytes 3080 | tf_op jit(solution)/shard_map/ppermute | solution.py:270
  26.2 1.3 %collective-permute-start.6 = (f32[2,128]{1,0:T(2,128)S(1)}, f32[2,128]{1,0:T(2,128)S(1)}, u32[]{:S(2)}, u32[]{:S(2)}) collective-permute-start(f32[2,128]{1,0:T(2,128)S(1)} %fusion.8), channel_id=1, source_target_pairs={{384,528},{432,480},{480,432},{528,384},{385,529},{433,481},{481,4... | collective-permute-start | bytes 3080 | tf_op jit(solution)/shard_map/ppermute | solution.py:263
  27.5 2.1 %collective-permute-start.8 = (f32[2,128]{1,0:T(2,128)S(1)}, f32[2,128]{1,0:T(2,128)S(1)}, u32[]{:S(2)}, u32[]{:S(2)}) collective-permute-start(f32[2,128]{1,0:T(2,128)S(1)} %get-tuple-element.42), channel_id=1, source_target_pairs={{576,624},{624,576},{672,720},{720,672},{577,625},{625,577},{673,7... | collective-permute-start | bytes 3080 | tf_op jit(solution)/shard_map/ppermute | solution.py:259
  28.9 2.2 %collective-permute-start.10 = (f32[2,128]{1,0:T(2,128)S(1)}, f32[2,128]{1,0:T(2,128)S(1)}, u32[]{:S(2)}, u32[]{:S(2)}) collective-permute-start(f32[2,128]{1,0:T(2,128)S(1)} %get-tuple-element.52), channel_id=1, source_target_pairs={{384,576},{432,624},{480,672},{528,720},{385,577},{433,625},{481,6... | collective-permute-start | bytes 3080 | tf_op jit(solution)/shard_map/ppermute | solution.py:270
  29.6 1.5 %collective-permute-start.9 = (f32[2,128]{1,0:T(2,128)S(1)}, f32[2,128]{1,0:T(2,128)S(1)}, u32[]{:S(2)}, u32[]{:S(2)}) collective-permute-start(f32[2,128]{1,0:T(2,128)S(1)} %fusion.9), channel_id=1, source_target_pairs={{576,720},{624,672},{672,624},{720,576},{577,721},{625,673},{673,6... | collective-permute-start | bytes 3080 | tf_op jit(solution)/shard_map/ppermute | solution.py:263

commit v5 on v3

--- a/solution.py
+++ b/solution.py
@@ -30,7 +30,7 @@
 
 def state_kernel(
     side, index_hbm, rates_hbm, residues_hbm, skip_hbm, key_hbm, value_hbm, query_hbm,
-    end_ref, rate_ref, gain_ref, far_ref, pair_ref, row_ref, skip_ref, mixed_ref, state_ref, query_ref,
+    end_ref, rate_ref, gain_ref, far_ref, pair_ref, row_ref, turn_ref, skip_ref, mixed_ref, state_ref, query_ref,
     index_ref, rates_ref, residues_ref, skip_row, key_ref, value_ref, sems,
 ):
     channels, length = key_ref.shape
@@ -76,6 +76,7 @@
     gain_row = lanes_of(residues_ref[...]) * jnp.sqrt(one_minus_exp(2.0 * rate_row))
     own = iota((HALF, BLOCK), 1) // modes == iota((HALF, BLOCK), 0)
     place = lax.axis_index("ctx") % side
+    first = lax.axis_index("ctx") < side
     odd, upper = place % 2 == 1, place >= 2
     same = iota((channels, channels), 0) == iota((channels, channels), 1)
     skip = jnp.sum(jnp.where(same, skip_row[...], 0.0), axis=1, keepdims=True)
@@ -90,9 +91,18 @@
         far_ref[0, here, :] = jnp.exp(passed * float(side))
         far_ref[1, here, :] = jnp.exp(passed * place.astype(F32))
         once, twice = jnp.exp(passed), jnp.exp(2.0 * passed)
-        pair_ref[0, here, :] = jnp.where(odd, 1.0, once)
-        pair_ref[1, here, :] = jnp.where(odd, once, 1.0)
-        pair_ref[2, here, :] = jnp.where(odd, jnp.ones_like(once), 0.0)
+
+        def to_side(k):
+            ahead = side - 1 - (place - k + side) % side
+            return jnp.exp(passed * ahead.astype(F32))
+
+        pair_ref[0, here, :] = jnp.where(first, to_side(0), jnp.where(odd, 1.0, once))
+        pair_ref[1, here, :] = jnp.where(first, to_side(1), jnp.where(odd, once, 1.0))
+        pair_ref[2, here, :] = jnp.where((first & (place >= 1)) | odd, jnp.ones_like(once), 0.0)
+        turn_ref[0, here, :] = to_side(2)
+        turn_ref[1, here, :] = to_side(3)
+        turn_ref[2, here, :] = jnp.where(place >= 2, once, 0.0)
+        turn_ref[3, here, :] = jnp.where(place >= 3, twice, 0.0)
         row_ref[0, here, :] = jnp.where(upper, 1.0, twice)
         row_ref[1, here, :] = jnp.where(upper, twice, 1.0)
         row_ref[2, here, :] = jnp.where(upper, jnp.where(odd, once, 1.0), 0.0)
@@ -211,14 +221,14 @@
     groups = channels // HALF
     line = (groups, BLOCK)
     stripes = (groups, blocks * HALF, BLOCK)
-    ends, rate, gain, far, pair, row, skip, mixed, state, query = pl.pallas_call(
+    ends, rate, gain, far, pair, row, turn, skip, mixed, state, query = pl.pallas_call(
         lambda *refs: state_kernel(SIDE, *refs),
         out_shape=(
-            shape(*line), shape(*line), shape(*line), shape(2, *line), shape(3, *line), shape(3, *line),
+            shape(*line), shape(*line), shape(*line), shape(2, *line), shape(3, *line), shape(3, *line), shape(4, *line),
             shape(channels, BLOCK), shape(*stripes), shape(*stripes), shape(channels, length),
         ),
         in_specs=[HBM] * 7,
-        out_specs=(VMEM,) * 10,
+        out_specs=(VMEM,) * 11,
         scratch_shapes=[
             pltpu.VMEM((1, channels), jnp.int32),
             pltpu.VMEM((modes, residues.shape[0]), F32),
@@ -251,19 +261,26 @@
             cost_estimate=pl.CostEstimate(flops=2 * 4 * 512 * 128 * 128, bytes_accessed=2**19, transcendentals=2**14),
         )(mixed, state, skip, rate, gain)
 
-    devices = lax.axis_size("ctx")
-    partner = lax.ppermute(ends, "ctx", [(d, d ^ 1) for d in range(devices)])
-    partner, first = lax.optimization_barrier((partner, local(0)))
+    rows = lax.axis_size("ctx") // SIDE
+    turns = [[(x, (x + k) % SIDE) for x in range(SIDE)] for k in range(SIDE)]
+    met = [(d, d ^ 1) for d in range(SIDE, rows * SIDE)]
+    partner = lax.ppermute(ends, "ctx", turns[1] + met)
+    second = lax.ppermute(ends, "ctx", turns[2])
+    third = lax.ppermute(ends, "ctx", turns[3])
+    partner, local_first = lax.optimization_barrier((partner, local(0)))
     both = pair[0] * ends + pair[1] * partner
-    across = lax.ppermute(both, "ctx", [(d, d ^ 3) for d in range(devices)])
-    across, second = lax.optimization_barrier((across, local(1)))
-    total = row[0] * both + row[1] * across
-    near = pair[2] * partner + row[2] * across
+    near = pair[2] * partner + turn[2] * second + turn[3] * third
+    sent = both + turn[0] * second + turn[1] * third
     carried = jnp.zeros(line, F32)
-    for r in range(devices // SIDE - 1):
-        sent = total + far[0] * carried if r else total
-        pairs = [(r * SIDE + x, (r + 1) * SIDE + x) for x in range(SIDE)]
-        carried = carried + lax.ppermute(sent, "ctx", pairs)
+    for r in range(1, rows):
+        sent, both = lax.optimization_barrier((sent, both))
+        passed = lax.ppermute(sent, "ctx", [((r - 1) * SIDE + x, r * SIDE + x) for x in range(SIDE)])
+        across = lax.ppermute(both, "ctx", [(r * SIDE + x, r * SIDE + (x ^ 3)) for x in range(SIDE)])
+        if r == rows - 1:
+            passed, local_second = lax.optimization_barrier((passed, local(1)))
+        carried = carried + passed
+        near = near + row[2] * across
+        sent = row[0] * both + row[1] * across + far[0] * carried
 
     return pl.pallas_call(
         lambda *refs: output_kernel(modes, *refs),
@@ -273,7 +290,7 @@
         scratch_shapes=[pltpu.VMEM((channels, length), F32), pltpu.SemaphoreType.DMA((groups * blocks // 16,))],
         compiler_params=pltpu.CompilerParams(vmem_limit_bytes=16 * 2**20),
         cost_estimate=pl.CostEstimate(flops=2 * 3 * 1024 * 128 * 128, bytes_accessed=2**21, transcendentals=2**16),
-    )(query, rate, gain, far, near, carried, first[0], second[0], first[1], second[1])
+    )(query, rate, gain, far, near, carried, local_first[0], local_second[0], local_first[1], local_second[1])
 
 
 def solution(mesh):

time: 30.1 us -> 31.5 us (1.047)
  the two profiles are of different devices: /device:TPU:766 before, /device:TPU:576 now
where the time goes in v5:
time: 31.5 us; the launch traced here: 31.2 us
  starting transfers between devices  13.3 us (42%)
  waiting for transfers between devices  13.2 us (42%)
  Pallas kernels  4.51 us (14%)
    ppermute x3, waiting for transfers between devices, per_device(): lax.ppermute(sent, 'ctx', [((r - 1) * SIDE + x, r * SIDE + x) for x in ra...  11.9 us
    ppermute x3, starting transfers between devices, per_device(): lax.ppermute(both, 'ctx', [(r * SIDE + x, r * SIDE + (x ^ 3)) for x in ra...  5.99 us
    ppermute x1, starting transfers between devices, per_device(): partner = lax.ppermute(ends, 'ctx', turns[1] + met)  3.4 us
    ppermute x3, starting transfers between devices, per_device(): lax.ppermute(sent, 'ctx', [((r - 1) * SIDE + x, r * SIDE + x) for x in ra...  2.62 us
    pallas_call x1, Pallas kernels, per_device(): pl.pallas_call(lambda *refs: state_kernel(SIDE, *refs), out_shape=(shape(...  1.72 us
    pallas_call x2, Pallas kernels, local(): pl.pallas_call(lambda *refs: local_kernel(g, modes, *refs), out_shape=(sh...  1.6 us
    ppermute x1, waiting for transfers between devices, per_device(): partner = lax.ppermute(ends, 'ctx', turns[1] + met)  1.25 us
    pallas_call x1, Pallas kernels, per_device(): pl.pallas_call(lambda *refs: output_kernel(modes, *refs), out_shape=shape...  1.2 us
  transfers between devices with their start and end apart: 9, of which 2 were waited for; matrix products, arithmetic and copies ran while one was open for 0% of the time, Pallas kernels for 5%

profile of v5, /device:TPU:576, one launch (start us, length us, event | category | flops | bytes accessed | tf_op | source)
XLA Modules:
  0.0 31.2 jit_solution(14387403632749000874)
XLA Ops:
  0.0 1.7 %shard_map.73 = (f32[2,128]{1,0:T(2,128)S(1)}, f32[2,128]{1,0:T(2,128)S(1)}, f32[2,128]{1,0:T(2,128)S(1)}, f32[2,2,128]{2,1,0:T(2,128)S(1)}, f32[3,2,128]{2,1,0:...) custom-call(s32[1,16]{1,0:T(1,128)} %bitcast.81, ...), custom_call_target="tpu_custom_call" | custom-call | flops 100663296 | bytes 1048576 | tf_op jit(solution)/shard_map/pallas_call | solution.py:224
  1.7 0.7 %collective-permute-start.2 = (f32[2,128]{1,0:T(2,128)S(1)}, f32[2,128]{1,0:T(2,128)S(1)}, u32[]{:S(2)}, u32[]{:S(2)}) collective-permute-start(f32[2,128]{1,0:T(2,128)S(1)} %get-tuple-element.37), channel_id=1, source_target_pairs={{0,144},{48,0},{96,48},{144,96},{1,145},{49,1},{97,49},{145,97},{2... | collective-permute-start | bytes 3080 | tf_op jit(solution)/shard_map/ppermute | solution.py:269
  2.4 0.7 %collective-permute-start.1 = (f32[2,128]{1,0:T(2,128)S(1)}, f32[2,128]{1,0:T(2,128)S(1)}, u32[]{:S(2)}, u32[]{:S(2)}) collective-permute-start(f32[2,128]{1,0:T(2,128)S(1)} %get-tuple-element.37), channel_id=1, source_target_pairs={{0,96},{48,144},{96,0},{144,48},{1,97},{49,145},{97,1},{145,49},{2... | collective-permute-start | bytes 3080 | tf_op jit(solution)/shard_map/ppermute | solution.py:268
  3.1 3.4 %collective-permute-start = (f32[2,128]{1,0:T(2,128)S(1)}, f32[2,128]{1,0:T(2,128)S(1)}, u32[]{:S(2)}, u32[]{:S(2)}) collective-permute-start(f32[2,128]{1,0:T(2,128)S(1)} %get-tuple-element.37), channel_id=1, source_target_pairs={{0,48},{48,96},{96,144},{144,0},{192,240},{240,192},{288,336},{336... | collective-permute-start | bytes 3080 | tf_op jit(solution)/shard_map/ppermute | solution.py:267
  6.5 0.8 %shard_map.74 = (f32[512,128]{1,0:T(8,128)S(1)}, f32[512,128]{1,0:T(8,128)S(1)}) custom-call(f32[2,512,128]{2,1,0:T(8,128)S(1)} %get-tuple-element.38.refs_0_, f32[2,512,128]{2,1,0:T(8,128)S(1)} %get-tuple-element.39.refs_1_, f32[16,128]{1,0:T(8,128)S(1)} %get-tuple-element.40.refs_2_, f32[2,128]{1,0:T(2,128)S(1)} %get-tuple-element.33.refs_3_.refs_1_, ...), custom_call_target="tpu_custom_call" | custom-call | flops 67108864 | bytes 524288 | tf_op jit(solution)/shard_map/pallas_call | solution.py:254
  7.3 1.3 %collective-permute-done = f32[2,128]{1,0:T(2,128)S(1)} collective-permute-done((f32[2,128]{1,0:T(2,128)S(1)}, f32[2,128]{1,0:T(2,128)S(1)}, u32[]{:S(2)}, u32[]{:S(2)}) %collective-permute-start) | collective-permute-done | bytes 1056 | tf_op jit(solution)/shard_map/ppermute | solution.py:267
  8.5 0.0 collective-permute-done.2
  8.5 0.0 collective-permute-done.1
  8.5 0.7 %collective-permute-start.3 = (f32[2,128]{1,0:T(2,128)S(1)}, f32[2,128]{1,0:T(2,128)S(1)}, u32[]{:S(2)}, u32[]{:S(2)}) collective-permute-start(f32[2,128]{1,0:T(2,128)S(1)} %get-tuple-element.50), channel_id=1, source_target_pairs={{192,336},{240,288},{288,240},{336,192},{193,337},{241,289},{289,2... | collective-permute-start | bytes 3080 | tf_op jit(solution)/shard_map/ppermute | solution.py:278
  9.2 0.7 %collective-permute-start.4 = (f32[2,128]{1,0:T(2,128)S(1)}, f32[2,128]{1,0:T(2,128)S(1)}, u32[]{:S(2)}, u32[]{:S(2)}) collective-permute-start(f32[2,128]{1,0:T(2,128)S(1)} %get-tuple-element.47), channel_id=1, source_target_pairs={{0,192},{48,240},{96,288},{144,336},{1,193},{49,241},{97,289},{145... | collective-permute-start | bytes 3080 | tf_op jit(solution)/shard_map/ppermute | solution.py:277
  9.9 0.0 collective-permute-done.3
  9.9 0.0 collective-permute-done.4
  9.9 0.7 %collective-permute-start.5 = (f32[2,128]{1,0:T(2,128)S(1)}, f32[2,128]{1,0:T(2,128)S(1)}, u32[]{:S(2)}, u32[]{:S(2)}) collective-permute-start(f32[2,128]{1,0:T(2,128)S(1)} %get-tuple-element.50), channel_id=1, source_target_pairs={{384,528},{432,480},{480,432},{528,384},{385,529},{433,481},{481,4... | collective-permute-start | bytes 3080 | tf_op jit(solution)/shard_map/ppermute | solution.py:278
  10.6 0.7 %collective-permute-start.6 = (f32[2,128]{1,0:T(2,128)S(1)}, f32[2,128]{1,0:T(2,128)S(1)}, u32[]{:S(2)}, u32[]{:S(2)}) collective-permute-start(f32[2,128]{1,0:T(2,128)S(1)} %fusion), channel_id=1, source_target_pairs={{192,384},{240,432},{288,480},{336,528},{193,385},{241,433},{289,4... | collective-permute-start | bytes 3080 | tf_op jit(solution)/shard_map/ppermute | solution.py:277
  11.3 0.0 collective-permute-done.5
  11.3 0.0 collective-permute-done.6
  11.3 4.7 %collective-permute-start.7 = (f32[2,128]{1,0:T(2,128)S(1)}, f32[2,128]{1,0:T(2,128)S(1)}, u32[]{:S(2)}, u32[]{:S(2)}) collective-permute-start(f32[2,128]{1,0:T(2,128)S(1)} %get-tuple-element.50), channel_id=1, source_target_pairs={{576,720},{624,672},{672,624},{720,576},{577,721},{625,673},{673,6... | collective-permute-start | bytes 3080 | tf_op jit(solution)/shard_map/ppermute | solution.py:278
  16.0 1.3 %collective-permute-start.8 = (f32[2,128]{1,0:T(2,128)S(1)}, f32[2,128]{1,0:T(2,128)S(1)}, u32[]{:S(2)}, u32[]{:S(2)}) collective-permute-start(f32[2,128]{1,0:T(2,128)S(1)} %get-tuple-element.51), channel_id=1, source_target_pairs={{384,576},{432,624},{480,672},{528,720},{385,577},{433,625},{481,6... | collective-permute-start | bytes 3080 | tf_op jit(solution)/shard_map/ppermute | solution.py:277
  17.3 0.8 %shard_map.75 = (f32[512,128]{1,0:T(8,128)S(1)}, f32[512,128]{1,0:T(8,128)S(1)}) custom-call(f32[2,512,128]{2,1,0:T(8,128)S(1)} %get-tuple-element.38.refs_0_, f32[2,512,128]{2,1,0:T(8,128)S(1)} %get-tuple-element.39.refs_1_, f32[16,128]{1,0:T(8,128)S(1)} %get-tuple-element.40.refs_2_, f32[2,128]{1,0:T(2,128)S(1)} %get-tuple-element.33.refs_3_.refs_1_, ...), custom_call_target="tpu_custom_call" | custom-call | flops 67108864 | bytes 524288 | tf_op jit(solution)/shard_map/pallas_call | solution.py:254
  18.1 11.9 %collective-permute-done.8 = f32[2,128]{1,0:T(2,128)S(1)} collective-permute-done((f32[2,128]{1,0:T(2,128)S(1)}, f32[2,128]{1,0:T(2,128)S(1)}, u32[]{:S(2)}, u32[]{:S(2)}) %collective-permute-start.8) | collective-permute-done | bytes 1056 | tf_op jit(solution)/shard_map/ppermute | solution.py:277
  30.0 0.0 collective-permute-done.7
  30.0 1.2 %shard_map.76 = f32[16,8192]{1,0:T(8,128)} custom-call(f32[16,8192]{1,0:T(8,128)S(1)} %get-tuple-element.32.refs_0_, f32[2,128]{1,0:T(2,128)S(1)} %get-tuple-element.33.refs_3_.refs_1_, f32[2,128]{1,0:T(2,128)S(1)} %get-tuple-element.34.refs_4_.refs_2_, f32[2,2,128]{2,1,0:T(2,128)S(1)} %get-tuple-element.35.refs_3_, f32[2,128]{1,0:T(2,128)S(1)} %fusion.9.refs_4_, ...), custom_call_target="tpu_custom_call" | custom-call | flops 100663296 | bytes 2097152 | tf_op jit(solution)/shard_map/pallas_call | solution.py:285
  (5 shorter events, 0.0 us)
Async XLA Ops:
  1.7 6.8 %collective-permute-start.2 = (f32[2,128]{1,0:T(2,128)S(1)}, f32[2,128]{1,0:T(2,128)S(1)}, u32[]{:S(2)}, u32[]{:S(2)}) collective-permute-start(f32[2,128]{1,0:T(2,128)S(1)} %get-tuple-element.37), channel_id=1, source_target_pairs={{0,144},{48,0},{96,48},{144,96},{1,145},{49,1},{97,49},{145,97},{2... | collective-permute-start | bytes 3080 | tf_op jit(solution)/shard_map/ppermute | solution.py:269
  2.4 6.1 %collective-permute-start.1 = (f32[2,128]{1,0:T(2,128)S(1)}, f32[2,128]{1,0:T(2,128)S(1)}, u32[]{:S(2)}, u32[]{:S(2)}) collective-permute-start(f32[2,128]{1,0:T(2,128)S(1)} %get-tuple-element.37), channel_id=1, source_target_pairs={{0,96},{48,144},{96,0},{144,48},{1,97},{49,145},{97,1},{145,49},{2... | collective-permute-start | bytes 3080 | tf_op jit(solution)/shard_map/ppermute | solution.py:268
  3.1 5.5 %collective-permute-start = (f32[2,128]{1,0:T(2,128)S(1)}, f32[2,128]{1,0:T(2,128)S(1)}, u32[]{:S(2)}, u32[]{:S(2)}) collective-permute-start(f32[2,128]{1,0:T(2,128)S(1)} %get-tuple-element.37), channel_id=1, source_target_pairs={{0,48},{48,96},{96,144},{144,0},{192,240},{240,192},{288,336},{336... | collective-permute-start | bytes 3080 | tf_op jit(solution)/shard_map/ppermute | solution.py:267
  8.5 1.3 %collective-permute-start.3 = (f32[2,128]{1,0:T(2,128)S(1)}, f32[2,128]{1,0:T(2,128)S(1)}, u32[]{:S(2)}, u32[]{:S(2)}) collective-permute-start(f32[2,128]{1,0:T(2,128)S(1)} %get-tuple-element.50), channel_id=1, source_target_pairs={{192,336},{240,288},{288,240},{336,192},{193,337},{241,289},{289,2... | collective-permute-start | bytes 3080 | tf_op jit(solution)/shard_map/ppermute | solution.py:278
  9.2 0.7 %collective-permute-start.4 = (f32[2,128]{1,0:T(2,128)S(1)}, f32[2,128]{1,0:T(2,128)S(1)}, u32[]{:S(2)}, u32[]{:S(2)}) collective-permute-start(f32[2,128]{1,0:T(2,128)S(1)} %get-tuple-element.47), channel_id=1, source_target_pairs={{0,192},{48,240},{96,288},{144,336},{1,193},{49,241},{97,289},{145... | collective-permute-start | bytes 3080 | tf_op jit(solution)/shard_map/ppermute | solution.py:277
  9.9 1.3 %collective-permute-start.5 = (f32[2,128]{1,0:T(2,128)S(1)}, f32[2,128]{1,0:T(2,128)S(1)}, u32[]{:S(2)}, u32[]{:S(2)}) collective-permute-start(f32[2,128]{1,0:T(2,128)S(1)} %get-tuple-element.50), channel_id=1, source_target_pairs={{384,528},{432,480},{480,432},{528,384},{385,529},{433,481},{481,4... | collective-permute-start | bytes 3080 | tf_op jit(solution)/shard_map/ppermute | solution.py:278
  10.6 0.7 %collective-permute-start.6 = (f32[2,128]{1,0:T(2,128)S(1)}, f32[2,128]{1,0:T(2,128)S(1)}, u32[]{:S(2)}, u32[]{:S(2)}) collective-permute-start(f32[2,128]{1,0:T(2,128)S(1)} %fusion), channel_id=1, source_target_pairs={{192,384},{240,432},{288,480},{336,528},{193,385},{241,433},{289,4... | collective-permute-start | bytes 3080 | tf_op jit(solution)/shard_map/ppermute | solution.py:277
  11.3 18.7 %collective-permute-start.7 = (f32[2,128]{1,0:T(2,128)S(1)}, f32[2,128]{1,0:T(2,128)S(1)}, u32[]{:S(2)}, u32[]{:S(2)}) collective-permute-start(f32[2,128]{1,0:T(2,128)S(1)} %get-tuple-element.50), channel_id=1, source_target_pairs={{576,720},{624,672},{672,624},{720,576},{577,721},{625,673},{673,6... | collective-permute-start | bytes 3080 | tf_op jit(solution)/shard_map/ppermute | solution.py:278
  16.0 14.0 %collective-permute-start.8 = (f32[2,128]{1,0:T(2,128)S(1)}, f32[2,128]{1,0:T(2,128)S(1)}, u32[]{:S(2)}, u32[]{:S(2)}) collective-permute-start(f32[2,128]{1,0:T(2,128)S(1)} %get-tuple-element.51), channel_id=1, source_target_pairs={{384,576},{432,624},{480,672},{528,720},{385,577},{433,625},{481,6... | collective-permute-start | bytes 3080 | tf_op jit(solution)/shard_map/ppermute | solution.py:277

commit v6 on v3

--- a/solution.py
+++ b/solution.py
@@ -30,7 +30,7 @@
 
 def state_kernel(
     side, index_hbm, rates_hbm, residues_hbm, skip_hbm, key_hbm, value_hbm, query_hbm,
-    end_ref, rate_ref, gain_ref, far_ref, pair_ref, row_ref, skip_ref, mixed_ref, state_ref, query_ref,
+    end_ref, rate_ref, gain_ref, far_ref, row_ref, before_ref, skip_ref, mixed_ref, state_ref, query_ref,
     index_ref, rates_ref, residues_ref, skip_row, key_ref, value_ref, sems,
 ):
     channels, length = key_ref.shape
@@ -76,7 +76,6 @@
     gain_row = lanes_of(residues_ref[...]) * jnp.sqrt(one_minus_exp(2.0 * rate_row))
     own = iota((HALF, BLOCK), 1) // modes == iota((HALF, BLOCK), 0)
     place = lax.axis_index("ctx") % side
-    odd, upper = place % 2 == 1, place >= 2
     same = iota((channels, channels), 0) == iota((channels, channels), 1)
     skip = jnp.sum(jnp.where(same, skip_row[...], 0.0), axis=1, keepdims=True)
     skip_ref[...] = jnp.broadcast_to(skip, skip_ref.shape)
@@ -89,13 +88,10 @@
         passed = -rate * float(length)
         far_ref[0, here, :] = jnp.exp(passed * float(side))
         far_ref[1, here, :] = jnp.exp(passed * place.astype(F32))
-        once, twice = jnp.exp(passed), jnp.exp(2.0 * passed)
-        pair_ref[0, here, :] = jnp.where(odd, 1.0, once)
-        pair_ref[1, here, :] = jnp.where(odd, once, 1.0)
-        pair_ref[2, here, :] = jnp.where(odd, jnp.ones_like(once), 0.0)
-        row_ref[0, here, :] = jnp.where(upper, 1.0, twice)
-        row_ref[1, here, :] = jnp.where(upper, twice, 1.0)
-        row_ref[2, here, :] = jnp.where(upper, jnp.where(odd, once, 1.0), 0.0)
+        for x in range(side):
+            row_ref[x, here, :] = jnp.exp(passed * float(side - 1 - x))
+            gap = (place - 1 - x).astype(F32)
+            before_ref[x, here, :] = jnp.where(gap >= 0.0, jnp.exp(passed * jnp.maximum(gap, 0.0)), 0.0)
         to_end = (BLOCK - 1 - iota((BLOCK, BLOCK), 0)).astype(F32)
         fade_high, fade_low = split(jnp.exp(-rate * to_end))
         fades = jnp.concatenate([fade_high, fade_high, fade_low], axis=0)
@@ -211,10 +207,10 @@
     groups = channels // HALF
     line = (groups, BLOCK)
     stripes = (groups, blocks * HALF, BLOCK)
-    ends, rate, gain, far, pair, row, skip, mixed, state, query = pl.pallas_call(
+    ends, rate, gain, far, row, before, skip, mixed, state, query = pl.pallas_call(
         lambda *refs: state_kernel(SIDE, *refs),
         out_shape=(
-            shape(*line), shape(*line), shape(*line), shape(2, *line), shape(3, *line), shape(3, *line),
+            shape(*line), shape(*line), shape(*line), shape(2, *line), shape(SIDE, *line), shape(SIDE, *line),
             shape(channels, BLOCK), shape(*stripes), shape(*stripes), shape(channels, length),
         ),
         in_specs=[HBM] * 7,
@@ -251,19 +247,17 @@
             cost_estimate=pl.CostEstimate(flops=2 * 4 * 512 * 128 * 128, bytes_accessed=2**19, transcendentals=2**14),
         )(mixed, state, skip, rate, gain)
 
-    devices = lax.axis_size("ctx")
-    partner = lax.ppermute(ends, "ctx", [(d, d ^ 1) for d in range(devices)])
-    partner, first = lax.optimization_barrier((partner, local(0)))
-    both = pair[0] * ends + pair[1] * partner
-    across = lax.ppermute(both, "ctx", [(d, d ^ 3) for d in range(devices)])
-    across, second = lax.optimization_barrier((across, local(1)))
-    total = row[0] * both + row[1] * across
-    near = pair[2] * partner + row[2] * across
+    rows = lax.axis_size("ctx") // SIDE
+    every = lax.all_gather(ends, "ctx", axis_index_groups=[[r * SIDE + x for x in range(SIDE)] for r in range(rows)])
+    total = jnp.sum(row * every, axis=0)
+    near = jnp.sum(before * every, axis=0)
     carried = jnp.zeros(line, F32)
-    for r in range(devices // SIDE - 1):
-        sent = total + far[0] * carried if r else total
-        pairs = [(r * SIDE + x, (r + 1) * SIDE + x) for x in range(SIDE)]
-        carried = carried + lax.ppermute(sent, "ctx", pairs)
+    for r in range(1, rows):
+        sent = total + far[0] * carried if r > 1 else total
+        passed = lax.ppermute(sent, "ctx", [((r - 1) * SIDE + x, r * SIDE + x) for x in range(SIDE)])
+        if r == rows - 1:
+            passed, local_first, local_second = lax.optimization_barrier((passed, local(0), local(1)))
+        carried = carried + passed
 
     return pl.pallas_call(
         lambda *refs: output_kernel(modes, *refs),
@@ -273,7 +267,7 @@
         scratch_shapes=[pltpu.VMEM((channels, length), F32), pltpu.SemaphoreType.DMA((groups * blocks // 16,))],
         compiler_params=pltpu.CompilerParams(vmem_limit_bytes=16 * 2**20),
         cost_estimate=pl.CostEstimate(flops=2 * 3 * 1024 * 128 * 128, bytes_accessed=2**21, transcendentals=2**16),
-    )(query, rate, gain, far, near, carried, first[0], second[0], first[1], second[1])
+    )(query, rate, gain, far, near, carried, local_first[0], local_second[0], local_first[1], local_second[1])
 
 
 def solution(mesh):

time: 30.1 us -> 27.7 us (0.920)
  the two profiles are of different devices: /device:TPU:766 before, /device:TPU:704 now
where the time goes in v6:
time: 27.7 us; the launch traced here: 27.5 us
  waiting for transfers between devices  10.6 us (38%)
  blocking collectives  9.72 us (35%)
  Pallas kernels  4.51 us (16%)
  starting transfers between devices  2.61 us (9%)
    ppermute x3, waiting for transfers between devices, per_device(): lax.ppermute(sent, 'ctx', [((r - 1) * SIDE + x, r * SIDE + x) for x in ra...  10.6 us
    all_gather x1, blocking collectives, per_device(): lax.all_gather(ends, 'ctx', axis_index_groups=[[r * SIDE + x for x in ran...  9.72 us
    ppermute x3, starting transfers between devices, per_device(): lax.ppermute(sent, 'ctx', [((r - 1) * SIDE + x, r * SIDE + x) for x in ra...  2.61 us
    pallas_call x1, Pallas kernels, per_device(): pl.pallas_call(lambda *refs: state_kernel(SIDE, *refs), out_shape=(shape(...  1.72 us
    pallas_call x2, Pallas kernels, local(): pl.pallas_call(lambda *refs: local_kernel(g, modes, *refs), out_shape=(sh...  1.6 us
    pallas_call x1, Pallas kernels, per_device(): pl.pallas_call(lambda *refs: output_kernel(modes, *refs), out_shape=shape...  1.19 us
  transfers between devices with their start and end apart: 3, of which 1 were waited for; matrix products, arithmetic and copies ran while one was open for 0% of the time, Pallas kernels for 6%

profile of v6, /device:TPU:704, one launch (start us, length us, event | category | flops | bytes accessed | tf_op | source)
XLA Modules:
  0.0 27.5 jit_solution(1035920525210340030)
XLA Ops:
  0.0 1.7 %shard_map.73 = (f32[2,128]{1,0:T(2,128)S(1)}, f32[2,128]{1,0:T(2,128)S(1)}, f32[2,128]{1,0:T(2,128)S(1)}, f32[2,2,128]{2,1,0:T(2,128)S(1)}, f32[4,2,128]{2,1,0:...) custom-call(s32[1,16]{1,0:T(1,128)} %bitcast.15, ...), custom_call_target="tpu_custom_call" | custom-call | flops 100663296 | bytes 1048576 | tf_op jit(solution)/shard_map/pallas_call | solution.py:210
  1.7 9.7 %all-gather.1 = f32[4,2,128]{2,1,0:T(2,128)S(1)} all-gather(f32[1,2,128]{2,1,0:T(2,128)S(1)} %bitcast.12), channel_id=2, replica_groups={{0,48,96,144},{192,240,288,336},{384,432,480,528},{576,624,672,720},{1,..., dimensions={0}, use_global_device_ids=true | all-gather | bytes 5120 | tf_op jit(solution)/shard_map/all_gather | solution.py:251
  11.5 0.7 %collective-permute-start = (f32[2,128]{1,0:T(2,128)S(1)}, f32[2,128]{1,0:T(2,128)S(1)}, u32[]{:S(2)}, u32[]{:S(2)}) collective-permute-start(f32[2,128]{1,0:T(2,128)S(1)} %get-tuple-element.43), channel_id=1, source_target_pairs={{0,192},{48,240},{96,288},{144,336},{1,193},{49,241},{97,289},{145... | collective-permute-start | bytes 3080 | tf_op jit(solution)/shard_map/ppermute | solution.py:257
  12.1 0.0 collective-permute-done
  12.2 0.7 %collective-permute-start.1 = (f32[2,128]{1,0:T(2,128)S(1)}, f32[2,128]{1,0:T(2,128)S(1)}, u32[]{:S(2)}, u32[]{:S(2)}) collective-permute-start(f32[2,128]{1,0:T(2,128)S(1)} %fusion), channel_id=1, source_target_pairs={{192,384},{240,432},{288,480},{336,528},{193,385},{241,433},{289,4... | collective-permute-start | bytes 3080 | tf_op jit(solution)/shard_map/ppermute | solution.py:257
  12.8 0.8 %shard_map.74 = (f32[512,128]{1,0:T(8,128)S(1)}, f32[512,128]{1,0:T(8,128)S(1)}) custom-call(f32[2,512,128]{2,1,0:T(8,128)S(1)} %get-tuple-element.31.refs_0_, f32[2,512,128]{2,1,0:T(8,128)S(1)} %get-tuple-element.32.refs_1_, f32[16,128]{1,0:T(8,128)S(1)} %get-tuple-element.33.refs_2_, f32[2,128]{1,0:T(2,128)S(1)} %get-tuple-element.25.refs_3_.refs_1_, ...), custom_call_target="tpu_custom_call" | custom-call | flops 67108864 | bytes 524288 | tf_op jit(solution)/shard_map/pallas_call | solution.py:240
  13.6 0.0 collective-permute-done.1
  13.7 1.3 %collective-permute-start.2 = (f32[2,128]{1,0:T(2,128)S(1)}, f32[2,128]{1,0:T(2,128)S(1)}, u32[]{:S(2)}, u32[]{:S(2)}) collective-permute-start(f32[2,128]{1,0:T(2,128)S(1)} %get-tuple-element.45), channel_id=1, source_target_pairs={{384,576},{432,624},{480,672},{528,720},{385,577},{433,625},{481,6... | collective-permute-start | bytes 3080 | tf_op jit(solution)/shard_map/ppermute | solution.py:257
  15.0 0.8 %shard_map.75 = (f32[512,128]{1,0:T(8,128)S(1)}, f32[512,128]{1,0:T(8,128)S(1)}) custom-call(f32[2,512,128]{2,1,0:T(8,128)S(1)} %get-tuple-element.31.refs_0_, f32[2,512,128]{2,1,0:T(8,128)S(1)} %get-tuple-element.32.refs_1_, f32[16,128]{1,0:T(8,128)S(1)} %get-tuple-element.33.refs_2_, f32[2,128]{1,0:T(2,128)S(1)} %get-tuple-element.25.refs_3_.refs_1_, ...), custom_call_target="tpu_custom_call" | custom-call | flops 67108864 | bytes 524288 | tf_op jit(solution)/shard_map/pallas_call | solution.py:240
  15.8 10.6 %collective-permute-done.2 = f32[2,128]{1,0:T(2,128)S(1)} collective-permute-done((f32[2,128]{1,0:T(2,128)S(1)}, f32[2,128]{1,0:T(2,128)S(1)}, u32[]{:S(2)}, u32[]{:S(2)}) %collective-permute-start.2) | collective-permute-done | bytes 1056 | tf_op jit(solution)/shard_map/ppermute | solution.py:257
  26.3 1.2 %shard_map.76 = f32[16,8192]{1,0:T(8,128)} custom-call(f32[16,8192]{1,0:T(8,128)S(1)} %get-tuple-element.24.refs_0_, f32[2,128]{1,0:T(2,128)S(1)} %get-tuple-element.25.refs_3_.refs_1_, f32[2,128]{1,0:T(2,128)S(1)} %get-tuple-element.26.refs_4_.refs_2_, f32[2,2,128]{2,1,0:T(2,128)S(1)} %get-tuple-element.27.refs_3_, f32[2,128]{1,0:T(2,128)S(1)} %get-tuple-element.44.refs_4_, ...), custom_call_target="tpu_custom_call" | custom-call | flops 100663296 | bytes 2097152 | tf_op jit(solution)/shard_map/pallas_call | solution.py:262
  (4 shorter events, 0.0 us)
Async XLA Ops:
  11.5 0.7 %collective-permute-start = (f32[2,128]{1,0:T(2,128)S(1)}, f32[2,128]{1,0:T(2,128)S(1)}, u32[]{:S(2)}, u32[]{:S(2)}) collective-permute-start(f32[2,128]{1,0:T(2,128)S(1)} %get-tuple-element.43), channel_id=1, source_target_pairs={{0,192},{48,240},{96,288},{144,336},{1,193},{49,241},{97,289},{145... | collective-permute-start | bytes 3080 | tf_op jit(solution)/shard_map/ppermute | solution.py:257
  12.2 1.5 %collective-permute-start.1 = (f32[2,128]{1,0:T(2,128)S(1)}, f32[2,128]{1,0:T(2,128)S(1)}, u32[]{:S(2)}, u32[]{:S(2)}) collective-permute-start(f32[2,128]{1,0:T(2,128)S(1)} %fusion), channel_id=1, source_target_pairs={{192,384},{240,432},{288,480},{336,528},{193,385},{241,433},{289,4... | collective-permute-start | bytes 3080 | tf_op jit(solution)/shard_map/ppermute | solution.py:257
  13.7 12.7 %collective-permute-start.2 = (f32[2,128]{1,0:T(2,128)S(1)}, f32[2,128]{1,0:T(2,128)S(1)}, u32[]{:S(2)}, u32[]{:S(2)}) collective-permute-start(f32[2,128]{1,0:T(2,128)S(1)} %get-tuple-element.45), channel_id=1, source_target_pairs={{384,576},{432,624},{480,672},{528,720},{385,577},{433,625},{481,6... | collective-permute-start | bytes 3080 | tf_op jit(solution)/shard_map/ppermute | solution.py:257

commit v7 on v6

--- a/solution.py
+++ b/solution.py
@@ -30,7 +30,7 @@
 
 def state_kernel(
     side, index_hbm, rates_hbm, residues_hbm, skip_hbm, key_hbm, value_hbm, query_hbm,
-    end_ref, rate_ref, gain_ref, far_ref, row_ref, before_ref, skip_ref, mixed_ref, state_ref, query_ref,
+    end_ref, rate_ref, gain_ref, far_ref, enter_ref, leave_ref, skip_ref, mixed_ref, state_ref, query_ref,
     index_ref, rates_ref, residues_ref, skip_row, key_ref, value_ref, sems,
 ):
     channels, length = key_ref.shape
@@ -75,7 +75,13 @@
     rate_row = lanes_of(rates_ref[...])
     gain_row = lanes_of(residues_ref[...]) * jnp.sqrt(one_minus_exp(2.0 * rate_row))
     own = iota((HALF, BLOCK), 1) // modes == iota((HALF, BLOCK), 0)
-    place = lax.axis_index("ctx") % side
+    me = lax.axis_index("ctx")
+    place, inner = me % side, (me >= side) & (me < 3 * side)
+    member = iota((2 * side, BLOCK), 0)
+    member_row = jnp.where(inner, 1 + member // side, 3 * (member // side))
+    source = member_row * side + member % side
+    counted = (source < me) & (inner | (member_row == me // side))
+    handed = inner & (member < side)
     same = iota((channels, channels), 0) == iota((channels, channels), 1)
     skip = jnp.sum(jnp.where(same, skip_row[...], 0.0), axis=1, keepdims=True)
     skip_ref[...] = jnp.broadcast_to(skip, skip_ref.shape)
@@ -86,12 +92,20 @@
         rate_ref[here, :] = rate
         gain_ref[here, :] = gain_row[:, lanes]
         passed = -rate * float(length)
-        far_ref[0, here, :] = jnp.exp(passed * float(side))
-        far_ref[1, here, :] = jnp.exp(passed * place.astype(F32))
-        for x in range(side):
-            row_ref[x, here, :] = jnp.exp(passed * float(side - 1 - x))
-            gap = (place - 1 - x).astype(F32)
-            before_ref[x, here, :] = jnp.where(gap >= 0.0, jnp.exp(passed * jnp.maximum(gap, 0.0)), 0.0)
+        far_ref[here, :] = jnp.exp(passed * place.astype(F32))
+
+        def faded(wanted, steps):
+            return jnp.where(wanted, jnp.exp(passed * jnp.maximum(steps, 0).astype(F32)), 0.0)
+
+        tables = (
+            (enter_ref, 0, faded(counted, me - 1 - source)),
+            (enter_ref, 1, faded(handed, me - 1 - member)),
+            (leave_ref, 0, faded(member >= 0, 2 * side - 1 - member)),
+            (leave_ref, 1, faded(member < side, 3 * side - 1 - member)),
+        )
+        for target, part, table in tables:
+            for j in range(2 * side):
+                target[j, part * groups + g : part * groups + g + 1, :] = table[j : j + 1, :]
         to_end = (BLOCK - 1 - iota((BLOCK, BLOCK), 0)).astype(F32)
         fade_high, fade_low = split(jnp.exp(-rate * to_end))
         fades = jnp.concatenate([fade_high, fade_high, fade_low], axis=0)
@@ -169,7 +183,7 @@
         after = iota(square, 0).astype(F32) + 1.0
         lead_high, lead_low = split(gain * jnp.exp(-rate * after))
         leads = jnp.concatenate([lead_high, lead_high, lead_low], axis=1)
-        entered = near_ref[here, :] + far_ref[1, here, :] * carried_ref[here, :]
+        entered = near_ref[here, :] + far_ref[here, :] * carried_ref[here, :]
         fades = entered * jnp.exp(-rate * (BLOCK * iota((blocks, BLOCK), 0)).astype(F32))
         for start in range(0, blocks, 16):
             some = slice(start * HALF, (start + 16) * HALF)
@@ -207,10 +221,10 @@
     groups = channels // HALF
     line = (groups, BLOCK)
     stripes = (groups, blocks * HALF, BLOCK)
-    ends, rate, gain, far, row, before, skip, mixed, state, query = pl.pallas_call(
+    ends, rate, gain, far, enter, leave, skip, mixed, state, query = pl.pallas_call(
         lambda *refs: state_kernel(SIDE, *refs),
         out_shape=(
-            shape(*line), shape(*line), shape(*line), shape(2, *line), shape(SIDE, *line), shape(SIDE, *line),
+            shape(*line), shape(*line), shape(*line), shape(*line), shape(2 * SIDE, 2 * groups, BLOCK), shape(2 * SIDE, 2 * groups, BLOCK),
             shape(channels, BLOCK), shape(*stripes), shape(*stripes), shape(channels, length),
         ),
         in_specs=[HBM] * 7,
@@ -247,17 +261,21 @@
             cost_estimate=pl.CostEstimate(flops=2 * 4 * 512 * 128 * 128, bytes_accessed=2**19, transcendentals=2**14),
         )(mixed, state, skip, rate, gain)
 
-    rows = lax.axis_size("ctx") // SIDE
-    every = lax.all_gather(ends, "ctx", axis_index_groups=[[r * SIDE + x for x in range(SIDE)] for r in range(rows)])
-    total = jnp.sum(row * every, axis=0)
-    near = jnp.sum(before * every, axis=0)
-    carried = jnp.zeros(line, F32)
-    for r in range(1, rows):
-        sent = total + far[0] * carried if r > 1 else total
-        passed = lax.ppermute(sent, "ctx", [((r - 1) * SIDE + x, r * SIDE + x) for x in range(SIDE)])
-        if r == rows - 1:
-            passed, local_first, local_second = lax.optimization_barrier((passed, local(0), local(1)))
-        carried = carried + passed
+    handed = lax.ppermute(ends, "ctx", [(x, SIDE + x) for x in range(SIDE)])
+    own = jnp.concatenate([ends, handed], axis=0).reshape(1, 1, -1)
+    every = lax.all_to_all(
+        jnp.broadcast_to(own, (2 * SIDE, 1, own.size)),
+        "ctx",
+        split_axis=0,
+        concat_axis=0,
+        tiled=True,
+        axis_index_groups=[[*range(SIDE), *range(3 * SIDE, 4 * SIDE)], [*range(SIDE, 3 * SIDE)]],
+    )
+    every, local_first, local_second = lax.optimization_barrier((every, local(0), local(1)))
+    every = every.reshape(2 * SIDE, 2 * groups, BLOCK)
+    near = jnp.sum((enter * every).reshape(4 * SIDE, *line), axis=0)
+    sent = jnp.sum((leave * every).reshape(4 * SIDE, *line), axis=0)
+    carried = lax.ppermute(sent, "ctx", [(2 * SIDE + x, 3 * SIDE + x) for x in range(SIDE)])
 
     return pl.pallas_call(
         lambda *refs: output_kernel(modes, *refs),

time: 27.7 us -> 30.8 us (1.11)
  the two profiles are of different devices: /device:TPU:704 before, /device:TPU:48 now
where the time goes in v7:
time: 30.8 us; the launch traced here: 30.6 us
  starting transfers between devices  16.4 us (53%)
  waiting for transfers between devices  8.9 us (29%)
  Pallas kernels  4.51 us (15%)
  local copies, waits for them, and re-layouts  0.62 us (2%)
    all_to_all x1, starting transfers between devices, per_device(): lax.all_to_all(jnp.broadcast_to(own, (2 * SIDE, 1, own.size)), 'ctx', spl...  7.9 us
    ppermute x1, starting transfers between devices, per_device(): handed = lax.ppermute(ends, 'ctx', [(x, SIDE + x) for x in range(SIDE)])  7.89 us
    all_to_all x1, waiting for transfers between devices, per_device(): lax.all_to_all(jnp.broadcast_to(own, (2 * SIDE, 1, own.size)), 'ctx', spl...  7.61 us
    pallas_call x1, Pallas kernels, per_device(): pl.pallas_call(lambda *refs: state_kernel(SIDE, *refs), out_shape=(shape(...  1.72 us
    pallas_call x2, Pallas kernels, local(): pl.pallas_call(lambda *refs: local_kernel(g, modes, *refs), out_shape=(sh...  1.59 us
    ppermute x1, waiting for transfers between devices, per_device(): handed = lax.ppermute(ends, 'ctx', [(x, SIDE + x) for x in range(SIDE)])  1.28 us
    pallas_call x1, Pallas kernels, per_device(): pl.pallas_call(lambda *refs: output_kernel(modes, *refs), out_shape=shape...  1.19 us
    ppermute x1, starting transfers between devices, per_device(): lax.ppermute(sent, 'ctx', [(2 * SIDE + x, 3 * SIDE + x) for x in range(SI...  0.65 us
  transfers between devices with their start and end apart: 3, of which 2 were waited for; matrix products, arithmetic and copies ran while one was open for 0% of the time, Pallas kernels for 5%

profile of v7, /device:TPU:48, one launch (start us, length us, event | category | flops | bytes accessed | tf_op | source)
XLA Modules:
  0.0 30.6 jit_solution(3216155328054109163)
XLA Ops:
  0.0 1.7 %shard_map.73 = (f32[2,128]{1,0:T(2,128)S(1)}, f32[2,128]{1,0:T(2,128)S(1)}, f32[2,128]{1,0:T(2,128)S(1)}, f32[2,128]{1,0:T(2,128)S(1)}, f32[8,4,128]{2,1,0:T(4,...) custom-call(s32[1,16]{1,0:T(1,128)} %bitcast.21, ...), custom_call_target="tpu_custom_call" | custom-call | flops 100663296 | bytes 1048576 | tf_op jit(solution)/shard_map/pallas_call | solution.py:224
  1.7 7.9 %collective-permute-start = (f32[2,128]{1,0:T(2,128)S(1)}, f32[2,128]{1,0:T(2,128)S(1)}, u32[]{:S(2)}, u32[]{:S(2)}) collective-permute-start(f32[2,128]{1,0:T(2,128)S(1)} %get-tuple-element.29), channel_id=1, source_target_pairs={{0,192},{48,240},{96,288},{144,336},{1,193},{49,241},{97,289},{145... | collective-permute-start | bytes 3080 | tf_op jit(solution)/shard_map/ppermute | solution.py:264
  9.6 1.3 %collective-permute-done = f32[2,128]{1,0:T(2,128)S(1)} collective-permute-done((f32[2,128]{1,0:T(2,128)S(1)}, f32[2,128]{1,0:T(2,128)S(1)}, u32[]{:S(2)}, u32[]{:S(2)}) %collective-permute-start) | collective-permute-done | bytes 1056 | tf_op jit(solution)/shard_map/ppermute | solution.py:264
  10.9 0.6 %broadcast_in_dim.8 = f32[8,1,512]{2,1,0:T(1,128)} broadcast(f32[512]{0:T(512)S(1)} %maximum_bitcast_fusion), dimensions={2} | broadcast | bytes 18432 | tf_op jit(solution)/shard_map/broadcast_in_dim | solution.py:267
  11.5 7.9 %all-to-all-start = ((f32[8,1,512]{2,1,0:T(1,128)}), f32[8,1,512]{2,1,0:T(1,128)S(1)}, u32[]{:S(2)}, u32[]{:S(2)}) async-start(f32[8,1,512]{2,1,0:T(1,128)} %broadcast_in_dim.8), calls=%async_computation | async-start | bytes 32768 | tf_op jit(solution)/shard_map/all_to_all | solution.py:266
  19.4 0.8 %shard_map.75 = (f32[512,128]{1,0:T(8,128)S(1)}, f32[512,128]{1,0:T(8,128)S(1)}) custom-call(f32[2,512,128]{2,1,0:T(8,128)S(1)} %get-tuple-element.30.refs_0_, f32[2,512,128]{2,1,0:T(8,128)S(1)} %get-tuple-element.31.refs_1_, f32[16,128]{1,0:T(8,128)S(1)} %get-tuple-element.32.refs_2_, f32[2,128]{1,0:T(2,128)S(1)} %get-tuple-element.25.refs_3_.refs_1_, ...), custom_call_target="tpu_custom_call" | custom-call | flops 67108864 | bytes 524288 | tf_op jit(solution)/shard_map/pallas_call | solution.py:254
  20.2 0.8 %shard_map.74 = (f32[512,128]{1,0:T(8,128)S(1)}, f32[512,128]{1,0:T(8,128)S(1)}) custom-call(f32[2,512,128]{2,1,0:T(8,128)S(1)} %get-tuple-element.30.refs_0_, f32[2,512,128]{2,1,0:T(8,128)S(1)} %get-tuple-element.31.refs_1_, f32[16,128]{1,0:T(8,128)S(1)} %get-tuple-element.32.refs_2_, f32[2,128]{1,0:T(2,128)S(1)} %get-tuple-element.25.refs_3_.refs_1_, ...), custom_call_target="tpu_custom_call" | custom-call | flops 67108864 | bytes 524288 | tf_op jit(solution)/shard_map/pallas_call | solution.py:254
  21.0 7.6 %all-to-all-done = f32[8,1,512]{2,1,0:T(1,128)S(1)} async-done(((f32[8,1,512]{2,1,0:T(1,128)}), f32[8,1,512]{2,1,0:T(1,128)S(1)}, u32[]{:S(2)}, u32[]{:S(2)}) %all-to-all-start) | async-done | bytes 16416 | tf_op jit(solution)/shard_map/all_to_all | solution.py:266
  28.7 0.7 %collective-permute-start.1 = (f32[2,128]{1,0:T(2,128)S(1)}, f32[2,128]{1,0:T(2,128)S(1)}, u32[]{:S(2)}, u32[]{:S(2)}) collective-permute-start(f32[2,128]{1,0:T(2,128)S(1)} %reduce_sum.19), channel_id=1, source_target_pairs={{384,576},{432,624},{480,672},{528,720},{385,577},{433,625},{481,6... | collective-permute-start | bytes 3080 | tf_op jit(solution)/shard_map/ppermute | solution.py:278
  29.4 0.0 collective-permute-done.1.refs_5_
  29.4 1.2 %shard_map.76 = f32[16,8192]{1,0:T(8,128)} custom-call(f32[16,8192]{1,0:T(8,128)S(1)} %get-tuple-element.24.refs_0_, f32[2,128]{1,0:T(2,128)S(1)} %get-tuple-element.25.refs_3_.refs_1_, f32[2,128]{1,0:T(2,128)S(1)} %get-tuple-element.26.refs_4_.refs_2_, f32[2,128]{1,0:T(2,128)S(1)} %get-tuple-element.27.refs_3_, f32[2,128]{1,0:T(2,128)S(1)} %reduce_sum.18.refs_4_, ...), custom_call_target="tpu_custom_call" | custom-call | flops 100663296 | bytes 2097152 | tf_op jit(solution)/shard_map/pallas_call | solution.py:280
  (4 shorter events, 0.1 us)
Async XLA Ops:
  1.7 9.2 %collective-permute-start = (f32[2,128]{1,0:T(2,128)S(1)}, f32[2,128]{1,0:T(2,128)S(1)}, u32[]{:S(2)}, u32[]{:S(2)}) collective-permute-start(f32[2,128]{1,0:T(2,128)S(1)} %get-tuple-element.29), channel_id=1, source_target_pairs={{0,192},{48,240},{96,288},{144,336},{1,193},{49,241},{97,289},{145... | collective-permute-start | bytes 3080 | tf_op jit(solution)/shard_map/ppermute | solution.py:264
  11.5 17.1 %all-to-all-start = ((f32[8,1,512]{2,1,0:T(1,128)}), f32[8,1,512]{2,1,0:T(1,128)S(1)}, u32[]{:S(2)}, u32[]{:S(2)}) async-start(f32[8,1,512]{2,1,0:T(1,128)} %broadcast_in_dim.8), calls=%async_computation | async-start | bytes 32768 | tf_op jit(solution)/shard_map/all_to_all | solution.py:266
  28.7 0.7 %collective-permute-start.1 = (f32[2,128]{1,0:T(2,128)S(1)}, f32[2,128]{1,0:T(2,128)S(1)}, u32[]{:S(2)}, u32[]{:S(2)}) collective-permute-start(f32[2,128]{1,0:T(2,128)S(1)} %reduce_sum.19), channel_id=1, source_target_pairs={{384,576},{432,624},{480,672},{528,720},{385,577},{433,625},{481,6... | collective-permute-start | bytes 3080 | tf_op jit(solution)/shard_map/ppermute | solution.py:278

commit v8 on v7

--- a/solution.py
+++ b/solution.py
@@ -78,9 +78,9 @@
     me = lax.axis_index("ctx")
     place, inner = me % side, (me >= side) & (me < 3 * side)
     member = iota((2 * side, BLOCK), 0)
-    member_row = jnp.where(inner, 1 + member // side, 3 * (member // side))
-    source = member_row * side + member % side
-    counted = (source < me) & (inner | (member_row == me // side))
+    own_part = member // side == lax.axis_index("chan") % 2
+    source = jnp.where(inner, side + member, me - place + member % side)
+    counted = (source < me) & (inner | own_part)
     handed = inner & (member < side)
     same = iota((channels, channels), 0) == iota((channels, channels), 1)
     skip = jnp.sum(jnp.where(same, skip_row[...], 0.0), axis=1, keepdims=True)
@@ -261,15 +261,22 @@
             cost_estimate=pl.CostEstimate(flops=2 * 4 * 512 * 128 * 128, bytes_accessed=2**19, transcendentals=2**14),
         )(mixed, state, skip, rate, gain)
 
+    parts = lax.axis_size("chan")
+    inner = [[d * parts + part for d in range(SIDE, 3 * SIDE)] for part in range(parts)]
+    outer = [
+        [(row + x) * parts + pair + core for core in range(2) for x in range(SIDE)]
+        for row in (0, 3 * SIDE)
+        for pair in range(0, parts, 2)
+    ]
     handed = lax.ppermute(ends, "ctx", [(x, SIDE + x) for x in range(SIDE)])
     own = jnp.concatenate([ends, handed], axis=0).reshape(1, 1, -1)
     every = lax.all_to_all(
         jnp.broadcast_to(own, (2 * SIDE, 1, own.size)),
-        "ctx",
+        ("ctx", "chan"),
         split_axis=0,
         concat_axis=0,
         tiled=True,
-        axis_index_groups=[[*range(SIDE), *range(3 * SIDE, 4 * SIDE)], [*range(SIDE, 3 * SIDE)]],
+        axis_index_groups=inner + outer,
     )
     every, local_first, local_second = lax.optimization_barrier((every, local(0), local(1)))
     every = every.reshape(2 * SIDE, 2 * groups, BLOCK)

time: 30.8 us -> 26.7 us (0.87)
  the two profiles are of different devices: /device:TPU:48 before, /device:TPU:192 now
where the time goes in v8:
time: 26.7 us; the launch traced here: 26.4 us
  waiting for transfers between devices  15.9 us (60%)
  starting transfers between devices  5.28 us (20%)
  Pallas kernels  4.51 us (17%)
  local copies, waits for them, and re-layouts  0.62 us (2%)
    ppermute x1, waiting for transfers between devices, per_device(): handed = lax.ppermute(ends, 'ctx', [(x, SIDE + x) for x in range(SIDE)])  8.37 us
    all_to_all x1, waiting for transfers between devices, per_device(): lax.all_to_all(jnp.broadcast_to(own, (2 * SIDE, 1, own.size)), ('ctx', 'c...  7.54 us
    all_to_all x1, starting transfers between devices, per_device(): lax.all_to_all(jnp.broadcast_to(own, (2 * SIDE, 1, own.size)), ('ctx', 'c...  3.34 us
    pallas_call x1, Pallas kernels, per_device(): pl.pallas_call(lambda *refs: state_kernel(SIDE, *refs), out_shape=(shape(...  1.72 us
    pallas_call x2, Pallas kernels, local(): pl.pallas_call(lambda *refs: local_kernel(g, modes, *refs), out_shape=(sh...  1.6 us
    ppermute x1, starting transfers between devices, per_device(): handed = lax.ppermute(ends, 'ctx', [(x, SIDE + x) for x in range(SIDE)])  1.29 us
    pallas_call x1, Pallas kernels, per_device(): pl.pallas_call(lambda *refs: output_kernel(modes, *refs), out_shape=shape...  1.19 us
    ppermute x1, starting transfers between devices, per_device(): lax.ppermute(sent, 'ctx', [(2 * SIDE + x, 3 * SIDE + x) for x in range(SI...  0.65 us
  transfers between devices with their start and end apart: 3, of which 2 were waited for; matrix products, arithmetic and copies ran while one was open for 0% of the time, Pallas kernels for 6%

profile of v8, /device:TPU:192, one launch (start us, length us, event | category | flops | bytes accessed | tf_op | source)
XLA Modules:
  0.0 26.4 jit_solution(8161158139290328030)
XLA Ops:
  0.0 1.7 %shard_map.73 = (f32[2,128]{1,0:T(2,128)S(1)}, f32[2,128]{1,0:T(2,128)S(1)}, f32[2,128]{1,0:T(2,128)S(1)}, f32[2,128]{1,0:T(2,128)S(1)}, f32[8,4,128]{2,1,0:T(4,...) custom-call(s32[1,16]{1,0:T(1,128)} %bitcast.21, ...), custom_call_target="tpu_custom_call" | custom-call | flops 100663296 | bytes 1048576 | tf_op jit(solution)/shard_map/pallas_call | solution.py:224
  1.7 1.3 %collective-permute-start = (f32[2,128]{1,0:T(2,128)S(1)}, f32[2,128]{1,0:T(2,128)S(1)}, u32[]{:S(2)}, u32[]{:S(2)}) collective-permute-start(f32[2,128]{1,0:T(2,128)S(1)} %get-tuple-element.29), channel_id=1, source_target_pairs={{0,192},{48,240},{96,288},{144,336},{1,193},{49,241},{97,289},{145... | collective-permute-start | bytes 3080 | tf_op jit(solution)/shard_map/ppermute | solution.py:271
  3.0 8.4 %collective-permute-done = f32[2,128]{1,0:T(2,128)S(1)} collective-permute-done((f32[2,128]{1,0:T(2,128)S(1)}, f32[2,128]{1,0:T(2,128)S(1)}, u32[]{:S(2)}, u32[]{:S(2)}) %collective-permute-start) | collective-permute-done | bytes 1056 | tf_op jit(solution)/shard_map/ppermute | solution.py:271
  11.4 0.6 %broadcast_in_dim.8 = f32[8,1,512]{2,1,0:T(1,128)} broadcast(f32[512]{0:T(512)S(1)} %maximum_bitcast_fusion), dimensions={2} | broadcast | bytes 18432 | tf_op jit(solution)/shard_map/broadcast_in_dim | solution.py:274
  12.0 3.3 %all-to-all-start = ((f32[8,1,512]{2,1,0:T(1,128)}), f32[8,1,512]{2,1,0:T(1,128)S(1)}, u32[]{:S(2)}, u32[]{:S(2)}) async-start(f32[8,1,512]{2,1,0:T(1,128)} %broadcast_in_dim.8), calls=%async_computation | async-start | bytes 32768 | tf_op jit(solution)/shard_map/all_to_all | solution.py:273
  15.4 0.8 %shard_map.75 = (f32[512,128]{1,0:T(8,128)S(1)}, f32[512,128]{1,0:T(8,128)S(1)}) custom-call(f32[2,512,128]{2,1,0:T(8,128)S(1)} %get-tuple-element.30.refs_0_, f32[2,512,128]{2,1,0:T(8,128)S(1)} %get-tuple-element.31.refs_1_, f32[16,128]{1,0:T(8,128)S(1)} %get-tuple-element.32.refs_2_, f32[2,128]{1,0:T(2,128)S(1)} %get-tuple-element.25.refs_3_.refs_1_, ...), custom_call_target="tpu_custom_call" | custom-call | flops 67108864 | bytes 524288 | tf_op jit(solution)/shard_map/pallas_call | solution.py:254
  16.2 0.8 %shard_map.74 = (f32[512,128]{1,0:T(8,128)S(1)}, f32[512,128]{1,0:T(8,128)S(1)}) custom-call(f32[2,512,128]{2,1,0:T(8,128)S(1)} %get-tuple-element.30.refs_0_, f32[2,512,128]{2,1,0:T(8,128)S(1)} %get-tuple-element.31.refs_1_, f32[16,128]{1,0:T(8,128)S(1)} %get-tuple-element.32.refs_2_, f32[2,128]{1,0:T(2,128)S(1)} %get-tuple-element.25.refs_3_.refs_1_, ...), custom_call_target="tpu_custom_call" | custom-call | flops 67108864 | bytes 524288 | tf_op jit(solution)/shard_map/pallas_call | solution.py:254
  17.0 7.5 %all-to-all-done = f32[8,1,512]{2,1,0:T(1,128)S(1)} async-done(((f32[8,1,512]{2,1,0:T(1,128)}), f32[8,1,512]{2,1,0:T(1,128)S(1)}, u32[]{:S(2)}, u32[]{:S(2)}) %all-to-all-start) | async-done | bytes 16416 | tf_op jit(solution)/shard_map/all_to_all | solution.py:273
  24.6 0.7 %collective-permute-start.1 = (f32[2,128]{1,0:T(2,128)S(1)}, f32[2,128]{1,0:T(2,128)S(1)}, u32[]{:S(2)}, u32[]{:S(2)}) collective-permute-start(f32[2,128]{1,0:T(2,128)S(1)} %reduce_sum.19), channel_id=1, source_target_pairs={{384,576},{432,624},{480,672},{528,720},{385,577},{433,625},{481,6... | collective-permute-start | bytes 3080 | tf_op jit(solution)/shard_map/ppermute | solution.py:285
  25.3 0.0 collective-permute-done.1.refs_5_
  25.3 1.2 %shard_map.76 = f32[16,8192]{1,0:T(8,128)} custom-call(f32[16,8192]{1,0:T(8,128)S(1)} %get-tuple-element.24.refs_0_, f32[2,128]{1,0:T(2,128)S(1)} %get-tuple-element.25.refs_3_.refs_1_, f32[2,128]{1,0:T(2,128)S(1)} %get-tuple-element.26.refs_4_.refs_2_, f32[2,128]{1,0:T(2,128)S(1)} %get-tuple-element.27.refs_3_, f32[2,128]{1,0:T(2,128)S(1)} %reduce_sum.18.refs_4_, ...), custom_call_target="tpu_custom_call" | custom-call | flops 100663296 | bytes 2097152 | tf_op jit(solution)/shard_map/pallas_call | solution.py:287
  (4 shorter events, 0.1 us)
Async XLA Ops:
  1.7 9.7 %collective-permute-start = (f32[2,128]{1,0:T(2,128)S(1)}, f32[2,128]{1,0:T(2,128)S(1)}, u32[]{:S(2)}, u32[]{:S(2)}) collective-permute-start(f32[2,128]{1,0:T(2,128)S(1)} %get-tuple-element.29), channel_id=1, source_target_pairs={{0,192},{48,240},{96,288},{144,336},{1,193},{49,241},{97,289},{145... | collective-permute-start | bytes 3080 | tf_op jit(solution)/shard_map/ppermute | solution.py:271
  12.0 12.5 %all-to-all-start = ((f32[8,1,512]{2,1,0:T(1,128)}), f32[8,1,512]{2,1,0:T(1,128)S(1)}, u32[]{:S(2)}, u32[]{:S(2)}) async-start(f32[8,1,512]{2,1,0:T(1,128)} %broadcast_in_dim.8), calls=%async_computation | async-start | bytes 32768 | tf_op jit(solution)/shard_map/all_to_all | solution.py:273
  24.6 0.7 %collective-permute-start.1 = (f32[2,128]{1,0:T(2,128)S(1)}, f32[2,128]{1,0:T(2,128)S(1)}, u32[]{:S(2)}, u32[]{:S(2)}) collective-permute-start(f32[2,128]{1,0:T(2,128)S(1)} %reduce_sum.19), channel_id=1, source_target_pairs={{384,576},{432,624},{480,672},{528,720},{385,577},{433,625},{481,6... | collective-permute-start | bytes 3080 | tf_op jit(solution)/shard_map/ppermute | solution.py:285

commit v9 on v8

--- a/solution.py
+++ b/solution.py
@@ -29,8 +29,8 @@
 
 
 def state_kernel(
-    side, index_hbm, rates_hbm, residues_hbm, skip_hbm, key_hbm, value_hbm, query_hbm,
-    end_ref, rate_ref, gain_ref, far_ref, enter_ref, leave_ref, skip_ref, mixed_ref, state_ref, query_ref,
+    index_hbm, rates_hbm, residues_hbm, skip_hbm, key_hbm, value_hbm, query_hbm,
+    end_ref, rate_ref, gain_ref, skip_ref, mixed_ref, state_ref, query_ref,
     index_ref, rates_ref, residues_ref, skip_row, key_ref, value_ref, sems,
 ):
     channels, length = key_ref.shape
@@ -57,7 +57,7 @@
         loads.append(pair)
     query_load = pltpu.make_async_copy(query_hbm, query_ref, sems.at[2 * groups])
     query_load.start()
-    for copy in small:
+    for copy in small + loads[0] + loads[1]:
         copy.wait()
 
     wide = (channels, channels * modes)
@@ -75,13 +75,6 @@
     rate_row = lanes_of(rates_ref[...])
     gain_row = lanes_of(residues_ref[...]) * jnp.sqrt(one_minus_exp(2.0 * rate_row))
     own = iota((HALF, BLOCK), 1) // modes == iota((HALF, BLOCK), 0)
-    me = lax.axis_index("ctx")
-    place, inner = me % side, (me >= side) & (me < 3 * side)
-    member = iota((2 * side, BLOCK), 0)
-    own_part = member // side == lax.axis_index("chan") % 2
-    source = jnp.where(inner, side + member, me - place + member % side)
-    counted = (source < me) & (inner | own_part)
-    handed = inner & (member < side)
     same = iota((channels, channels), 0) == iota((channels, channels), 1)
     skip = jnp.sum(jnp.where(same, skip_row[...], 0.0), axis=1, keepdims=True)
     skip_ref[...] = jnp.broadcast_to(skip, skip_ref.shape)
@@ -91,21 +84,6 @@
         here = slice(g, g + 1)
         rate_ref[here, :] = rate
         gain_ref[here, :] = gain_row[:, lanes]
-        passed = -rate * float(length)
-        far_ref[here, :] = jnp.exp(passed * place.astype(F32))
-
-        def faded(wanted, steps):
-            return jnp.where(wanted, jnp.exp(passed * jnp.maximum(steps, 0).astype(F32)), 0.0)
-
-        tables = (
-            (enter_ref, 0, faded(counted, me - 1 - source)),
-            (enter_ref, 1, faded(handed, me - 1 - member)),
-            (leave_ref, 0, faded(member >= 0, 2 * side - 1 - member)),
-            (leave_ref, 1, faded(member < side, 3 * side - 1 - member)),
-        )
-        for target, part, table in tables:
-            for j in range(2 * side):
-                target[j, part * groups + g : part * groups + g + 1, :] = table[j : j + 1, :]
         to_end = (BLOCK - 1 - iota((BLOCK, BLOCK), 0)).astype(F32)
         fade_high, fade_low = split(jnp.exp(-rate * to_end))
         fades = jnp.concatenate([fade_high, fade_high, fade_low], axis=0)
@@ -113,8 +91,6 @@
         block_fade = jnp.exp(-rate * later)
         rows = slice(g * HALF, (g + 1) * HALF)
         total = jnp.zeros((HALF, BLOCK), F32)
-        for copy in loads[g]:
-            copy.wait()
         for start in range(0, blocks, 16):
             mixed = jnp.concatenate(
                 [
@@ -135,7 +111,39 @@
     query_load.wait()
 
 
-def local_kernel(g, modes, mixed_ref, state_ref, skip_ref, rate_ref, gain_ref, base_ref, enter_ref, conv_rows):
+def weight_tables(side, length, rate_ref, far_ref, enter_ref, leave_ref):
+    me = lax.axis_index("ctx")
+    place, inner = me % side, (me >= side) & (me < 3 * side)
+    member = iota((2 * side, BLOCK), 0)
+    own_part = member // side == lax.axis_index("chan") % 2
+    source = jnp.where(inner, side + member, me - place + member % side)
+    counted = (source < me) & (inner | own_part)
+    handed = inner & (member < side)
+    groups = rate_ref.shape[0]
+    for g in range(groups):
+        here = slice(g, g + 1)
+        rate = rate_ref[here, :]
+        passed = -rate * float(length)
+        far_ref[here, :] = jnp.exp(passed * place.astype(F32))
+
+        def faded(wanted, steps):
+            return jnp.where(wanted, jnp.exp(passed * jnp.maximum(steps, 0).astype(F32)), 0.0)
+
+        tables = (
+            (enter_ref, 0, faded(counted, me - 1 - source)),
+            (enter_ref, 1, faded(handed, me - 1 - member)),
+            (leave_ref, 0, faded(member >= 0, 2 * side - 1 - member)),
+            (leave_ref, 1, faded(member < side, 3 * side - 1 - member)),
+        )
+        for target, part, table in tables:
+            for j in range(2 * side):
+                target[j, part * groups + g : part * groups + g + 1, :] = table[j : j + 1, :]
+
+
+def local_kernel(g, modes, side, length, mixed_ref, state_ref, skip_ref, rate_ref, gain_ref, base_ref, enter_ref, *rest):
+    conv_rows = rest[-1]
+    if rest[:-1]:
+        weight_tables(side, length, rate_ref, *rest[:-1])
     blocks = base_ref.shape[0] // HALF
     square = (BLOCK, BLOCK)
     own = iota((HALF, BLOCK), 1) // modes == iota((HALF, BLOCK), 0)
@@ -221,14 +229,14 @@
     groups = channels // HALF
     line = (groups, BLOCK)
     stripes = (groups, blocks * HALF, BLOCK)
-    ends, rate, gain, far, enter, leave, skip, mixed, state, query = pl.pallas_call(
-        lambda *refs: state_kernel(SIDE, *refs),
+    ends, rate, gain, skip, mixed, state, query = pl.pallas_call(
+        state_kernel,
         out_shape=(
-            shape(*line), shape(*line), shape(*line), shape(*line), shape(2 * SIDE, 2 * groups, BLOCK), shape(2 * SIDE, 2 * groups, BLOCK),
+            shape(*line), shape(*line), shape(*line),
             shape(channels, BLOCK), shape(*stripes), shape(*stripes), shape(channels, length),
         ),
         in_specs=[HBM] * 7,
-        out_specs=(VMEM,) * 10,
+        out_specs=(VMEM,) * 7,
         scratch_shapes=[
             pltpu.VMEM((1, channels), jnp.int32),
             pltpu.VMEM((modes, residues.shape[0]), F32),
@@ -250,12 +258,14 @@
         )
     )
 
-    def local(g):
+    tables = (shape(*line), shape(2 * SIDE, 2 * groups, BLOCK), shape(2 * SIDE, 2 * groups, BLOCK))
+
+    def local(g, more=()):
         return pl.pallas_call(
-            lambda *refs: local_kernel(g, modes, *refs),
-            out_shape=(shape(*stripes[1:]), shape(*stripes[1:])),
+            lambda *refs: local_kernel(g, modes, SIDE, length, *refs),
+            out_shape=(shape(*stripes[1:]), shape(*stripes[1:]), *more),
             in_specs=[VMEM] * 5,
-            out_specs=(VMEM, VMEM),
+            out_specs=(VMEM,) * (2 + len(more)),
             scratch_shapes=[pltpu.VMEM(stripes[1:], F32)],
             compiler_params=pltpu.CompilerParams(vmem_limit_bytes=16 * 2**20),
             cost_estimate=pl.CostEstimate(flops=2 * 4 * 512 * 128 * 128, bytes_accessed=2**19, transcendentals=2**14),
@@ -269,6 +279,8 @@
         for pair in range(0, parts, 2)
     ]
     handed = lax.ppermute(ends, "ctx", [(x, SIDE + x) for x in range(SIDE)])
+    handed, local_first, local_second = lax.optimization_barrier((handed, local(0, tables), local(1)))
+    far, enter, leave = local_first[2:]
     own = jnp.concatenate([ends, handed], axis=0).reshape(1, 1, -1)
     every = lax.all_to_all(
         jnp.broadcast_to(own, (2 * SIDE, 1, own.size)),
@@ -278,7 +290,6 @@
         tiled=True,
         axis_index_groups=inner + outer,
     )
-    every, local_first, local_second = lax.optimization_barrier((every, local(0), local(1)))
     every = every.reshape(2 * SIDE, 2 * groups, BLOCK)
     near = jnp.sum((enter * every).reshape(4 * SIDE, *line), axis=0)
     sent = jnp.sum((leave * every).reshape(4 * SIDE, *line), axis=0)

time: 26.7 us -> 26.4 us (0.989)
  blocking collectives: 0 us -> 12.6 us
  waiting for transfers between devices: 15.9 us -> 6.75 us
  starting transfers between devices: 5.28 us -> 1.94 us
  local copies, waits for them, and re-layouts: 0.62 us -> 0.01 us
  Pallas kernels: 4.51 us -> 4.81 us
    all_to_all x0 -> x1, blocking collectives: none -> 12.6 us  [per_device(): lax.all_to_all(jnp.broadcast_to(own, (2 * SIDE, 1, own.size)), ('ctx', 'c...]
    all_to_all x1 -> x0, waiting for transfers between devices: 7.54 us -> none  [per_device(): lax.all_to_all(jnp.broadcast_to(own, (2 * SIDE, 1, own.size)), ('ctx', 'c...]
    all_to_all x1 -> x0, starting transfers between devices: 3.34 us -> none  [per_device(): lax.all_to_all(jnp.broadcast_to(own, (2 * SIDE, 1, own.size)), ('ctx', 'c...]
    ppermute x1, waiting for transfers between devices: 8.37 us -> 6.75 us  [per_device(): handed = lax.ppermute(ends, 'ctx', [(x, SIDE + x) for x in range(SIDE)])]
    broadcast_in_dim x1, local copies, waits for them, and re-layouts: 0.62 us -> 0.01 us  [per_device(): jnp.broadcast_to(own, (2 * SIDE, 1, own.size))]
    pallas_call x3, Pallas kernels: 3.32 us -> 3.62 us  [the longest x1 2.02 us: per_device(): pl.pallas_call(state_kernel, out_shape=(shape(*line), shape(*line), shape...]
  transfers between devices with their start and end apart: 3 -> 2, of which waited for: 2 -> 1; matrix products, arithmetic and copies ran while one was open for 0% -> 0% of each run, Pallas kernels for 6% -> 6%
where the time goes in v9:
time: 26.4 us; the launch traced here: 26.2 us
  blocking collectives  12.6 us (48%)
  waiting for transfers between devices  6.75 us (26%)
  Pallas kernels  4.81 us (18%)
  starting transfers between devices  1.94 us (7%)
    all_to_all x1, blocking collectives, per_device(): lax.all_to_all(jnp.broadcast_to(own, (2 * SIDE, 1, own.size)), ('ctx', 'c...  12.6 us
    ppermute x1, waiting for transfers between devices, per_device(): handed = lax.ppermute(ends, 'ctx', [(x, SIDE + x) for x in range(SIDE)])  6.75 us
    pallas_call x1, Pallas kernels, per_device(): pl.pallas_call(state_kernel, out_shape=(shape(*line), shape(*line), shape...  2.02 us
    pallas_call x2, Pallas kernels, local(): pl.pallas_call(lambda *refs: local_kernel(g, modes, SIDE, length, *refs),...  1.6 us
    ppermute x1, starting transfers between devices, per_device(): handed = lax.ppermute(ends, 'ctx', [(x, SIDE + x) for x in range(SIDE)])  1.29 us
    pallas_call x1, Pallas kernels, per_device(): pl.pallas_call(lambda *refs: output_kernel(modes, *refs), out_shape=shape...  1.19 us
    ppermute x1, starting transfers between devices, per_device(): lax.ppermute(sent, 'ctx', [(2 * SIDE + x, 3 * SIDE + x) for x in range(SI...  0.65 us
  transfers between devices with their start and end apart: 2, of which 1 were waited for; matrix products, arithmetic and copies ran while one was open for 0% of the time, Pallas kernels for 6%

profile of v9, /device:TPU:192, one launch (start us, length us, event | category | flops | bytes accessed | tf_op | source)
XLA Modules:
  0.0 26.2 jit_solution(3927245405327649871)
XLA Ops:
  0.0 2.0 %shard_map.73 = (f32[2,128]{1,0:T(2,128)S(1)}, f32[2,128]{1,0:T(2,128)S(1)}, f32[2,128]{1,0:T(2,128)S(1)}, f32[16,128]{1,0:T(8,128)S(1)}, f32[2,512,128]{2,1,0:T...) custom-call(s32[1,16]{1,0:T(1,128)} %bitcast.21, f32[16,48]{1,0:T(8,128)} %bitcast.19, ...), custom_call_target="tpu_custom_call" | custom-call | flops 100663296 | bytes 1048576 | tf_op jit(solution)/shard_map/pallas_call | solution.py:232
  2.0 1.3 %collective-permute-start = (f32[2,128]{1,0:T(2,128)S(1)}, f32[2,128]{1,0:T(2,128)S(1)}, u32[]{:S(2)}, u32[]{:S(2)}) collective-permute-start(f32[2,128]{1,0:T(2,128)S(1)} %get-tuple-element.30), channel_id=1, source_target_pairs={{0,192},{48,240},{96,288},{144,336},{1,193},{49,241},{97,289},{145... | collective-permute-start | bytes 3080 | tf_op jit(solution)/shard_map/ppermute | solution.py:281
  3.3 0.8 %shard_map.74 = (f32[512,128]{1,0:T(8,128)S(1)}, f32[512,128]{1,0:T(8,128)S(1)}, f32[2,128]{1,0:T(2,128)S(1)}, f32[8,4,128]{2,1,0:T(4,128)S(1)}, f32[8,4,128]{2,1,0:T(4,128)S(1)}) custom-call(f32[2,512,128]{2,1,0:T(8,128)S(1)} %get-tuple-element.31.refs_0_, f32[2,512,128]{2,1,0:T(8,128)S(1)} %get-tuple-element.32.refs_1_, ...), custom_call_target="tpu_custom_call" | custom-call | flops 67108864 | bytes 524288 | tf_op jit(solution)/shard_map/pallas_call | solution.py:264
  4.1 0.8 %shard_map.75 = (f32[512,128]{1,0:T(8,128)S(1)}, f32[512,128]{1,0:T(8,128)S(1)}) custom-call(f32[2,512,128]{2,1,0:T(8,128)S(1)} %get-tuple-element.31.refs_0_, f32[2,512,128]{2,1,0:T(8,128)S(1)} %get-tuple-element.32.refs_1_, f32[16,128]{1,0:T(8,128)S(1)} %get-tuple-element.33.refs_2_, f32[2,128]{1,0:T(2,128)S(1)} %get-tuple-element.28.refs_3_.refs_1_, ...), custom_call_target="tpu_custom_call" | custom-call | flops 67108864 | bytes 524288 | tf_op jit(solution)/shard_map/pallas_call | solution.py:264
  4.9 6.8 %collective-permute-done = f32[2,128]{1,0:T(2,128)S(1)} collective-permute-done((f32[2,128]{1,0:T(2,128)S(1)}, f32[2,128]{1,0:T(2,128)S(1)}, u32[]{:S(2)}, u32[]{:S(2)}) %collective-permute-start) | collective-permute-done | bytes 1056 | tf_op jit(solution)/shard_map/ppermute | solution.py:281
  11.7 12.6 %all_to_all.5 = f32[8,1,512]{2,1,0:T(1,128)S(1)} all-to-all(f32[8,1,512]{2,1,0:T(1,128)S(1)} %broadcast_in_dim.8), channel_id=1, replica_groups={{192,240,288,336,384,432,480,528},{193,241,289,337,385,433,481,529},{19..., dimensions={0} | all-to-all | bytes 32768 | tf_op jit(solution)/shard_map/all_to_all | solution.py:285
  24.4 0.7 %collective-permute-start.1 = (f32[2,128]{1,0:T(2,128)S(1)}, f32[2,128]{1,0:T(2,128)S(1)}, u32[]{:S(2)}, u32[]{:S(2)}) collective-permute-start(f32[2,128]{1,0:T(2,128)S(1)} %reduce_sum.19), channel_id=1, source_target_pairs={{384,576},{432,624},{480,672},{528,720},{385,577},{433,625},{481,6... | collective-permute-start | bytes 3080 | tf_op jit(solution)/shard_map/ppermute | solution.py:296
  25.0 0.0 collective-permute-done.1.refs_5_
  25.0 1.2 %shard_map.76 = f32[16,8192]{1,0:T(8,128)} custom-call(f32[16,8192]{1,0:T(8,128)S(1)} %get-tuple-element.27.refs_0_, f32[2,128]{1,0:T(2,128)S(1)} %get-tuple-element.28.refs_3_.refs_1_, f32[2,128]{1,0:T(2,128)S(1)} %get-tuple-element.29.refs_4_.refs_2_, f32[2,128]{1,0:T(2,128)S(1)} %get-tuple-element.41.refs_3_, f32[2,128]{1,0:T(2,128)S(1)} %reduce_sum.18.refs_4_, ...), custom_call_target="tpu_custom_call" | custom-call | flops 100663296 | bytes 2097152 | tf_op jit(solution)/shard_map/pallas_call | solution.py:298
  (5 shorter events, 0.1 us)
Async XLA Ops:
  2.0 9.7 %collective-permute-start = (f32[2,128]{1,0:T(2,128)S(1)}, f32[2,128]{1,0:T(2,128)S(1)}, u32[]{:S(2)}, u32[]{:S(2)}) collective-permute-start(f32[2,128]{1,0:T(2,128)S(1)} %get-tuple-element.30), channel_id=1, source_target_pairs={{0,192},{48,240},{96,288},{144,336},{1,193},{49,241},{97,289},{145... | collective-permute-start | bytes 3080 | tf_op jit(solution)/shard_map/ppermute | solution.py:281
  24.4 0.7 %collective-permute-start.1 = (f32[2,128]{1,0:T(2,128)S(1)}, f32[2,128]{1,0:T(2,128)S(1)}, u32[]{:S(2)}, u32[]{:S(2)}) collective-permute-start(f32[2,128]{1,0:T(2,128)S(1)} %reduce_sum.19), channel_id=1, source_target_pairs={{384,576},{432,624},{480,672},{528,720},{385,577},{433,625},{481,6... | collective-permute-start | bytes 3080 | tf_op jit(solution)/shard_map/ppermute | solution.py:296

commit v10 on v9

--- a/solution.py
+++ b/solution.py
@@ -30,7 +30,7 @@
 
 def state_kernel(
     index_hbm, rates_hbm, residues_hbm, skip_hbm, key_hbm, value_hbm, query_hbm,
-    end_ref, rate_ref, gain_ref, skip_ref, mixed_ref, state_ref, query_ref,
+    end_ref, rate_ref, weight_ref, skip_ref, mixed_ref, state_ref, query_ref,
     index_ref, rates_ref, residues_ref, skip_row, key_ref, value_ref, sems,
 ):
     channels, length = key_ref.shape
@@ -57,7 +57,7 @@
         loads.append(pair)
     query_load = pltpu.make_async_copy(query_hbm, query_ref, sems.at[2 * groups])
     query_load.start()
-    for copy in small + loads[0] + loads[1]:
+    for copy in small:
         copy.wait()
 
     wide = (channels, channels * modes)
@@ -73,7 +73,7 @@
         return jnp.sum(jnp.where(own_mode, spread_table, 0.0), axis=0, keepdims=True)
 
     rate_row = lanes_of(rates_ref[...])
-    gain_row = lanes_of(residues_ref[...]) * jnp.sqrt(one_minus_exp(2.0 * rate_row))
+    weight_row = lanes_of(residues_ref[...])
     own = iota((HALF, BLOCK), 1) // modes == iota((HALF, BLOCK), 0)
     same = iota((channels, channels), 0) == iota((channels, channels), 1)
     skip = jnp.sum(jnp.where(same, skip_row[...], 0.0), axis=1, keepdims=True)
@@ -83,7 +83,7 @@
         rate = rate_row[:, lanes]
         here = slice(g, g + 1)
         rate_ref[here, :] = rate
-        gain_ref[here, :] = gain_row[:, lanes]
+        weight_ref[here, :] = weight_row[:, lanes]
         to_end = (BLOCK - 1 - iota((BLOCK, BLOCK), 0)).astype(F32)
         fade_high, fade_low = split(jnp.exp(-rate * to_end))
         fades = jnp.concatenate([fade_high, fade_high, fade_low], axis=0)
@@ -91,6 +91,8 @@
         block_fade = jnp.exp(-rate * later)
         rows = slice(g * HALF, (g + 1) * HALF)
         total = jnp.zeros((HALF, BLOCK), F32)
+        for copy in loads[g]:
+            copy.wait()
         for start in range(0, blocks, 16):
             mixed = jnp.concatenate(
                 [
@@ -140,7 +142,7 @@
                 target[j, part * groups + g : part * groups + g + 1, :] = table[j : j + 1, :]
 
 
-def local_kernel(g, modes, side, length, mixed_ref, state_ref, skip_ref, rate_ref, gain_ref, base_ref, enter_ref, *rest):
+def local_kernel(g, modes, side, length, mixed_ref, state_ref, skip_ref, rate_ref, weight_ref, base_ref, enter_ref, lead_ref, fade_ref, *rest):
     conv_rows = rest[-1]
     if rest[:-1]:
         weight_tables(side, length, rate_ref, *rest[:-1])
@@ -148,7 +150,11 @@
     square = (BLOCK, BLOCK)
     own = iota((HALF, BLOCK), 1) // modes == iota((HALF, BLOCK), 0)
     causal = iota(square, 1) >= iota(square, 0)
-    rate, gain = rate_ref[g : g + 1, :], gain_ref[g : g + 1, :]
+    rate = rate_ref[g : g + 1, :]
+    gain = weight_ref[g : g + 1, :] * jnp.sqrt(one_minus_exp(2.0 * rate))
+    lead_high, lead_low = split(gain * jnp.exp(-rate * (iota(square, 0).astype(F32) + 1.0)))
+    lead_ref[...] = jnp.concatenate([lead_high, lead_high, lead_low], axis=1)
+    fade_ref[...] = jnp.exp(-rate * (BLOCK * iota((blocks, BLOCK), 0)).astype(F32))
     tail = gain * jnp.exp(-rate * iota(square, 0).astype(F32))
     taps = lax.dot_general(
         own.astype(F32), tail, NT, precision=lax.Precision.HIGHEST, preferred_element_type=F32
@@ -174,25 +180,21 @@
 
 
 def output_kernel(
-    modes, query_ref, rate_ref, gain_ref, far_ref, near_ref, carried_ref, *rest
+    modes, query_ref, far_ref, near_ref, carried_ref, *rest
 ):
-    groups = rate_ref.shape[0]
-    bases, enters = rest[:groups], rest[groups : 2 * groups]
-    out_hbm, out_ref, sems = rest[2 * groups :]
+    groups = far_ref.shape[0]
+    bases, enters, lead_refs, fade_refs = (rest[i * groups : (i + 1) * groups] for i in range(4))
+    out_hbm, out_ref, sems = rest[4 * groups :]
     channels, length = query_ref.shape
     blocks = length // BLOCK
     own = iota((HALF, BLOCK), 1) // modes == iota((HALF, BLOCK), 0)
-    square = (BLOCK, BLOCK)
     stores = []
     for g in range(groups):
         rows = slice(g * HALF, (g + 1) * HALF)
         here = slice(g, g + 1)
-        rate, gain = rate_ref[here, :], gain_ref[here, :]
-        after = iota(square, 0).astype(F32) + 1.0
-        lead_high, lead_low = split(gain * jnp.exp(-rate * after))
-        leads = jnp.concatenate([lead_high, lead_high, lead_low], axis=1)
+        leads = lead_refs[g][...]
         entered = near_ref[here, :] + far_ref[here, :] * carried_ref[here, :]
-        fades = entered * jnp.exp(-rate * (BLOCK * iota((blocks, BLOCK), 0)).astype(F32))
+        fades = entered * fade_refs[g][...]
         for start in range(0, blocks, 16):
             some = slice(start * HALF, (start + 16) * HALF)
             added = jnp.concatenate(
@@ -229,7 +231,7 @@
     groups = channels // HALF
     line = (groups, BLOCK)
     stripes = (groups, blocks * HALF, BLOCK)
-    ends, rate, gain, skip, mixed, state, query = pl.pallas_call(
+    ends, rate, weight, skip, mixed, state, query = pl.pallas_call(
         state_kernel,
         out_shape=(
             shape(*line), shape(*line), shape(*line),
@@ -263,13 +265,19 @@
     def local(g, more=()):
         return pl.pallas_call(
             lambda *refs: local_kernel(g, modes, SIDE, length, *refs),
-            out_shape=(shape(*stripes[1:]), shape(*stripes[1:]), *more),
+            out_shape=(
+                shape(*stripes[1:]),
+                shape(*stripes[1:]),
+                jax.ShapeDtypeStruct((BLOCK, 3 * BLOCK), BF16),
+                shape(blocks, BLOCK),
+                *more,
+            ),
             in_specs=[VMEM] * 5,
-            out_specs=(VMEM,) * (2 + len(more)),
+            out_specs=(VMEM,) * (4 + len(more)),
             scratch_shapes=[pltpu.VMEM(stripes[1:], F32)],
             compiler_params=pltpu.CompilerParams(vmem_limit_bytes=16 * 2**20),
             cost_estimate=pl.CostEstimate(flops=2 * 4 * 512 * 128 * 128, bytes_accessed=2**19, transcendentals=2**14),
-        )(mixed, state, skip, rate, gain)
+        )(mixed, state, skip, rate, weight)
 
     parts = lax.axis_size("chan")
     inner = [[d * parts + part for d in range(SIDE, 3 * SIDE)] for part in range(parts)]
@@ -280,7 +288,7 @@
     ]
     handed = lax.ppermute(ends, "ctx", [(x, SIDE + x) for x in range(SIDE)])
     handed, local_first, local_second = lax.optimization_barrier((handed, local(0, tables), local(1)))
-    far, enter, leave = local_first[2:]
+    far, enter, leave = local_first[4:]
     own = jnp.concatenate([ends, handed], axis=0).reshape(1, 1, -1)
     every = lax.all_to_all(
         jnp.broadcast_to(own, (2 * SIDE, 1, own.size)),
@@ -298,12 +306,12 @@
     return pl.pallas_call(
         lambda *refs: output_kernel(modes, *refs),
         out_shape=shape(channels, length),
-        in_specs=[VMEM] * (6 + 2 * groups),
+        in_specs=[VMEM] * (4 + 4 * groups),
         out_specs=HBM,
         scratch_shapes=[pltpu.VMEM((channels, length), F32), pltpu.SemaphoreType.DMA((groups * blocks // 16,))],
         compiler_params=pltpu.CompilerParams(vmem_limit_bytes=16 * 2**20),
         cost_estimate=pl.CostEstimate(flops=2 * 3 * 1024 * 128 * 128, bytes_accessed=2**21, transcendentals=2**16),
-    )(query, rate, gain, far, near, carried, local_first[0], local_second[0], local_first[1], local_second[1])
+    )(query, far, near, carried, *(made[i] for i in range(4) for made in (local_first, local_second)))
 
 
 def solution(mesh):

time: 26.4 us -> 26.2 us (level)
  the two profiles are of different devices: /device:TPU:192 before, /device:TPU:224 now
where the time goes in v10:
time: 26.2 us; the launch traced here: 26 us
  blocking collectives  15.1 us (58%)
  Pallas kernels  4.56 us (17%)
  waiting for transfers between devices  4.28 us (16%)
  starting transfers between devices  1.94 us (7%)
    all_to_all x1, blocking collectives, per_device(): lax.all_to_all(jnp.broadcast_to(own, (2 * SIDE, 1, own.size)), ('ctx', 'c...  15.1 us
    ppermute x1, waiting for transfers between devices, per_device(): handed = lax.ppermute(ends, 'ctx', [(x, SIDE + x) for x in range(SIDE)])  4.28 us
    pallas_call x1, Pallas kernels, per_device(): pl.pallas_call(state_kernel, out_shape=(shape(*line), shape(*line), shape...  1.72 us
    pallas_call x2, Pallas kernels, local(): pl.pallas_call(lambda *refs: local_kernel(g, modes, SIDE, length, *refs),...  1.66 us
    ppermute x1, starting transfers between devices, per_device(): handed = lax.ppermute(ends, 'ctx', [(x, SIDE + x) for x in range(SIDE)])  1.29 us
    pallas_call x1, Pallas kernels, per_device(): pl.pallas_call(lambda *refs: output_kernel(modes, *refs), out_shape=shape...  1.18 us
    ppermute x1, starting transfers between devices, per_device(): lax.ppermute(sent, 'ctx', [(2 * SIDE + x, 3 * SIDE + x) for x in range(SI...  0.65 us
  transfers between devices with their start and end apart: 2, of which 1 were waited for; matrix products, arithmetic and copies ran while one was open for 0% of the time, Pallas kernels for 6%

profile of v10, /device:TPU:224, one launch (start us, length us, event | category | flops | bytes accessed | tf_op | source)
XLA Modules:
  0.0 26.0 jit_solution(4880859924271564175)
XLA Ops:
  0.0 1.7 %shard_map.73 = (f32[2,128]{1,0:T(2,128)S(1)}, f32[2,128]{1,0:T(2,128)S(1)}, f32[2,128]{1,0:T(2,128)S(1)}, f32[16,128]{1,0:T(8,128)S(1)}, f32[2,512,128]{2,1,0:T...) custom-call(s32[1,16]{1,0:T(1,128)} %bitcast.21, f32[16,48]{1,0:T(8,128)} %bitcast.19, ...), custom_call_target="tpu_custom_call" | custom-call | flops 100663296 | bytes 1048576 | tf_op jit(solution)/shard_map/pallas_call | solution.py:234
  1.7 1.3 %collective-permute-start = (f32[2,128]{1,0:T(2,128)S(1)}, f32[2,128]{1,0:T(2,128)S(1)}, u32[]{:S(2)}, u32[]{:S(2)}) collective-permute-start(f32[2,128]{1,0:T(2,128)S(1)} %get-tuple-element.36), channel_id=1, source_target_pairs={{0,192},{48,240},{96,288},{144,336},{1,193},{49,241},{97,289},{145... | collective-permute-start | bytes 3080 | tf_op jit(solution)/shard_map/ppermute | solution.py:289
  3.0 0.8 %shard_map.74 = (f32[512,128]{1,0:T(8,128)S(1)}, f32[512,128]{1,0:T(8,128)S(1)}, bf16[128,384]{1,0:T(8,128)(2,1)S(1)}, f32[64,128]{1,0:T(8,128)S(1)}, f32[2,128]...) custom-call(f32[2,512,128]{2,1,0:T(8,128)S(1)} %get-tuple-element.37.refs_0_, ...), custom_call_target="tpu_custom_call" | custom-call | flops 67108864 | bytes 524288 | tf_op jit(solution)/shard_map/pallas_call | solution.py:266
  3.9 0.8 %shard_map.75 = (f32[512,128]{1,0:T(8,128)S(1)}, f32[512,128]{1,0:T(8,128)S(1)}, bf16[128,384]{1,0:T(8,128)(2,1)S(1)}, f32[64,128]{1,0:T(8,128)S(1)}) custom-call(f32[2,512,128]{2,1,0:T(8,128)S(1)} %get-tuple-element.37.refs_0_, f32[2,512,128]{2,1,0:T(8,128)S(1)} %get-tuple-element.38.refs_1_, f32[16,128]{1,0:T(8,128)S(1)} %get-tuple-element.39.refs_2_, ...), custom_call_target="tpu_custom_call" | custom-call | flops 67108864 | bytes 524288 | tf_op jit(solution)/shard_map/pallas_call | solution.py:266
  4.7 4.3 %collective-permute-done = f32[2,128]{1,0:T(2,128)S(1)} collective-permute-done((f32[2,128]{1,0:T(2,128)S(1)}, f32[2,128]{1,0:T(2,128)S(1)}, u32[]{:S(2)}, u32[]{:S(2)}) %collective-permute-start) | collective-permute-done | bytes 1056 | tf_op jit(solution)/shard_map/ppermute | solution.py:289
  9.0 15.1 %all_to_all.5 = f32[8,1,512]{2,1,0:T(1,128)S(1)} all-to-all(f32[8,1,512]{2,1,0:T(1,128)S(1)} %broadcast_in_dim.8), channel_id=1, replica_groups={{192,240,288,336,384,432,480,528},{193,241,289,337,385,433,481,529},{19..., dimensions={0} | all-to-all | bytes 32768 | tf_op jit(solution)/shard_map/all_to_all | solution.py:293
  24.1 0.7 %collective-permute-start.1 = (f32[2,128]{1,0:T(2,128)S(1)}, f32[2,128]{1,0:T(2,128)S(1)}, u32[]{:S(2)}, u32[]{:S(2)}) collective-permute-start(f32[2,128]{1,0:T(2,128)S(1)} %reduce_sum.19), channel_id=1, source_target_pairs={{384,576},{432,624},{480,672},{528,720},{385,577},{433,625},{481,6... | collective-permute-start | bytes 3080 | tf_op jit(solution)/shard_map/ppermute | solution.py:304
  24.8 0.0 collective-permute-done.1.refs_3_
  24.8 1.2 %shard_map.76 = f32[16,8192]{1,0:T(8,128)} custom-call(f32[16,8192]{1,0:T(8,128)S(1)} %get-tuple-element.35.refs_0_, f32[2,128]{1,0:T(2,128)S(1)} %get-tuple-element.53.refs_1_, f32[2,128]{1,0:T(2,128)S(1)} %reduce_sum.18.refs_2_, f32[2,128]{1,0:T(2,128)S(1)} %collective-permute-done.1.refs_3_, f32[512,128]{1,0:T(8,128)S(1)} %get-tuple-element.57.refs_4_, ...), custom_call_target="tpu_custom_call" | custom-call | flops 100663296 | bytes 2097152 | tf_op jit(solution)/shard_map/pallas_call | solution.py:306
  (5 shorter events, 0.1 us)
Async XLA Ops:
  1.7 7.3 %collective-permute-start = (f32[2,128]{1,0:T(2,128)S(1)}, f32[2,128]{1,0:T(2,128)S(1)}, u32[]{:S(2)}, u32[]{:S(2)}) collective-permute-start(f32[2,128]{1,0:T(2,128)S(1)} %get-tuple-element.36), channel_id=1, source_target_pairs={{0,192},{48,240},{96,288},{144,336},{1,193},{49,241},{97,289},{145... | collective-permute-start | bytes 3080 | tf_op jit(solution)/shard_map/ppermute | solution.py:289
  24.1 0.7 %collective-permute-start.1 = (f32[2,128]{1,0:T(2,128)S(1)}, f32[2,128]{1,0:T(2,128)S(1)}, u32[]{:S(2)}, u32[]{:S(2)}) collective-permute-start(f32[2,128]{1,0:T(2,128)S(1)} %reduce_sum.19), channel_id=1, source_target_pairs={{384,576},{432,624},{480,672},{528,720},{385,577},{433,625},{481,6... | collective-permute-start | bytes 3080 | tf_op jit(solution)/shard_map/ppermute | solution.py:304

commit v11 on v10

--- a/solution.py
+++ b/solution.py
@@ -289,16 +289,8 @@
     handed = lax.ppermute(ends, "ctx", [(x, SIDE + x) for x in range(SIDE)])
     handed, local_first, local_second = lax.optimization_barrier((handed, local(0, tables), local(1)))
     far, enter, leave = local_first[4:]
-    own = jnp.concatenate([ends, handed], axis=0).reshape(1, 1, -1)
-    every = lax.all_to_all(
-        jnp.broadcast_to(own, (2 * SIDE, 1, own.size)),
-        ("ctx", "chan"),
-        split_axis=0,
-        concat_axis=0,
-        tiled=True,
-        axis_index_groups=inner + outer,
-    )
-    every = every.reshape(2 * SIDE, 2 * groups, BLOCK)
+    own = jnp.concatenate([ends, handed], axis=0)
+    every = lax.all_gather(own, ("ctx", "chan"), axis_index_groups=inner + outer)
     near = jnp.sum((enter * every).reshape(4 * SIDE, *line), axis=0)
     sent = jnp.sum((leave * every).reshape(4 * SIDE, *line), axis=0)
     carried = lax.ppermute(sent, "ctx", [(2 * SIDE + x, 3 * SIDE + x) for x in range(SIDE)])

time: 26.2 us -> 49.1 us (1.87)
  the two profiles are of different devices: /device:TPU:224 before, /device:TPU:192 now
where the time goes in v11:
time: 49.1 us; the launch traced here: 49 us
  blocking collectives  35.7 us (73%)
  waiting for transfers between devices  6.69 us (14%)
  Pallas kernels  4.55 us (9%)
  starting transfers between devices  1.95 us (4%)
    all_gather x1, blocking collectives, per_device(): lax.all_gather(own, ('ctx', 'chan'), axis_index_groups=inner + outer)  35.7 us
    ppermute x1, waiting for transfers between devices, per_device(): handed = lax.ppermute(ends, 'ctx', [(x, SIDE + x) for x in range(SIDE)])  6.69 us
    pallas_call x1, Pallas kernels, per_device(): pl.pallas_call(state_kernel, out_shape=(shape(*line), shape(*line), shape...  1.72 us
    pallas_call x2, Pallas kernels, local(): pl.pallas_call(lambda *refs: local_kernel(g, modes, SIDE, length, *refs),...  1.66 us
    ppermute x1, starting transfers between devices, per_device(): handed = lax.ppermute(ends, 'ctx', [(x, SIDE + x) for x in range(SIDE)])  1.29 us
    pallas_call x1, Pallas kernels, per_device(): pl.pallas_call(lambda *refs: output_kernel(modes, *refs), out_shape=shape...  1.17 us
  transfers between devices with their start and end apart: 2, of which 1 were waited for; matrix products, arithmetic and copies ran while one was open for 0% of the time, Pallas kernels for 3%

profile of v11, /device:TPU:192, one launch (start us, length us, event | category | flops | bytes accessed | tf_op | source)
XLA Modules:
  0.0 49.0 jit_solution(11492438422336410020)
XLA Ops:
  0.0 1.7 %shard_map.73 = (f32[2,128]{1,0:T(2,128)S(1)}, f32[2,128]{1,0:T(2,128)S(1)}, f32[2,128]{1,0:T(2,128)S(1)}, f32[16,128]{1,0:T(8,128)S(1)}, f32[2,512,128]{2,1,0:T...) custom-call(s32[1,16]{1,0:T(1,128)} %bitcast.20, f32[16,48]{1,0:T(8,128)} %bitcast.18, ...), custom_call_target="tpu_custom_call" | custom-call | flops 100663296 | bytes 1048576 | tf_op jit(solution)/shard_map/pallas_call | solution.py:234
  1.7 1.3 %collective-permute-start = (f32[2,128]{1,0:T(2,128)S(1)}, f32[2,128]{1,0:T(2,128)S(1)}, u32[]{:S(2)}, u32[]{:S(2)}) collective-permute-start(f32[2,128]{1,0:T(2,128)S(1)} %get-tuple-element.36), channel_id=1, source_target_pairs={{0,192},{48,240},{96,288},{144,336},{1,193},{49,241},{97,289},{145... | collective-permute-start | bytes 3080 | tf_op jit(solution)/shard_map/ppermute | solution.py:289
  3.0 0.8 %shard_map.74 = (f32[512,128]{1,0:T(8,128)S(1)}, f32[512,128]{1,0:T(8,128)S(1)}, bf16[128,384]{1,0:T(8,128)(2,1)S(1)}, f32[64,128]{1,0:T(8,128)S(1)}, f32[2,128]...) custom-call(f32[2,512,128]{2,1,0:T(8,128)S(1)} %get-tuple-element.37.refs_0_, ...), custom_call_target="tpu_custom_call" | custom-call | flops 67108864 | bytes 524288 | tf_op jit(solution)/shard_map/pallas_call | solution.py:266
  3.9 0.8 %shard_map.75 = (f32[512,128]{1,0:T(8,128)S(1)}, f32[512,128]{1,0:T(8,128)S(1)}, bf16[128,384]{1,0:T(8,128)(2,1)S(1)}, f32[64,128]{1,0:T(8,128)S(1)}) custom-call(f32[2,512,128]{2,1,0:T(8,128)S(1)} %get-tuple-element.37.refs_0_, f32[2,512,128]{2,1,0:T(8,128)S(1)} %get-tuple-element.38.refs_1_, f32[16,128]{1,0:T(8,128)S(1)} %get-tuple-element.39.refs_2_, ...), custom_call_target="tpu_custom_call" | custom-call | flops 67108864 | bytes 524288 | tf_op jit(solution)/shard_map/pallas_call | solution.py:266
  4.7 6.7 %collective-permute-done = f32[2,128]{1,0:T(2,128)S(1)} collective-permute-done((f32[2,128]{1,0:T(2,128)S(1)}, f32[2,128]{1,0:T(2,128)S(1)}, u32[]{:S(2)}, u32[]{:S(2)}) %collective-permute-start) | collective-permute-done | bytes 1056 | tf_op jit(solution)/shard_map/ppermute | solution.py:289
  11.4 35.7 %all-gather.1 = f32[8,4,128]{2,1,0:T(4,128)S(1)} all-gather(f32[1,4,128]{2,1,0:T(4,128)S(1)} %maximum_bitcast_fusion), channel_id=2, replica_groups={{192,240,288,336,384,432,480,528},{193,241,289,337,385,433,481,529},{19..., dimensions={0}, use_global_device_ids=true | all-gather | bytes 18432 | tf_op jit(solution)/shard_map/all_gather | solution.py:293
  47.1 0.7 %collective-permute-start.1 = (f32[2,128]{1,0:T(2,128)S(1)}, f32[2,128]{1,0:T(2,128)S(1)}, u32[]{:S(2)}, u32[]{:S(2)}) collective-permute-start(f32[2,128]{1,0:T(2,128)S(1)} %reduce_sum.19), channel_id=1, source_target_pairs={{384,576},{432,624},{480,672},{528,720},{385,577},{433,625},{481,6... | collective-permute-start | bytes 3080 | tf_op jit(solution)/shard_map/ppermute | solution.py:296
  47.8 0.0 collective-permute-done.1.refs_3_
  47.8 1.2 %shard_map.76 = f32[16,8192]{1,0:T(8,128)} custom-call(f32[16,8192]{1,0:T(8,128)S(1)} %get-tuple-element.35.refs_0_, f32[2,128]{1,0:T(2,128)S(1)} %get-tuple-element.53.refs_1_, f32[2,128]{1,0:T(2,128)S(1)} %reduce_sum.18.refs_2_, f32[2,128]{1,0:T(2,128)S(1)} %collective-permute-done.1.refs_3_, f32[512,128]{1,0:T(8,128)S(1)} %get-tuple-element.57.refs_4_, ...), custom_call_target="tpu_custom_call" | custom-call | flops 100663296 | bytes 2097152 | tf_op jit(solution)/shard_map/pallas_call | solution.py:298
  (4 shorter events, 0.1 us)
Async XLA Ops:
  1.7 9.7 %collective-permute-start = (f32[2,128]{1,0:T(2,128)S(1)}, f32[2,128]{1,0:T(2,128)S(1)}, u32[]{:S(2)}, u32[]{:S(2)}) collective-permute-start(f32[2,128]{1,0:T(2,128)S(1)} %get-tuple-element.36), channel_id=1, source_target_pairs={{0,192},{48,240},{96,288},{144,336},{1,193},{49,241},{97,289},{145... | collective-permute-start | bytes 3080 | tf_op jit(solution)/shard_map/ppermute | solution.py:289
  47.1 0.7 %collective-permute-start.1 = (f32[2,128]{1,0:T(2,128)S(1)}, f32[2,128]{1,0:T(2,128)S(1)}, u32[]{:S(2)}, u32[]{:S(2)}) collective-permute-start(f32[2,128]{1,0:T(2,128)S(1)} %reduce_sum.19), channel_id=1, source_target_pairs={{384,576},{432,624},{480,672},{528,720},{385,577},{433,625},{481,6... | collective-permute-start | bytes 3080 | tf_op jit(solution)/shard_map/ppermute | solution.py:296

commit v12 on v10

--- a/solution.py
+++ b/solution.py
@@ -29,8 +29,8 @@
 
 
 def state_kernel(
-    index_hbm, rates_hbm, residues_hbm, skip_hbm, key_hbm, value_hbm, query_hbm,
-    end_ref, rate_ref, weight_ref, skip_ref, mixed_ref, state_ref, query_ref,
+    index_hbm, rates_hbm, residues_hbm, skip_hbm, key_hbm, value_hbm,
+    end_ref, rate_ref, weight_ref, skip_ref, mixed_ref, state_ref,
     index_ref, rates_ref, residues_ref, skip_row, key_ref, value_ref, sems,
 ):
     channels, length = key_ref.shape
@@ -38,7 +38,7 @@
     blocks = length // BLOCK
     groups = channels // HALF
     small = [
-        pltpu.make_async_copy(source, target, sems.at[2 * groups + 1 + i])
+        pltpu.make_async_copy(source, target, sems.at[2 * groups + i])
         for i, (source, target) in enumerate(
             ((index_hbm, index_ref), (rates_hbm, rates_ref), (residues_hbm, residues_ref), (skip_hbm, skip_row))
         )
@@ -55,8 +55,6 @@
         for copy in pair:
             copy.start()
         loads.append(pair)
-    query_load = pltpu.make_async_copy(query_hbm, query_ref, sems.at[2 * groups])
-    query_load.start()
     for copy in small:
         copy.wait()
 
@@ -110,7 +108,6 @@
             for b in range(16):
                 total = total + block_fade[start + b : start + b + 1, :] * states[b * HALF : (b + 1) * HALF, :]
         end_ref[here, :] = jnp.sum(jnp.where(own, total, 0.0), axis=0, keepdims=True)
-    query_load.wait()
 
 
 def weight_tables(side, length, rate_ref, far_ref, enter_ref, leave_ref):
@@ -179,6 +176,14 @@
         base_ref[some, :] = conv_rows[some, :] + skip * mixed_ref[g, some, :]
 
 
+def opening_kernel(modes, side, length, *refs):
+    query_hbm, query_ref, sem = refs[5], refs[13], refs[15]
+    load = pltpu.make_async_copy(query_hbm, query_ref, sem)
+    load.start()
+    local_kernel(0, modes, side, length, *refs[:5], *refs[6:13], refs[14])
+    load.wait()
+
+
 def output_kernel(
     modes, query_ref, far_ref, near_ref, carried_ref, *rest
 ):
@@ -231,14 +236,14 @@
     groups = channels // HALF
     line = (groups, BLOCK)
     stripes = (groups, blocks * HALF, BLOCK)
-    ends, rate, weight, skip, mixed, state, query = pl.pallas_call(
+    ends, rate, weight, skip, mixed, state = pl.pallas_call(
         state_kernel,
         out_shape=(
             shape(*line), shape(*line), shape(*line),
-            shape(channels, BLOCK), shape(*stripes), shape(*stripes), shape(channels, length),
+            shape(channels, BLOCK), shape(*stripes), shape(*stripes),
         ),
-        in_specs=[HBM] * 7,
-        out_specs=(VMEM,) * 7,
+        in_specs=[HBM] * 6,
+        out_specs=(VMEM,) * 6,
         scratch_shapes=[
             pltpu.VMEM((1, channels), jnp.int32),
             pltpu.VMEM((modes, residues.shape[0]), F32),
@@ -246,7 +251,7 @@
             pltpu.VMEM((1, channels), F32),
             pltpu.VMEM((channels, length), F32),
             pltpu.VMEM((channels, length), F32),
-            pltpu.SemaphoreType.DMA((2 * groups + 5,)),
+            pltpu.SemaphoreType.DMA((2 * groups + 4,)),
         ],
         compiler_params=pltpu.CompilerParams(vmem_limit_bytes=16 * 2**20),
         cost_estimate=pl.CostEstimate(flops=2 * 3 * 1024 * 128 * 128, bytes_accessed=2**20, transcendentals=2**16),
@@ -255,16 +260,19 @@
             pltpu.with_memory_space_constraint(array, pltpu.HBM)
             for array in (
                 filter_index.reshape(1, channels), decay_rates.T, residues.T, skip_gain.reshape(1, channels),
-                key_gate, value_rows, query_gate,
+                key_gate, value_rows,
             )
         )
     )
 
-    tables = (shape(*line), shape(2 * SIDE, 2 * groups, BLOCK), shape(2 * SIDE, 2 * groups, BLOCK))
+    weights = shape(2 * SIDE, 2 * groups, BLOCK)
+    opening = (shape(*line), weights, weights, shape(channels, length))
+    query_here = pltpu.with_memory_space_constraint(query_gate, pltpu.HBM)
 
     def local(g, more=()):
+        kernel = opening_kernel if more else lambda *refs: local_kernel(g, *refs)
         return pl.pallas_call(
-            lambda *refs: local_kernel(g, modes, SIDE, length, *refs),
+            lambda *refs: kernel(modes, SIDE, length, *refs),
             out_shape=(
                 shape(*stripes[1:]),
                 shape(*stripes[1:]),
@@ -272,12 +280,12 @@
                 shape(blocks, BLOCK),
                 *more,
             ),
-            in_specs=[VMEM] * 5,
+            in_specs=[VMEM] * 5 + [HBM] * bool(more),
             out_specs=(VMEM,) * (4 + len(more)),
-            scratch_shapes=[pltpu.VMEM(stripes[1:], F32)],
+            scratch_shapes=[pltpu.VMEM(stripes[1:], F32)] + [pltpu.SemaphoreType.DMA] * bool(more),
             compiler_params=pltpu.CompilerParams(vmem_limit_bytes=16 * 2**20),
             cost_estimate=pl.CostEstimate(flops=2 * 4 * 512 * 128 * 128, bytes_accessed=2**19, transcendentals=2**14),
-        )(mixed, state, skip, rate, weight)
+        )(mixed, state, skip, rate, weight, *((query_here,) if more else ()))
 
     parts = lax.axis_size("chan")
     inner = [[d * parts + part for d in range(SIDE, 3 * SIDE)] for part in range(parts)]
@@ -287,8 +295,8 @@
         for pair in range(0, parts, 2)
     ]
     handed = lax.ppermute(ends, "ctx", [(x, SIDE + x) for x in range(SIDE)])
-    handed, local_first, local_second = lax.optimization_barrier((handed, local(0, tables), local(1)))
-    far, enter, leave = local_first[4:]
+    handed, local_first, local_second = lax.optimization_barrier((handed, local(0, opening), local(1)))
+    far, enter, leave, query = local_first[4:]
     own = jnp.concatenate([ends, handed], axis=0).reshape(1, 1, -1)
     every = lax.all_to_all(
         jnp.broadcast_to(own, (2 * SIDE, 1, own.size)),

time: 26.2 us -> 26.9 us (1.027)
  blocking collectives: 15.1 us -> 15.8 us
  waiting for transfers between devices: 4.28 us -> 3.59 us
  Pallas kernels: 4.56 us -> 5.24 us
    ppermute x1, waiting for transfers between devices: 4.28 us -> 3.59 us  [per_device(): handed = lax.ppermute(ends, 'ctx', [(x, SIDE + x) for x in range(SIDE)])]
    pallas_call x2, Pallas kernels: 1.66 us -> 2.35 us  [local(): pl.pallas_call(lambda *refs: kernel(modes, SIDE, length, *refs), out_shap...]
    all_to_all x1, blocking collectives: 15.1 us -> 15.8 us  [per_device(): lax.all_to_all(jnp.broadcast_to(own, (2 * SIDE, 1, own.size)), ('ctx', 'c...]
  transfers between devices with their start and end apart: 2 -> 2, of which waited for: 1 -> 1; matrix products, arithmetic and copies ran while one was open for 0% -> 0% of each run, Pallas kernels for 6% -> 9%
where the time goes in v12:
time: 26.9 us; the launch traced here: 26.7 us
  blocking collectives  15.8 us (59%)
  Pallas kernels  5.24 us (19%)
  waiting for transfers between devices  3.59 us (13%)
  starting transfers between devices  1.94 us (7%)
    all_to_all x1, blocking collectives, per_device(): lax.all_to_all(jnp.broadcast_to(own, (2 * SIDE, 1, own.size)), ('ctx', 'c...  15.8 us
    ppermute x1, waiting for transfers between devices, per_device(): handed = lax.ppermute(ends, 'ctx', [(x, SIDE + x) for x in range(SIDE)])  3.59 us
    pallas_call x2, Pallas kernels, local(): pl.pallas_call(lambda *refs: kernel(modes, SIDE, length, *refs), out_shap...  2.35 us
    pallas_call x1, Pallas kernels, per_device(): pl.pallas_call(state_kernel, out_shape=(shape(*line), shape(*line), shape...  1.71 us
    ppermute x1, starting transfers between devices, per_device(): handed = lax.ppermute(ends, 'ctx', [(x, SIDE + x) for x in range(SIDE)])  1.29 us
    pallas_call x1, Pallas kernels, per_device(): pl.pallas_call(lambda *refs: output_kernel(modes, *refs), out_shape=shape...  1.18 us
    ppermute x1, starting transfers between devices, per_device(): lax.ppermute(sent, 'ctx', [(2 * SIDE + x, 3 * SIDE + x) for x in range(SI...  0.65 us
  transfers between devices with their start and end apart: 2, of which 1 were waited for; matrix products, arithmetic and copies ran while one was open for 0% of the time, Pallas kernels for 9%

profile of v12, /device:TPU:224, one launch (start us, length us, event | category | flops | bytes accessed | tf_op | source)
XLA Modules:
  0.0 26.7 jit_solution(4675006650237907964)
XLA Ops:
  0.0 1.7 %shard_map.73 = (f32[2,128]{1,0:T(2,128)S(1)}, f32[2,128]{1,0:T(2,128)S(1)}, f32[2,128]{1,0:T(2,128)S(1)}, f32[16,128]{1,0:T(8,128)S(1)}, f32[2,512,128]{2,1,0:T(8,128)S(1)}, /*index=5*/f32[2,512,128]{2,1,0:T(8,128)S(1)}) custom-call(s32[1,16]{1,0:T(1,128)} %bitcast.21, f32[16,48]{1,0:T(8,128)} %bitcast.19, f32[16,48]{1,0:T(8,128)} %bitcast.20, ...), custom_call_target="tpu_custom_call" | custom-call | flops 100663296 | bytes 1048576 | tf_op jit(solution)/shard_map/pallas_call | solution.py:239
  1.7 1.3 %collective-permute-start = (f32[2,128]{1,0:T(2,128)S(1)}, f32[2,128]{1,0:T(2,128)S(1)}, u32[]{:S(2)}, u32[]{:S(2)}) collective-permute-start(f32[2,128]{1,0:T(2,128)S(1)} %get-tuple-element.36), channel_id=1, source_target_pairs={{0,192},{48,240},{96,288},{144,336},{1,193},{49,241},{97,289},{145... | collective-permute-start | bytes 3080 | tf_op jit(solution)/shard_map/ppermute | solution.py:297
  3.0 0.8 %shard_map.75 = (f32[512,128]{1,0:T(8,128)S(1)}, f32[512,128]{1,0:T(8,128)S(1)}, bf16[128,384]{1,0:T(8,128)(2,1)S(1)}, f32[64,128]{1,0:T(8,128)S(1)}) custom-call(f32[2,512,128]{2,1,0:T(8,128)S(1)} %get-tuple-element.37.refs_0_, f32[2,512,128]{2,1,0:T(8,128)S(1)} %get-tuple-element.38.refs_1_, f32[16,128]{1,0:T(8,128)S(1)} %get-tuple-element.39.refs_2_, ...), custom_call_target="tpu_custom_call" | custom-call | flops 67108864 | bytes 524288 | tf_op jit(solution)/shard_map/pallas_call | solution.py:274
  3.9 1.5 %shard_map.74 = (f32[512,128]{1,0:T(8,128)S(1)}, f32[512,128]{1,0:T(8,128)S(1)}, bf16[128,384]{1,0:T(8,128)(2,1)S(1)}, f32[64,128]{1,0:T(8,128)S(1)}, f32[2,128]...) custom-call(f32[2,512,128]{2,1,0:T(8,128)S(1)} %get-tuple-element.37.refs_0_, ...), custom_call_target="tpu_custom_call" | custom-call | flops 67108864 | bytes 524288 | tf_op jit(solution)/shard_map/pallas_call | solution.py:274
  5.4 3.6 %collective-permute-done = f32[2,128]{1,0:T(2,128)S(1)} collective-permute-done((f32[2,128]{1,0:T(2,128)S(1)}, f32[2,128]{1,0:T(2,128)S(1)}, u32[]{:S(2)}, u32[]{:S(2)}) %collective-permute-start) | collective-permute-done | bytes 1056 | tf_op jit(solution)/shard_map/ppermute | solution.py:297
  9.0 15.8 %all_to_all.5 = f32[8,1,512]{2,1,0:T(1,128)S(1)} all-to-all(f32[8,1,512]{2,1,0:T(1,128)S(1)} %broadcast_in_dim.8), channel_id=1, replica_groups={{192,240,288,336,384,432,480,528},{193,241,289,337,385,433,481,529},{19..., dimensions={0} | all-to-all | bytes 32768 | tf_op jit(solution)/shard_map/all_to_all | solution.py:301
  24.8 0.7 %collective-permute-start.1 = (f32[2,128]{1,0:T(2,128)S(1)}, f32[2,128]{1,0:T(2,128)S(1)}, u32[]{:S(2)}, u32[]{:S(2)}) collective-permute-start(f32[2,128]{1,0:T(2,128)S(1)} %reduce_sum.19), channel_id=1, source_target_pairs={{384,576},{432,624},{480,672},{528,720},{385,577},{433,625},{481,6... | collective-permute-start | bytes 3080 | tf_op jit(solution)/shard_map/ppermute | solution.py:312
  25.5 0.0 collective-permute-done.1.refs_3_
  25.5 1.2 %shard_map.76 = f32[16,8192]{1,0:T(8,128)} custom-call(f32[16,8192]{1,0:T(8,128)S(1)} %get-tuple-element.54.refs_0_, f32[2,128]{1,0:T(2,128)S(1)} %get-tuple-element.55.refs_1_, f32[2,128]{1,0:T(2,128)S(1)} %reduce_sum.18.refs_2_, f32[2,128]{1,0:T(2,128)S(1)} %collective-permute-done.1.refs_3_, f32[512,128]{1,0:T(8,128)S(1)} %get-tuple-element.59.refs_4_, ...), custom_call_target="tpu_custom_call" | custom-call | flops 100663296 | bytes 2097152 | tf_op jit(solution)/shard_map/pallas_call | solution.py:314
  (5 shorter events, 0.1 us)
Async XLA Ops:
  1.7 7.3 %collective-permute-start = (f32[2,128]{1,0:T(2,128)S(1)}, f32[2,128]{1,0:T(2,128)S(1)}, u32[]{:S(2)}, u32[]{:S(2)}) collective-permute-start(f32[2,128]{1,0:T(2,128)S(1)} %get-tuple-element.36), channel_id=1, source_target_pairs={{0,192},{48,240},{96,288},{144,336},{1,193},{49,241},{97,289},{145... | collective-permute-start | bytes 3080 | tf_op jit(solution)/shard_map/ppermute | solution.py:297
  24.8 0.7 %collective-permute-start.1 = (f32[2,128]{1,0:T(2,128)S(1)}, f32[2,128]{1,0:T(2,128)S(1)}, u32[]{:S(2)}, u32[]{:S(2)}) collective-permute-start(f32[2,128]{1,0:T(2,128)S(1)} %reduce_sum.19), channel_id=1, source_target_pairs={{384,576},{432,624},{480,672},{528,720},{385,577},{433,625},{481,6... | collective-permute-start | bytes 3080 | tf_op jit(solution)/shard_map/ppermute | solution.py:312

commit v13 on v10

--- a/solution.py
+++ b/solution.py
@@ -195,19 +195,19 @@
         leads = lead_refs[g][...]
         entered = near_ref[here, :] + far_ref[here, :] * carried_ref[here, :]
         fades = entered * fade_refs[g][...]
-        for start in range(0, blocks, 16):
-            some = slice(start * HALF, (start + 16) * HALF)
+        for start in range(0, blocks, 8):
+            some = slice(start * HALF, (start + 8) * HALF)
             added = jnp.concatenate(
-                [jnp.where(own, fades[b : b + 1, :], 0.0) for b in range(start, start + 16)], axis=0
+                [jnp.where(own, fades[b : b + 1, :], 0.0) for b in range(start, start + 8)], axis=0
             )
             high, low = split(enters[g][some, :] + added)
             conv = bases[g][some, :] + lax.dot_general(
                 jnp.concatenate([high, low, high], axis=1), leads, NT, preferred_element_type=F32
             )
-            for b in range(16):
+            for b in range(8):
                 lanes = slice((start + b) * BLOCK, (start + b + 1) * BLOCK)
                 out_ref[rows, lanes] = query_ref[rows, lanes] * conv[b * HALF : (b + 1) * HALF, :]
-            lanes = slice(start * BLOCK, (start + 16) * BLOCK)
+            lanes = slice(start * BLOCK, (start + 8) * BLOCK)
             store = pltpu.make_async_copy(out_ref.at[rows, lanes], out_hbm.at[rows, lanes], sems.at[len(stores)])
             store.start()
             stores.append(store)
@@ -308,7 +308,7 @@
         out_shape=shape(channels, length),
         in_specs=[VMEM] * (4 + 4 * groups),
         out_specs=HBM,
-        scratch_shapes=[pltpu.VMEM((channels, length), F32), pltpu.SemaphoreType.DMA((groups * blocks // 16,))],
+        scratch_shapes=[pltpu.VMEM((channels, length), F32), pltpu.SemaphoreType.DMA((groups * blocks // 8,))],
         compiler_params=pltpu.CompilerParams(vmem_limit_bytes=16 * 2**20),
         cost_estimate=pl.CostEstimate(flops=2 * 3 * 1024 * 128 * 128, bytes_accessed=2**21, transcendentals=2**16),
     )(query, far, near, carried, *(made[i] for i in range(4) for made in (local_first, local_second)))

time: 26.2 us -> 26.6 us (1.015)
  the two profiles are of different devices: /device:TPU:224 before, /device:TPU:240 now
where the time goes in v13:
time: 26.6 us; the launch traced here: 26.4 us
  blocking collectives  15.1 us (57%)
  Pallas kernels  4.95 us (19%)
  waiting for transfers between devices  4.28 us (16%)
  starting transfers between devices  1.94 us (7%)
    all_to_all x1, blocking collectives, per_device(): lax.all_to_all(jnp.broadcast_to(own, (2 * SIDE, 1, own.size)), ('ctx', 'c...  15.1 us
    ppermute x1, waiting for transfers between devices, per_device(): handed = lax.ppermute(ends, 'ctx', [(x, SIDE + x) for x in range(SIDE)])  4.28 us
    pallas_call x1, Pallas kernels, per_device(): pl.pallas_call(state_kernel, out_shape=(shape(*line), shape(*line), shape...  1.71 us
    pallas_call x2, Pallas kernels, local(): pl.pallas_call(lambda *refs: local_kernel(g, modes, SIDE, length, *refs),...  1.66 us
    pallas_call x1, Pallas kernels, per_device(): pl.pallas_call(lambda *refs: output_kernel(modes, *refs), out_shape=shape...  1.58 us
    ppermute x1, starting transfers between devices, per_device(): handed = lax.ppermute(ends, 'ctx', [(x, SIDE + x) for x in range(SIDE)])  1.29 us
    ppermute x1, starting transfers between devices, per_device(): lax.ppermute(sent, 'ctx', [(2 * SIDE + x, 3 * SIDE + x) for x in range(SI...  0.65 us
  transfers between devices with their start and end apart: 2, of which 1 were waited for; matrix products, arithmetic and copies ran while one was open for 0% of the time, Pallas kernels for 6%

profile of v13, /device:TPU:240, one launch (start us, length us, event | category | flops | bytes accessed | tf_op | source)
XLA Modules:
  0.0 26.4 jit_solution(1918814337587502745)
XLA Ops:
  0.0 1.7 %shard_map.73 = (f32[2,128]{1,0:T(2,128)S(1)}, f32[2,128]{1,0:T(2,128)S(1)}, f32[2,128]{1,0:T(2,128)S(1)}, f32[16,128]{1,0:T(8,128)S(1)}, f32[2,512,128]{2,1,0:T...) custom-call(s32[1,16]{1,0:T(1,128)} %bitcast.21, f32[16,48]{1,0:T(8,128)} %bitcast.19, ...), custom_call_target="tpu_custom_call" | custom-call | flops 100663296 | bytes 1048576 | tf_op jit(solution)/shard_map/pallas_call | solution.py:234
  1.7 1.3 %collective-permute-start = (f32[2,128]{1,0:T(2,128)S(1)}, f32[2,128]{1,0:T(2,128)S(1)}, u32[]{:S(2)}, u32[]{:S(2)}) collective-permute-start(f32[2,128]{1,0:T(2,128)S(1)} %get-tuple-element.36), channel_id=1, source_target_pairs={{0,192},{48,240},{96,288},{144,336},{1,193},{49,241},{97,289},{145... | collective-permute-start | bytes 3080 | tf_op jit(solution)/shard_map/ppermute | solution.py:289
  3.0 0.8 %shard_map.74 = (f32[512,128]{1,0:T(8,128)S(1)}, f32[512,128]{1,0:T(8,128)S(1)}, bf16[128,384]{1,0:T(8,128)(2,1)S(1)}, f32[64,128]{1,0:T(8,128)S(1)}, f32[2,128]...) custom-call(f32[2,512,128]{2,1,0:T(8,128)S(1)} %get-tuple-element.37.refs_0_, ...), custom_call_target="tpu_custom_call" | custom-call | flops 67108864 | bytes 524288 | tf_op jit(solution)/shard_map/pallas_call | solution.py:266
  3.9 0.8 %shard_map.75 = (f32[512,128]{1,0:T(8,128)S(1)}, f32[512,128]{1,0:T(8,128)S(1)}, bf16[128,384]{1,0:T(8,128)(2,1)S(1)}, f32[64,128]{1,0:T(8,128)S(1)}) custom-call(f32[2,512,128]{2,1,0:T(8,128)S(1)} %get-tuple-element.37.refs_0_, f32[2,512,128]{2,1,0:T(8,128)S(1)} %get-tuple-element.38.refs_1_, f32[16,128]{1,0:T(8,128)S(1)} %get-tuple-element.39.refs_2_, ...), custom_call_target="tpu_custom_call" | custom-call | flops 67108864 | bytes 524288 | tf_op jit(solution)/shard_map/pallas_call | solution.py:266
  4.7 4.3 %collective-permute-done = f32[2,128]{1,0:T(2,128)S(1)} collective-permute-done((f32[2,128]{1,0:T(2,128)S(1)}, f32[2,128]{1,0:T(2,128)S(1)}, u32[]{:S(2)}, u32[]{:S(2)}) %collective-permute-start) | collective-permute-done | bytes 1056 | tf_op jit(solution)/shard_map/ppermute | solution.py:289
  9.0 15.1 %all_to_all.5 = f32[8,1,512]{2,1,0:T(1,128)S(1)} all-to-all(f32[8,1,512]{2,1,0:T(1,128)S(1)} %broadcast_in_dim.8), channel_id=1, replica_groups={{192,240,288,336,384,432,480,528},{193,241,289,337,385,433,481,529},{19..., dimensions={0} | all-to-all | bytes 32768 | tf_op jit(solution)/shard_map/all_to_all | solution.py:293
  24.1 0.7 %collective-permute-start.1 = (f32[2,128]{1,0:T(2,128)S(1)}, f32[2,128]{1,0:T(2,128)S(1)}, u32[]{:S(2)}, u32[]{:S(2)}) collective-permute-start(f32[2,128]{1,0:T(2,128)S(1)} %reduce_sum.19), channel_id=1, source_target_pairs={{384,576},{432,624},{480,672},{528,720},{385,577},{433,625},{481,6... | collective-permute-start | bytes 3080 | tf_op jit(solution)/shard_map/ppermute | solution.py:304
  24.8 0.0 collective-permute-done.1.refs_3_
  24.8 1.6 %shard_map.76 = f32[16,8192]{1,0:T(8,128)} custom-call(f32[16,8192]{1,0:T(8,128)S(1)} %get-tuple-element.35.refs_0_, f32[2,128]{1,0:T(2,128)S(1)} %get-tuple-element.53.refs_1_, f32[2,128]{1,0:T(2,128)S(1)} %reduce_sum.18.refs_2_, f32[2,128]{1,0:T(2,128)S(1)} %collective-permute-done.1.refs_3_, f32[512,128]{1,0:T(8,128)S(1)} %get-tuple-element.57.refs_4_, ...), custom_call_target="tpu_custom_call" | custom-call | flops 100663296 | bytes 2097152 | tf_op jit(solution)/shard_map/pallas_call | solution.py:306
  (5 shorter events, 0.1 us)
Async XLA Ops:
  1.7 7.3 %collective-permute-start = (f32[2,128]{1,0:T(2,128)S(1)}, f32[2,128]{1,0:T(2,128)S(1)}, u32[]{:S(2)}, u32[]{:S(2)}) collective-permute-start(f32[2,128]{1,0:T(2,128)S(1)} %get-tuple-element.36), channel_id=1, source_target_pairs={{0,192},{48,240},{96,288},{144,336},{1,193},{49,241},{97,289},{145... | collective-permute-start | bytes 3080 | tf_op jit(solution)/shard_map/ppermute | solution.py:289
  24.1 0.7 %collective-permute-start.1 = (f32[2,128]{1,0:T(2,128)S(1)}, f32[2,128]{1,0:T(2,128)S(1)}, u32[]{:S(2)}, u32[]{:S(2)}) collective-permute-start(f32[2,128]{1,0:T(2,128)S(1)} %reduce_sum.19), channel_id=1, source_target_pairs={{384,576},{432,624},{480,672},{528,720},{385,577},{433,625},{481,6... | collective-permute-start | bytes 3080 | tf_op jit(solution)/shard_map/ppermute | solution.py:304
